TPU v7x, 256 devices: a whole 4x4x8 slice. The times are simulated.
256 devices in a mesh: sec: 32 (over z, x), op: 8 (over y, core).
Axes of the slice: x: 4, y: 4, z: 8, core: 2. Of those that a mesh axis runs over, the one named last changes fastest.
Arguments:
- trial: bfloat16 [2, 256, 256, 256], P(None, 'sec'), may hold values from -16 to 16
- left_env: bfloat16 [32, 256, 256, 256], P('op', 'sec'), may hold values from -2 to 2
- right_env: bfloat16 [32, 256, 256, 256], P('op', 'sec'), may hold values from -2 to 2
- left_block_ham: bfloat16 [256, 256, 256], P('sec', 'op'), may hold values from -1 to 3
- right_block_ham: bfloat16 [256, 256, 256], P('sec'), may hold values from -1 to 3
- target: int32 [32, 256], P('op', 'sec'), may hold values from 0 to 255, as said below
Outputs:
- hpsi: bfloat16 [2, 256, 256, 256], P(None, 'sec', 'op')
- gram: float32 [2, 2], replicated
Inputs may be any that keep to these rules, and one draw needn't show every extreme that they name: Within one device's block of target (4 terms by 8 sectors) at most 2 entries name sectors of any one owner (owner of sector t is t // 8), and some owner is named exactly 2 times.
All inputs are finite; a program needn't handle non-finite values.
Results may differ from a plain program's by a relative error of at most 0.0055.
Values may be sent and summed in bfloat16 or wider, within the bound.
No kernel may reach another device: no remote copies, remote signals or barrier semaphores. Data moves between devices by JAX's collectives and lax.ppermute only.
A program may use at most 128 MiB of HBM per device.

v0:
```python
import jax
import jax.numpy as jnp
from jax import lax
from jax.sharding import PartitionSpec as P


def contract(trial_part, left_env, right_env, packing):
    halfway = jnp.einsum(
        "wsij,vsjk->vwsik", left_env, trial_part, preferred_element_type=jnp.float32
    ).astype(jnp.bfloat16)
    pieces = jnp.einsum(
        "vwsik,wskl->vwsil", halfway, right_env, preferred_element_type=jnp.float32
    ).astype(jnp.bfloat16)
    count = pieces.shape[0]
    pieces = pieces.reshape(count, packing.shape[1], pieces.shape[3], pieces.shape[4])
    return jnp.einsum("pk,vkij->vpij", packing, pieces, preferred_element_type=jnp.float32).astype(
        jnp.bfloat16
    )


def body(trial, left_env, right_env, left_block_ham, right_block_ham, target):
    sec_count = lax.axis_size("sec")
    op_count = lax.axis_size("op")
    terms_here = left_env.shape[0]
    sectors_here = left_env.shape[1]
    width = left_env.shape[2]
    pairs = terms_here * sectors_here
    capacity = max(2, 2 * pairs // sec_count)
    slot_count = sec_count * capacity
    flat_target = target.reshape(pairs)
    owner = flat_target // sectors_here
    within = flat_target % sectors_here
    order = jnp.arange(pairs)
    earlier = order[None, :] < order[:, None]
    same_owner = owner[:, None] == owner[None, :]
    rank = jnp.sum(jnp.logical_and(earlier, same_owner).astype(jnp.int32), axis=1)
    slot = owner * capacity + rank
    slot_match = jnp.arange(slot_count)[:, None] == slot[None, :]
    slot_sector = jnp.sum(jnp.where(slot_match, within[None, :] + 1, 0), axis=1) - 1
    packing = slot_match.astype(jnp.bfloat16)
    packed_both = contract(trial, left_env, right_env, packing)
    received, labels = (
        lax.all_to_all(packed_both, "sec", split_axis=1, concat_axis=1, tiled=True),
        lax.all_to_all(slot_sector[None, :], "sec", split_axis=1, concat_axis=1, tiled=True),
    )
    rows = width // op_count
    first_row = lax.axis_index("op") * rows
    trial_rows = lax.dynamic_slice_in_dim(trial, first_row, rows, 2)
    local_part = jnp.einsum(
        "sij,vsjk->vsik", left_block_ham, trial, preferred_element_type=jnp.float32
    )
    local_part = local_part + jnp.einsum(
        "vsij,sjk->vsik", trial_rows, right_block_ham, preferred_element_type=jnp.float32
    )
    trial_rows_wide = trial_rows.astype(jnp.float32)
    scale = 1.0 / (sectors_here * sec_count * width * width)
    arrived = labels[0]
    unpacking = (jnp.arange(sectors_here)[:, None] == arrived[None, :]).astype(jnp.bfloat16)
    carried = lax.psum_scatter(
        jnp.einsum("sp,vpij->ivsj", unpacking, received, preferred_element_type=jnp.float32),
        "op",
        scatter_dimension=0,
        tiled=True,
    )
    total = jnp.transpose(carried, (1, 2, 0, 3)) + local_part
    partial_value = jnp.einsum("asij,bsij->ab", trial_rows_wide, total)
    gram = lax.psum(partial_value * scale, ("sec", "op"))
    return (total.astype(jnp.bfloat16), gram)


def solution(mesh):
    return jax.shard_map(
        body,
        mesh=mesh,
        in_specs=(
            P(None, "sec", None, None),
            P("op", "sec", None, None),
            P("op", "sec", None, None),
            P("sec", "op", None),
            P("sec", None, None),
            P("op", "sec"),
        ),
        out_specs=(P(None, "sec", "op", None), P()),
        check_vma=False,
    )
```

profile of v0, /device:TPU:1, one launch (start us, length us, event | category | flops | bytes accessed | tf_op | source)
XLA Modules:
  0.0 619.6 jit_solution(13271720439806921464)
XLA Ops:
  7.2 0.9 reshape.119
  8.1 0.2 convert_reduce_fusion
  8.3 0.1 select_reduce_fusion
  8.4 0.7 sub.14
  9.1 11.9 %all-to-all-start.1 = ((s32[1,32,2]{2,0,1:T(1,128)}), s32[1,32,2]{2,0,1:T(1,128)S(1)}, u32[]{:S(2)}, u32[]{:S(2)}) async-start(s32[1,32,2]{2,0,1:T(1,128)} %bitcast.11), calls=%async_computation.1 | async-start | bytes 32768 | tf_op jit(solution)/shard_map/all_to_all | solution.py:44
  21.0 9.2 %fusion.6 = bf16[4,8,2,256,256]{4,3,2,1,0:T(8,128)(2,1)} fusion(bf16[4,8,256,256]{3,2,1,0:T(8,128)(2,1)} %param.8, bf16[4,8,256,256]{3,2,1,0:T(8,128)(2,1)} %param.7, bf16[2,8,256,256]{3,2,1,0:T(8,128)(2,1)S(1)} %copy-done), kind=kOutput, calls=%fused_computation.7 | convolution fusion | flops 4303355904 | bytes 18874368 | tf_op jit(solution)/shard_map/vwsik,wskl->vwsil/dot_general | solution.py:11
  30.2 15.1 %convert_bitcast_fusion = bf16[2,64,256,256]{3,1,2,0:T(8,128)(2,1)} fusion(bf16[2,32,256,256]{3,2,0,1:T(8,128)(2,1)} %bitcast.78, s32[32]{0:T(128)S(1)} %multiply_add_fusion), kind=kOutput, calls=%fused_computation.2 | convolution fusion | flops 545261568 | bytes 25165952 | tf_op jit(solution)/shard_map/pk,vkij->vpij/dot_general | solution.py:16
  45.2 15.6 %copy.37 = bf16[2,64,256,256]{3,2,0,1:T(8,128)(2,1)} copy(bf16[2,64,256,256]{3,1,2,0:T(8,128)(2,1)} %convert_bitcast_fusion) | data formatting | bytes 33554432 | tf_op jit(solution)/shard_map/convert_element_type | solution.py:16
  60.9 9.3 %all-to-all-start = ((bf16[2,64,256,256]{3,2,0,1:T(8,128)(2,1)}), bf16[2,64,256,256]{3,2,0,1:T(8,128)(2,1)}, u32[]{:S(2)}, u32[]{:S(2)}) async-start(bf16[2,64,256,256]{3,2,0,1:T(8,128)(2,1)} %copy.37), calls=%async_computation | async-start | bytes 33554432 | tf_op jit(solution)/shard_map/all_to_all | solution.py:43
  70.3 0.2 reduce-scatter.5.cloned.1.call-start
  70.5 0.5 broadcast.148
  71.0 0.7 reduce.3
  71.7 0.1 eq.50
  71.8 369.9 %all-to-all-done = bf16[2,64,256,256]{3,2,0,1:T(8,128)(2,1)} async-done(((bf16[2,64,256,256]{3,2,0,1:T(8,128)(2,1)}), bf16[2,64,256,256]{3,2,0,1:T(8,128)(2,1)}, u32[]{:S(2)}, u32[]{:S(2)}) %all-to-all-start) | async-done | bytes 16777248 | tf_op jit(solution)/shard_map/all_to_all | solution.py:43
  441.7 16.7 %fusion.14 = f32[256,2,8,256]{3,2,0,1:T(8,128)S(1)} fusion(bf16[2,64,256,256]{3,2,0,1:T(8,128)(2,1)} %all-to-all-done, s32[64]{0:T(128)S(1)} %eq.50), kind=kOutput, calls=%fused_computation.11 | convolution fusion | flops 134218240 | bytes 20971776 | tf_op jit(solution)/shard_map/sp,vpij->ivsj/dot_general | solution.py:60
  458.4 0.6 copy.57
  459.1 5.7 copy.60
  464.9 1.5 convolution_bitcast_fusion.1
  466.4 64.0 %reduce-scatter.5.cloned.1.call-done = f32[32,4096]{1,0:T(8,128)} async-done(((f32[256,4096]{1,0:T(8,128)}), f32[32,4096]{1,0:T(8,128)}) %reduce-scatter.5.cloned.1.call-update) | async-done | bytes 524304
  530.4 1.2 copy.61
  531.6 0.5 fusion.20
  532.1 0.9 fusion.21
  533.1 0.7 copy.45
  533.8 78.9 %psum.7 = f32[2,2]{1,0:T(2,128)} all-reduce(f32[2,2]{1,0:T(2,128)S(1)} %fusion.21), channel_id=1, replica_groups=mesh['sec'=32,'op'=8] {'sec','op'}, use_global_device_ids=true, to_apply=%region_3.4 | all-reduce | flops 4 | bytes 32 | tf_op jit(solution)/shard_map/psum | solution.py:67
  (10 shorter events, 0.1 us)
Async XLA Ops:
  7.2 13.8 %copy-start = (bf16[2,8,256,256]{3,2,1,0:T(8,128)(2,1)S(1)}, bf16[2,8,256,256]{3,2,1,0:T(8,128)(2,1)}, u32[]{:S(2)}) copy-start(bf16[2,8,256,256]{3,2,1,0:T(8,128)(2,1)} %param.6) | copy-start | bytes 6291460
  9.1 51.8 %all-to-all-start.1 = ((s32[1,32,2]{2,0,1:T(1,128)}), s32[1,32,2]{2,0,1:T(1,128)S(1)}, u32[]{:S(2)}, u32[]{:S(2)}) async-start(s32[1,32,2]{2,0,1:T(1,128)} %bitcast.11), calls=%async_computation.1 | async-start | bytes 32768 | tf_op jit(solution)/shard_map/all_to_all | solution.py:44
  60.9 380.8 %all-to-all-start = ((bf16[2,64,256,256]{3,2,0,1:T(8,128)(2,1)}), bf16[2,64,256,256]{3,2,0,1:T(8,128)(2,1)}, u32[]{:S(2)}, u32[]{:S(2)}) async-start(bf16[2,64,256,256]{3,2,0,1:T(8,128)(2,1)} %copy.37), calls=%async_computation | async-start | bytes 33554432 | tf_op jit(solution)/shard_map/all_to_all | solution.py:43
  70.3 460.1 %reduce-scatter.5.cloned.1.call-start = ((), (), s32[]{:S(2)}) async-start(), calls=%async_computation.3 | async-start | bytes 4718592
  464.8 66.8 %copy-start.1 = (bf16[8,32,256]{2,1,0:T(8,128)(2,1)S(1)}, bf16[8,32,256]{2,1,0:T(8,128)(2,1)}, u32[]{:S(2)}) copy-start(bf16[8,32,256]{2,1,0:T(8,128)(2,1)} %param.9) | copy-start | bytes 393220
Sparse Core Ops, SparseCore 0:
  465.0 65.3 reduce-scatter.4
where the time goes:
time: 620 us
  waiting for transfers between devices  434 us (70%)
  blocking collectives  78.9 us (13%)
  matrix products  43.9 us (7%)
  local copies, waits for them, and re-layouts  26.2 us (4%)
  starting transfers between devices  21.4 us (3%)
  between operations  14.1 us (2%)
    all_to_all x1, waiting for transfers between devices, body(): lax.all_to_all(packed_both, 'sec', split_axis=1, concat_axis=1, tiled=True)  370 us
    psum x1, blocking collectives, body(): gram = lax.psum(partial_value * scale, ('sec', 'op'))  78.9 us
    unnamed x2, waiting for transfers between devices  64 us
    dot_general x1, matrix products, body(): jnp.einsum('sp,vpij->ivsj', unpacking, received, preferred_element_type=j...  16.7 us
    convert_element_type x1, local copies, waits for them, and re-layouts, contract(): jnp.einsum('pk,vkij->vpij', packing, pieces, preferred_element_type=jnp.f...  15.6 us
    dot_general x1, matrix products, contract(): jnp.einsum('pk,vkij->vpij', packing, pieces, preferred_element_type=jnp.f...  15.1 us
  transfers between devices with their start and end apart: 3, of which 2 were waited for; matrix products, arithmetic and copies ran while one was open for 7% of the time, Pallas kernels for 0%

commit v1 on v0

v1 whole, which is shorter than its diff:
```python
import functools

import jax
import jax.numpy as jnp
from jax import lax
from jax.experimental import pallas as pl
from jax.experimental.pallas import tpu as pltpu
from jax.sharding import Mesh
from jax.sharding import PartitionSpec as P

BF16 = jnp.bfloat16
F32 = jnp.float32


def contract_kernel(groups, rows, left_ref, right_ref, trial_ref, out_ref):
    for s in range(left_ref.shape[1]):
        half = jnp.dot(left_ref[0, s], trial_ref[0, s], preferred_element_type=F32).astype(BF16)
        piece = jnp.dot(half, right_ref[0, s], preferred_element_type=F32).astype(BF16)
        width = out_ref.shape[-1]
        for j in range(out_ref.shape[0]):
            out_ref[j, :, s] = piece[:, j * width : (j + 1) * width].reshape(groups, rows, width)


def contract(trial, left_env, right_env, v, groups, parts):
    terms, sectors, size, _ = left_env.shape
    rows = size // groups
    width = size // parts
    return pl.pallas_call(
        functools.partial(contract_kernel, groups, rows),
        grid=(terms,),
        in_specs=[
            pl.BlockSpec((1, sectors, size, size), lambda w: (w, 0, 0, 0)),
            pl.BlockSpec((1, sectors, size, size), lambda w: (w, 0, 0, 0)),
            pl.BlockSpec((1, sectors, size, size), lambda w: (v, 0, 0, 0)),
        ],
        out_specs=pl.BlockSpec((parts, groups, sectors, rows, width), lambda w: (0, 0, w, 0, 0)),
        out_shape=jax.ShapeDtypeStruct((parts, groups, terms * sectors, rows, width), BF16),
        cost_estimate=pl.CostEstimate(
            flops=4 * terms * sectors * size**3,
            bytes_accessed=6 * terms * sectors * size * size,
            transcendentals=0,
        ),
        compiler_params=pltpu.CompilerParams(vmem_limit_bytes=32 * 2**20),
    )(left_env, right_env, trial)


def merge_kernel(target_ref, pieces_ref, out_ref, sums):
    sums[...] = jnp.zeros_like(sums)

    def add(p, carry):
        t = target_ref[p]
        sums[t] += pieces_ref[p].astype(F32)
        return carry

    lax.fori_loop(0, pieces_ref.shape[0], add, 0, unroll=8)
    out_ref[...] = sums[...].astype(BF16)


def merge(targets, pieces, sectors):
    count, rows, width = pieces.shape
    return pl.pallas_call(
        merge_kernel,
        in_specs=[
            pl.BlockSpec(memory_space=pltpu.SMEM),
            pl.BlockSpec(memory_space=pltpu.VMEM),
        ],
        out_specs=pl.BlockSpec(memory_space=pltpu.VMEM),
        out_shape=jax.ShapeDtypeStruct((sectors, rows, width), BF16),
        scratch_shapes=[pltpu.VMEM((sectors, rows, width), F32)],
        cost_estimate=pl.CostEstimate(
            flops=count * rows * width,
            bytes_accessed=2 * (count + sectors) * rows * width,
            transcendentals=0,
        ),
        compiler_params=pltpu.CompilerParams(vmem_limit_bytes=32 * 2**20),
    )(targets, pieces)


PARTS = 2


def body(trial, left_env, right_env, left_block_ham, right_block_ham, target):
    nz, nx = lax.axis_size("z"), lax.axis_size("x")
    groups = lax.axis_size("y") * lax.axis_size("core")
    op = ("y", "core")
    terms, here, size, _ = left_env.shape
    pairs = terms * here
    sectors = nz * nx * here
    rows = size // groups
    width = size // PARTS
    all_targets = lax.all_to_all(
        jnp.broadcast_to(target.reshape(1, pairs), (groups, pairs)), op, 0, 0, tiled=True
    ).reshape(groups * pairs)

    first_row = lax.axis_index(op) * rows
    trial_rows = lax.dynamic_slice_in_dim(trial, first_row, rows, 2)
    local = jnp.einsum("sij,vsjk->vsik", left_block_ham, trial, preferred_element_type=F32)
    local = local + jnp.einsum(
        "vsij,sjk->vsik", trial_rows, right_block_ham, preferred_element_type=F32
    )

    carried = []
    for v in range(trial.shape[0]):
        pieces = contract(trial, left_env, right_env, v, groups, PARTS)
        sums = []
        for j in range(PARTS):
            got = lax.all_to_all(pieces[j], op, 0, 0, tiled=True)
            dense = merge(all_targets, got.reshape(groups * pairs, rows, width), sectors)
            part = lax.psum_scatter(dense, "z", scatter_dimension=0, tiled=True)
            part = lax.all_to_all(part.reshape(nx, here, rows, width), "x", 0, 0, tiled=True)
            sums.append(jnp.sum(part.astype(F32), axis=0))
        carried.append(jnp.concatenate(sums, axis=-1))
    total = jnp.stack(carried) + local
    scale = 1.0 / (sectors * size * size)
    partial = jnp.einsum("asij,bsij->ab", trial_rows.astype(F32), total) * scale

    def spread(x, axes, n):
        x = lax.all_to_all(jnp.broadcast_to(x[None], (n, *x.shape)), axes, 0, 0, tiled=True)
        return jnp.sum(x, axis=0)

    gram = spread(spread(partial, ("z", "x"), nz * nx), op, groups)
    return total.astype(BF16), gram


def solution(mesh):
    sizes = {"z": 8, "x": 4, "y": 4, "core": 2}
    fine = Mesh(mesh.devices.reshape(tuple(sizes.values())), tuple(sizes))
    sec, op = ("z", "x"), ("y", "core")
    return jax.shard_map(
        body,
        mesh=fine,
        in_specs=(
            P(None, sec, None, None),
            P(op, sec, None, None),
            P(op, sec, None, None),
            P(sec, op, None),
            P(sec, None, None),
            P(op, sec),
        ),
        out_specs=(P(None, sec, op, None), P()),
        check_vma=False,
    )
```

time: 620 us -> 284 us (0.46)
  waiting for transfers between devices: 434 us -> 70 us
  matrix products: 43.9 us -> 3.65 us
  blocking collectives: 78.9 us -> 106 us
  starting transfers between devices: 21.4 us -> 39.9 us
  Pallas kernels: 0 us -> 16.1 us
  other arithmetic: 0.99 us -> 7.58 us
    all_to_all x2 -> x7, waiting for transfers between devices: 370 us -> 41.1 us  [the longest x1 25.1 us: body(): got = lax.all_to_all(pieces[j], op, 0, 0, tiled=True)]
    all_to_all x0 -> x4, blocking collectives: none -> 106 us  [the longest x3 91.8 us: body(): got = lax.all_to_all(pieces[j], op, 0, 0, tiled=True)]
    psum x1 -> x0, blocking collectives: 78.9 us -> none  [body(): gram = lax.psum(partial_value * scale, ('sec', 'op'))]
    unnamed x2 -> x4, waiting for transfers between devices: 64 us -> 0.07 us
    dot_general x4 -> x1, matrix products: 41.9 us -> 0.94 us  [body(): partial = jnp.einsum('asij,bsij->ab', trial_rows.astype(F32), total) * scale]
    reduce_scatter x0 -> x4, waiting for transfers between devices: none -> 28.9 us  [body(): part = lax.psum_scatter(dense, 'z', scatter_dimension=0, tiled=True)]
    all_to_all x2 -> x7, starting transfers between devices: 21.2 us -> 39.8 us  [the longest x4 16.8 us: body(): lax.all_to_all(part.reshape(nx, here, rows, width), 'x', 0, 0, tiled=True)]
    pallas_call x0 -> x6, Pallas kernels: none -> 16.1 us  [the longest x4 9.19 us: merge(): pl.pallas_call(merge_kernel, in_specs=[pl.BlockSpec(memory_space=pltpu.SM...]
  transfers between devices with their start and end apart: 3 -> 11, of which waited for: 2 -> 6; matrix products, arithmetic and copies ran while one was open for 7% -> 5% of each run, Pallas kernels for 0% -> 5%
where the time goes in v1:
time: 284 us; the launch traced here: 282 us
  blocking collectives  106 us (37%)
  waiting for transfers between devices  70 us (25%)
  starting transfers between devices  39.9 us (14%)
  local copies, waits for them, and re-layouts  25.5 us (9%)
  Pallas kernels  16.1 us (6%)
  between operations  14 us (5%)
  other arithmetic  7.58 us (3%)
  matrix products  3.65 us (1%)
    all_to_all x3, blocking collectives, body(): got = lax.all_to_all(pieces[j], op, 0, 0, tiled=True)  91.8 us
    reduce_scatter x4, waiting for transfers between devices, body(): part = lax.psum_scatter(dense, 'z', scatter_dimension=0, tiled=True)  28.9 us
    all_to_all x1, waiting for transfers between devices, body(): got = lax.all_to_all(pieces[j], op, 0, 0, tiled=True)  25.1 us
    unnamed x23, local copies, waits for them, and re-layouts  17.6 us
    all_to_all x4, starting transfers between devices, body(): lax.all_to_all(part.reshape(nx, here, rows, width), 'x', 0, 0, tiled=True)  16.8 us
    all_to_all x1, blocking collectives, spread(): lax.all_to_all(jnp.broadcast_to(x[None], (n, *x.shape)), axes, 0, 0, tile...  13.8 us
    all_to_all x4, waiting for transfers between devices, body(): lax.all_to_all(part.reshape(nx, here, rows, width), 'x', 0, 0, tiled=True)  13 us
    all_to_all x1, starting transfers between devices, spread(): lax.all_to_all(jnp.broadcast_to(x[None], (n, *x.shape)), axes, 0, 0, tile...  11.8 us
  transfers between devices with their start and end apart: 11, of which 6 were waited for; matrix products, arithmetic and copies ran while one was open for 5% of the time, Pallas kernels for 5%

profile of v1, /device:TPU:1, one launch (start us, length us, event | category | flops | bytes accessed | tf_op | source)
XLA Modules:
  0.0 282.4 jit_solution(13971595248120509834)
XLA Ops:
  8.6 6.5 %all-to-all-start = ((s32[8,1,32]{2,1,0:T(1,128)}), s32[8,1,32]{2,1,0:T(1,128)S(1)}, u32[]{:S(2)}, u32[]{:S(2)}) async-start(s32[8,1,32]{2,1,0:T(1,128)} %broadcast_in_dim.9), calls=%async_computation | async-start | bytes 8192 | tf_op jit(solution)/shard_map/all_to_all | solution.py:91
  21.1 3.4 %shard_map.80 = bf16[2,8,32,32,128]{4,3,2,1,0:T(8,128)(2,1)S(1)} custom-call(bf16[4,8,256,256]{3,2,1,0:T(8,128)(2,1)S(1)} %copy-done.3, bf16[4,8,256,256]{3,2,1,0:T(8,128)(2,1)S(1)} %copy-done.5, bf16[2,8,256,256]{3,2,1,0:T(8,128)(2,1)S(1)} %copy-done.1), custom_call_target="tpu_custom_call" | custom-call | flops 2147483648 | bytes 12582912 | tf_op jit(solution)/shard_map/pallas_call | solution.py:28
  24.5 2.9 %slice_bitcast_fusion.1 = (bf16[8,32,32,128]{3,2,1,0:T(8,128)(2,1)}, bf16[8,32,32,128]{3,2,1,0:T(8,128)(2,1)}) fusion(bf16[2,8,32,32,128]{4,3,2,1,0:T(8,128)(2,1)S(1)} %shard_map.80), kind=kLoop, calls=%fused_computation.1 | loop fusion | bytes 8388608 | tf_op jit(solution)/shard_map/squeeze | solution.py:107
  27.4 4.8 %all-to-all-start.5 = ((bf16[8,32,32,128]{3,2,1,0:T(8,128)(2,1)}), bf16[8,32,32,128]{3,2,1,0:T(8,128)(2,1)S(1)}, u32[]{:S(2)}, u32[]{:S(2)}) async-start(bf16[8,32,32,128]{3,2,1,0:T(8,128)(2,1)} %get-tuple-element.10), calls=%async_computation.7 | async-start | bytes 4194304 | tf_op jit(solution)/shard_map/all_to_all | solution.py:107
  33.5 25.1 %all-to-all-done.5 = bf16[8,32,32,128]{3,2,1,0:T(8,128)(2,1)S(1)} async-done(((bf16[8,32,32,128]{3,2,1,0:T(8,128)(2,1)}), bf16[8,32,32,128]{3,2,1,0:T(8,128)(2,1)S(1)}, u32[]{:S(2)}, u32[]{:S(2)}) %all-to-all-start.5) | async-done | bytes 2097184 | tf_op jit(solution)/shard_map/all_to_all | solution.py:107
  58.6 3.3 %shard_map.81 = bf16[256,32,128]{2,1,0:T(8,128)(2,1)} custom-call(s32[256]{0:T(256)S(1)} %reshape.43.target_ref, bf16[256,32,128]{2,1,0:T(8,128)(2,1)S(1)} %bitcast.45), custom_call_target="tpu_custom_call" | custom-call | flops 1048576 | bytes 4194304 | tf_op jit(solution)/shard_map/pallas_call | solution.py:61
  61.9 30.9 %all_to_all.56 = bf16[8,32,32,128]{3,2,1,0:T(8,128)(2,1)S(1)} all-to-all(bf16[8,32,32,128]{3,2,1,0:T(8,128)(2,1)} %get-tuple-element.11), channel_id=1, replica_groups=mesh['z'=8,'x'=4,'y'=4,'core'=2] {'y','core'}, dimensions={0} | all-to-all | bytes 4194304 | tf_op jit(solution)/shard_map/all_to_all | solution.py:107
  97.7 2.2 copy-done.4
  100.0 2.2 copy-done.6
  102.2 3.4 %shard_map.77 = bf16[2,8,32,32,128]{4,3,2,1,0:T(8,128)(2,1)S(1)} custom-call(bf16[4,8,256,256]{3,2,1,0:T(8,128)(2,1)S(1)} %copy-done.4, bf16[4,8,256,256]{3,2,1,0:T(8,128)(2,1)S(1)} %copy-done.6, bf16[2,8,256,256]{3,2,1,0:T(8,128)(2,1)S(1)} %copy-done.2), custom_call_target="tpu_custom_call" | custom-call | flops 2147483648 | bytes 12582912 | tf_op jit(solution)/shard_map/pallas_call | solution.py:28
  105.6 2.3 slice_bitcast_fusion.3
  107.9 29.9 %all_to_all.57 = bf16[8,32,32,128]{3,2,1,0:T(8,128)(2,1)S(1)} all-to-all(bf16[8,32,32,128]{3,2,1,0:T(8,128)(2,1)S(1)} %get-tuple-element.8), channel_id=1, replica_groups=mesh['z'=8,'x'=4,'y'=4,'core'=2] {'y','core'}, dimensions={0} | all-to-all | bytes 4194304 | tf_op jit(solution)/shard_map/all_to_all | solution.py:107
  141.2 31.0 %all_to_all.58 = bf16[8,32,32,128]{3,2,1,0:T(8,128)(2,1)S(1)} all-to-all(bf16[8,32,32,128]{3,2,1,0:T(8,128)(2,1)} %get-tuple-element.9), channel_id=1, replica_groups=mesh['z'=8,'x'=4,'y'=4,'core'=2] {'y','core'}, dimensions={0} | all-to-all | bytes 4194304 | tf_op jit(solution)/shard_map/all_to_all | solution.py:107
  175.6 4.1 %all-to-all-start.6 = ((bf16[4,8,32,128]{3,2,1,0:T(8,128)(2,1)}), bf16[4,8,32,128]{3,2,1,0:T(8,128)(2,1)}, u32[]{:S(2)}, u32[]{:S(2)}) async-start(bf16[4,8,32,128]{3,2,1,0:T(8,128)(2,1)} %bitcast.49), calls=%async_computation.9 | async-start | bytes 524288 | tf_op jit(solution)/shard_map/all_to_all | solution.py:110
  179.8 5.5 %all-to-all-done.6 = bf16[4,8,32,128]{3,2,1,0:T(8,128)(2,1)} async-done(((bf16[4,8,32,128]{3,2,1,0:T(8,128)(2,1)}), bf16[4,8,32,128]{3,2,1,0:T(8,128)(2,1)}, u32[]{:S(2)}, u32[]{:S(2)}) %all-to-all-start.6) | async-done | bytes 262176 | tf_op jit(solution)/shard_map/all_to_all | solution.py:110
  185.3 4.0 %all-to-all-start.8 = ((bf16[4,8,32,128]{3,2,1,0:T(8,128)(2,1)}), bf16[4,8,32,128]{3,2,1,0:T(8,128)(2,1)}, u32[]{:S(2)}, u32[]{:S(2)}) async-start(bf16[4,8,32,128]{3,2,1,0:T(8,128)(2,1)} %bitcast.50), calls=%async_computation.12 | async-start | bytes 524288 | tf_op jit(solution)/shard_map/all_to_all | solution.py:110
  190.5 4.5 %all-to-all-done.8 = bf16[4,8,32,128]{3,2,1,0:T(8,128)(2,1)} async-done(((bf16[4,8,32,128]{3,2,1,0:T(8,128)(2,1)}), bf16[4,8,32,128]{3,2,1,0:T(8,128)(2,1)}, u32[]{:S(2)}, u32[]{:S(2)}) %all-to-all-start.8) | async-done | bytes 262176 | tf_op jit(solution)/shard_map/all_to_all | solution.py:110
  194.9 4.0 %all-to-all-start.2 = ((bf16[4,8,32,128]{3,2,1,0:T(8,128)(2,1)}), bf16[4,8,32,128]{3,2,1,0:T(8,128)(2,1)}, u32[]{:S(2)}, u32[]{:S(2)}) async-start(bf16[4,8,32,128]{3,2,1,0:T(8,128)(2,1)} %bitcast.51), calls=%async_computation.3 | async-start | bytes 524288 | tf_op jit(solution)/shard_map/all_to_all | solution.py:110
  201.7 28.9 %reduce-scatter.7.cloned.1.call-done = bf16[32,32,128]{2,1,0:T(8,128)(2,1)} async-done(((bf16[256,32,128]{2,1,0:T(8,128)(2,1)}), bf16[32,32,128]{2,1,0:T(8,128)(2,1)}) %reduce-scatter.7.cloned.1.call-update) | async-done | bytes 262160 | tf_op jit(solution)/shard_map/reduce_scatter | solution.py:109
  230.5 4.6 %all-to-all-start.4 = ((bf16[4,8,32,128]{3,2,1,0:T(8,128)(2,1)}), bf16[4,8,32,128]{3,2,1,0:T(8,128)(2,1)}, u32[]{:S(2)}, u32[]{:S(2)}) async-start(bf16[4,8,32,128]{3,2,1,0:T(8,128)(2,1)} %bitcast.52), calls=%async_computation.6 | async-start | bytes 524288 | tf_op jit(solution)/shard_map/all_to_all | solution.py:110
  237.8 3.0 %all-to-all-done.4 = bf16[4,8,32,128]{3,2,1,0:T(8,128)(2,1)} async-done(((bf16[4,8,32,128]{3,2,1,0:T(8,128)(2,1)}), bf16[4,8,32,128]{3,2,1,0:T(8,128)(2,1)}, u32[]{:S(2)}, u32[]{:S(2)}) %all-to-all-start.4) | async-done | bytes 262176 | tf_op jit(solution)/shard_map/all_to_all | solution.py:110
  244.4 13.8 %all_to_all.59 = f32[32,2,2]{2,1,0:T(2,128)S(1)} all-to-all(f32[32,2,2]{2,1,0:T(2,128)S(1)} %broadcast_in_dim.10), channel_id=1, replica_groups=mesh['z'=8,'x'=4,'y'=4,'core'=2] {'z','x'}, dimensions={0} | all-to-all | bytes 1024 | tf_op jit(solution)/shard_map/all_to_all | solution.py:118
  258.9 11.8 %all-to-all-start.10 = ((f32[8,2,2]{2,1,0:T(2,128)}), f32[8,2,2]{2,1,0:T(2,128)S(1)}, u32[]{:S(2)}, u32[]{:S(2)}) async-start(f32[8,2,2]{2,1,0:T(2,128)} %broadcast_in_dim.22), calls=%async_computation.14 | async-start | bytes 16384 | tf_op jit(solution)/shard_map/all_to_all | solution.py:118
  272.3 2.9 %all-to-all-done.10 = f32[8,2,2]{2,1,0:T(2,128)S(1)} async-done(((f32[8,2,2]{2,1,0:T(2,128)}), f32[8,2,2]{2,1,0:T(2,128)S(1)}, u32[]{:S(2)}, u32[]{:S(2)}) %all-to-all-start.10) | async-done | bytes 160 | tf_op jit(solution)/shard_map/all_to_all | solution.py:118
  (56 shorter events, 33.2 us)
Async XLA Ops:
  7.2 182.2 %copy-start = (bf16[8,256,256]{2,1,0:T(8,128)(2,1)S(1)}, bf16[8,256,256]{2,1,0:T(8,128)(2,1)}, u32[]{:S(2)}) copy-start(bf16[8,256,256]{2,1,0:T(8,128)(2,1)} %param.10) | copy-start | bytes 3145732
  8.6 18.8 %all-to-all-start = ((s32[8,1,32]{2,1,0:T(1,128)}), s32[8,1,32]{2,1,0:T(1,128)S(1)}, u32[]{:S(2)}, u32[]{:S(2)}) async-start(s32[8,1,32]{2,1,0:T(1,128)} %broadcast_in_dim.9), calls=%async_computation | async-start | bytes 8192 | tf_op jit(solution)/shard_map/all_to_all | solution.py:91
  15.1 1.6 copy-start.1
  16.7 2.2 copy-start.3
  18.9 2.2 copy-start.5
  27.4 31.2 %all-to-all-start.5 = ((bf16[8,32,32,128]{3,2,1,0:T(8,128)(2,1)}), bf16[8,32,32,128]{3,2,1,0:T(8,128)(2,1)S(1)}, u32[]{:S(2)}, u32[]{:S(2)}) async-start(bf16[8,32,32,128]{3,2,1,0:T(8,128)(2,1)} %get-tuple-element.10), calls=%async_computation.7 | async-start | bytes 4194304 | tf_op jit(solution)/shard_map/all_to_all | solution.py:107
  32.2 143.4 %reduce-scatter.9.cloned.1.call-start = ((), (), s32[]{:S(2)}) async-start(), calls=%async_computation.17 | async-start | bytes 2359296 | tf_op jit(solution)/shard_map/reduce_scatter | solution.py:109
  61.9 117.9 %reduce-scatter.11.cloned.1.call-start = ((), (), s32[]{:S(2)}) async-start(), calls=%async_computation.18 | async-start | bytes 2359296 | tf_op jit(solution)/shard_map/reduce_scatter | solution.py:109
  94.8 1.3 copy-start.7
  96.1 1.6 copy-start.2
  96.2 94.3 %reduce-scatter.5.cloned.1.call-start = ((), (), s32[]{:S(2)}) async-start(), calls=%async_computation.15 | async-start | bytes 2359296 | tf_op jit(solution)/shard_map/reduce_scatter | solution.py:109
  97.7 2.2 copy-start.4
  100.0 2.2 copy-start.6
  139.8 1.3 copy-start.9
  141.2 89.4 %reduce-scatter.7.cloned.1.call-start = ((), (), s32[]{:S(2)}) async-start(), calls=%async_computation.16 | async-start | bytes 2359296 | tf_op jit(solution)/shard_map/reduce_scatter | solution.py:109
  174.2 1.4 copy-start.8
  175.6 9.7 %all-to-all-start.6 = ((bf16[4,8,32,128]{3,2,1,0:T(8,128)(2,1)}), bf16[4,8,32,128]{3,2,1,0:T(8,128)(2,1)}, u32[]{:S(2)}, u32[]{:S(2)}) async-start(bf16[4,8,32,128]{3,2,1,0:T(8,128)(2,1)} %bitcast.49), calls=%async_computation.9 | async-start | bytes 524288 | tf_op jit(solution)/shard_map/all_to_all | solution.py:110
  185.3 9.6 %all-to-all-start.8 = ((bf16[4,8,32,128]{3,2,1,0:T(8,128)(2,1)}), bf16[4,8,32,128]{3,2,1,0:T(8,128)(2,1)}, u32[]{:S(2)}, u32[]{:S(2)}) async-start(bf16[4,8,32,128]{3,2,1,0:T(8,128)(2,1)} %bitcast.50), calls=%async_computation.12 | async-start | bytes 524288 | tf_op jit(solution)/shard_map/all_to_all | solution.py:110
  194.9 35.6 %all-to-all-start.2 = ((bf16[4,8,32,128]{3,2,1,0:T(8,128)(2,1)}), bf16[4,8,32,128]{3,2,1,0:T(8,128)(2,1)}, u32[]{:S(2)}, u32[]{:S(2)}) async-start(bf16[4,8,32,128]{3,2,1,0:T(8,128)(2,1)} %bitcast.51), calls=%async_computation.3 | async-start | bytes 524288 | tf_op jit(solution)/shard_map/all_to_all | solution.py:110
  230.5 10.2 %all-to-all-start.4 = ((bf16[4,8,32,128]{3,2,1,0:T(8,128)(2,1)}), bf16[4,8,32,128]{3,2,1,0:T(8,128)(2,1)}, u32[]{:S(2)}, u32[]{:S(2)}) async-start(bf16[4,8,32,128]{3,2,1,0:T(8,128)(2,1)} %bitcast.52), calls=%async_computation.6 | async-start | bytes 524288 | tf_op jit(solution)/shard_map/all_to_all | solution.py:110
  243.4 0.9 copy-start.10
  258.9 16.4 %all-to-all-start.10 = ((f32[8,2,2]{2,1,0:T(2,128)}), f32[8,2,2]{2,1,0:T(2,128)S(1)}, u32[]{:S(2)}, u32[]{:S(2)}) async-start(f32[8,2,2]{2,1,0:T(2,128)} %broadcast_in_dim.22), calls=%async_computation.14 | async-start | bytes 16384 | tf_op jit(solution)/shard_map/all_to_all | solution.py:118
Sparse Core Ops, SparseCore 0:
  62.0 38.6 reduce-scatter.8
  103.2 40.6 reduce-scatter.10
  146.5 41.0 reduce-scatter.4
  189.9 40.5 reduce-scatter.6

commit v2 on v1

v2 whole, which is shorter than its diff:
```python
import jax
import jax.numpy as jnp
from jax import lax
from jax.experimental import pallas as pl
from jax.experimental.pallas import tpu as pltpu
from jax.sharding import Mesh
from jax.sharding import PartitionSpec as P

BF16 = jnp.bfloat16
F32 = jnp.float32
SUB, LANES = 16, 128


def params(mib):
    return pltpu.CompilerParams(vmem_limit_bytes=mib * 2**20)


def contract_kernel(left_ref, right_ref, trial_ref, out_ref):
    groups = 8
    for s in range(left_ref.shape[1]):
        for v in range(2):
            half = jnp.dot(left_ref[0, s], trial_ref[v, s], preferred_element_type=F32)
            piece = jnp.dot(half.astype(BF16), right_ref[0, s], preferred_element_type=F32)
            piece = piece.astype(BF16)
            for j in range(2):
                cols = piece[:, j * LANES : (j + 1) * LANES].reshape(groups, 2, SUB, LANES)
                for i in range(2):
                    x = 2 * i + j
                    out_ref[x * groups : (x + 1) * groups, s, v] = cols[:, i]


def contract(trial, left_env, right_env, devices):
    terms, here, size, _ = left_env.shape
    cut = 1
    some = here // cut
    return pl.pallas_call(
        contract_kernel,
        grid=(cut, terms),
        in_specs=[
            pl.BlockSpec((1, some, size, size), lambda h, w: (w, h, 0, 0)),
            pl.BlockSpec((1, some, size, size), lambda h, w: (w, h, 0, 0)),
            pl.BlockSpec((2, some, size, size), lambda h, w: (0, h, 0, 0)),
        ],
        out_specs=pl.BlockSpec(
            (devices, some, 2, SUB, LANES), lambda h, w: (0, w * cut + h, 0, 0, 0)
        ),
        out_shape=jax.ShapeDtypeStruct((devices, terms * here, 2, SUB, LANES), BF16),
        cost_estimate=pl.CostEstimate(
            flops=8 * terms * here * size**3,
            bytes_accessed=8 * terms * here * size * size,
            transcendentals=0,
        ),
        compiler_params=params(40),
    )(left_env, right_env, trial)


def merge_kernel(target_ref, pieces_ref, out_ref, sums):
    step = pl.program_id(0)
    sources, pairs = pieces_ref.shape[:2]

    @pl.when(step == 0)
    def _():
        sums[...] = jnp.zeros_like(sums)

    for a in range(sources):

        def add(p, carry, a=a):
            t = target_ref[(step * sources + a) * pairs + p]
            sums[t] += pieces_ref[a, p].astype(F32)
            return carry

        lax.fori_loop(0, pairs, add, 0, unroll=8)

    @pl.when(step == pl.num_programs(0) - 1)
    def _():
        out_ref[...] = sums[...].astype(BF16)


def merge(targets, pieces, sectors):
    devices, pairs = pieces.shape[:2]
    steps = 8
    return pl.pallas_call(
        merge_kernel,
        grid=(steps,),
        in_specs=[
            pl.BlockSpec(memory_space=pltpu.SMEM),
            pl.BlockSpec((devices // steps, pairs, 2, SUB, LANES), lambda i: (i, 0, 0, 0, 0)),
        ],
        out_specs=pl.BlockSpec((sectors, 2, SUB, LANES), lambda i: (0, 0, 0, 0)),
        out_shape=jax.ShapeDtypeStruct((sectors, 2, SUB, LANES), BF16),
        scratch_shapes=[pltpu.VMEM((sectors, 2, SUB, LANES), F32)],
        cost_estimate=pl.CostEstimate(
            flops=devices * pairs * 2 * SUB * LANES,
            bytes_accessed=2 * (devices * pairs + sectors) * 2 * SUB * LANES,
            transcendentals=0,
        ),
        compiler_params=params(32),
    )(targets, pieces)


def finish_kernel(scale, got_ref, local_ref, rows_ref, out_ref, gram_ref):
    nz = got_ref.shape[0]
    found = [[jnp.zeros((SUB, LANES), F32) for _ in range(2)] for _ in range(2)]
    for x in range(4):
        i, j = x // 2, x % 2
        acc = got_ref[0, x].astype(F32)
        for z in range(1, nz):
            acc = acc + got_ref[z, x].astype(F32)
        here = (slice(None), slice(i * SUB, (i + 1) * SUB), slice(j * LANES, (j + 1) * LANES))
        for b in range(2):
            total = acc[:, b] + local_ref[(b, *here)]
            out_ref[(b, *here)] = total.astype(BF16)
            for a in range(2):
                found[a][b] += jnp.sum(rows_ref[(a, *here)].astype(F32) * total, axis=0)
    for a in range(2):
        for b in range(2):
            gram_ref[a, b] = jnp.sum(found[a][b]) * scale


def finish(got, local, trial_rows, scale):
    vmem = pl.BlockSpec(memory_space=pltpu.VMEM)
    return pl.pallas_call(
        lambda *refs: finish_kernel(scale, *refs),
        in_specs=[vmem] * 3,
        out_specs=[vmem, pl.BlockSpec(memory_space=pltpu.SMEM)],
        out_shape=[
            jax.ShapeDtypeStruct(local.shape, BF16),
            jax.ShapeDtypeStruct((2, 2), F32),
        ],
        compiler_params=params(32),
    )(got, local, trial_rows)


def to_all(x, axes):
    return lax.all_to_all(x, axes, 0, 0, tiled=True)


def spread(x, axes):
    return to_all(jnp.broadcast_to(x[None], (lax.axis_size(axes), *x.shape)), axes)


def body(trial, left_env, right_env, left_block_ham, right_block_ham, target):
    sec, op, plane = ("z", "x"), ("y", "core"), ("x", "y", "core")
    nz, nx, devices = lax.axis_size("z"), lax.axis_size("x"), lax.axis_size(plane)
    terms, here, size, _ = left_env.shape
    sectors = nz * nx * here
    rows = size // lax.axis_size(op)
    targets = spread(target.reshape(terms * here), plane).reshape(-1)

    first_row = lax.axis_index(op) * rows
    trial_rows = lax.dynamic_slice_in_dim(trial, first_row, rows, 2)
    local = jnp.einsum("sij,vsjk->vsik", left_block_ham, trial, preferred_element_type=F32)
    local = local + jnp.einsum(
        "vsij,sjk->vsik", trial_rows, right_block_ham, preferred_element_type=F32
    )

    pieces = to_all(contract(trial, left_env, right_env, devices), plane)
    sums = to_all(merge(targets, pieces, sectors).reshape(-1, here, 2, SUB, LANES), sec)
    scale = 1.0 / (sectors * size * size)
    hpsi, partial = finish(sums.reshape(nz, nx, here, 2, SUB, LANES), local, trial_rows, scale)
    gram = jnp.sum(spread(partial, sec), axis=0)
    gram = jnp.sum(spread(gram, op), axis=0)
    return hpsi, gram


def solution(mesh):
    sizes = {"z": 8, "x": 4, "y": 4, "core": 2}
    fine = Mesh(mesh.devices.reshape(tuple(sizes.values())), tuple(sizes))
    sec, op = ("z", "x"), ("y", "core")
    return jax.shard_map(
        body,
        mesh=fine,
        in_specs=(
            P(None, sec, None, None),
            P(op, sec, None, None),
            P(op, sec, None, None),
            P(sec, op, None),
            P(sec, None, None),
            P(op, sec),
        ),
        out_specs=(P(None, sec, op, None), P()),
        check_vma=False,
    )
```

time: 284 us -> 255 us (0.90)
  waiting for transfers between devices: 70 us -> 150 us
  blocking collectives: 106 us -> 43.4 us
  local copies, waits for them, and re-layouts: 25.5 us -> 11 us
  between operations: 14 us -> 0.76 us
  starting transfers between devices: 39.9 us -> 28.3 us
  other arithmetic: 7.58 us -> 1.31 us
    all_to_all x7 -> x3, waiting for transfers between devices: 41.1 us -> 150 us  [to_all(): return lax.all_to_all(x, axes, 0, 0, tiled=True)]
    all_to_all x4 -> x2, blocking collectives: 106 us -> 43.4 us  [to_all(): return lax.all_to_all(x, axes, 0, 0, tiled=True)]
    reduce_scatter x4 -> x0, waiting for transfers between devices: 28.9 us -> none  [body(): part = lax.psum_scatter(dense, 'z', scatter_dimension=0, tiled=True)]
    all_to_all x7 -> x3, starting transfers between devices: 39.8 us -> 28.3 us  [to_all(): return lax.all_to_all(x, axes, 0, 0, tiled=True)]
    unnamed x23 -> x16, local copies, waits for them, and re-layouts: 17.6 us -> 8.86 us
    squeeze x2 -> x0, local copies, waits for them, and re-layouts: 5.23 us -> none  [body(): got = lax.all_to_all(pieces[j], op, 0, 0, tiled=True)]
    reduce_sum x6 -> x2, other arithmetic: 5.27 us -> 0.62 us  [the longest x1 0.58 us: body(): gram = jnp.sum(spread(gram, op), axis=0)]
    pallas_call x6 -> x3, Pallas kernels: 16.1 us -> 18 us  [the longest x1 8.45 us: merge(): pl.pallas_call(merge_kernel, grid=(steps,), in_specs=[pl.BlockSpec(memory...]
  transfers between devices with their start and end apart: 11 -> 3, of which waited for: 6 -> 2; matrix products, arithmetic and copies ran while one was open for 5% -> 1% of each run, Pallas kernels for 5% -> 3%
where the time goes in v2:
time: 255 us; the launch traced here: 254 us
  waiting for transfers between devices  150 us (59%)
  blocking collectives  43.4 us (17%)
  starting transfers between devices  28.3 us (11%)
  Pallas kernels  18 us (7%)
  local copies, waits for them, and re-layouts  11 us (4%)
    all_to_all x3, waiting for transfers between devices, to_all(): return lax.all_to_all(x, axes, 0, 0, tiled=True)  150 us
    all_to_all x2, blocking collectives, to_all(): return lax.all_to_all(x, axes, 0, 0, tiled=True)  43.4 us
    all_to_all x3, starting transfers between devices, to_all(): return lax.all_to_all(x, axes, 0, 0, tiled=True)  28.3 us
    unnamed x16, local copies, waits for them, and re-layouts  8.86 us
    pallas_call x1, Pallas kernels, merge(): pl.pallas_call(merge_kernel, grid=(steps,), in_specs=[pl.BlockSpec(memory...  8.45 us
    pallas_call x1, Pallas kernels, contract(): pl.pallas_call(contract_kernel, grid=(cut, terms), in_specs=[pl.BlockSpec...  6.86 us
  transfers between devices with their start and end apart: 3, of which 2 were waited for; matrix products, arithmetic and copies ran while one was open for 1% of the time, Pallas kernels for 3%

profile of v2, /device:TPU:1, one launch (start us, length us, event | category | flops | bytes accessed | tf_op | source)
XLA Modules:
  0.0 254.0 jit_solution(13312005208848890379)
XLA Ops:
  0.6 0.9 broadcast_in_dim.8
  1.5 0.6 broadcast_in_dim.9
  2.1 8.6 %all-to-all-start = ((s32[32,1,32]{2,1,0:T(1,128)}), s32[32,1,32]{2,1,0:T(1,128)S(1)}, u32[]{:S(2)}, u32[]{:S(2)}) async-start(s32[32,1,32]{2,1,0:T(1,128)} %broadcast_in_dim.9), calls=%async_computation | async-start | bytes 32768 | tf_op jit(solution)/shard_map/all_to_all | solution.py:135
  10.7 1.6 copy-done.1
  12.3 2.2 copy-done.4
  14.5 2.2 copy-done.5
  16.7 6.9 %shard_map.77 = bf16[32,32,2,16,128]{4,3,2,1,0:T(8,128)(2,1)} custom-call(bf16[4,8,256,256]{3,2,1,0:T(8,128)(2,1)S(1)} %copy-done.4, bf16[4,8,256,256]{3,2,1,0:T(8,128)(2,1)S(1)} %copy-done.5, bf16[2,8,256,256]{3,2,1,0:T(8,128)(2,1)S(1)} %copy-done.1), custom_call_target="tpu_custom_call" | custom-call | flops 4294967296 | bytes 16777216 | tf_op jit(solution)/shard_map/pallas_call | solution.py:36
  23.5 7.4 %all-to-all-start.1 = ((bf16[32,32,2,16,128]{4,3,2,1,0:T(8,128)(2,1)}), bf16[32,32,2,16,128]{4,3,2,1,0:T(8,128)(2,1)}, u32[]{:S(2)}, u32[]{:S(2)}) async-start(bf16[32,32,2,16,128]{4,3,2,1,0:T(8,128)(2,1)} %shard_map.77), calls=%async_computation.1 | async-start | bytes 16777216 | tf_op jit(solution)/shard_map/all_to_all | solution.py:135
  31.0 0.5 broadcast.8
  31.5 0.7 reduce.3
  32.2 0.1 reshape.24.target_ref
  32.3 107.3 %all-to-all-done.1.pieces_ref = bf16[32,32,2,16,128]{4,3,2,1,0:T(8,128)(2,1)} async-done(((bf16[32,32,2,16,128]{4,3,2,1,0:T(8,128)(2,1)}), bf16[32,32,2,16,128]{4,3,2,1,0:T(8,128)(2,1)}, u32[]{:S(2)}, u32[]{:S(2)}) %all-to-all-start.1) | async-done | bytes 8388640 | tf_op jit(solution)/shard_map/all_to_all | solution.py:135
  139.5 8.5 %shard_map.78 = bf16[256,2,16,128]{3,2,1,0:T(8,128)(2,1)S(1)} custom-call(s32[1024]{0:T(1024)S(1)} %reshape.24.target_ref, bf16[32,32,2,16,128]{4,3,2,1,0:T(8,128)(2,1)} %all-to-all-done.1.pieces_ref), custom_call_target="tpu_custom_call" | custom-call | flops 4194304 | bytes 10485760 | tf_op jit(solution)/shard_map/pallas_call | solution.py:82
  148.0 1.3 copy-done.3
  149.3 12.3 %all-to-all-start.2 = ((bf16[32,8,2,16,128]{4,3,2,1,0:T(8,128)(2,1)}), bf16[32,8,2,16,128]{4,3,2,1,0:T(8,128)(2,1)}, u32[]{:S(2)}, u32[]{:S(2)}) async-start(bf16[32,8,2,16,128]{4,3,2,1,0:T(8,128)(2,1)} %bitcast.16), calls=%async_computation.2 | async-start | bytes 4194304 | tf_op jit(solution)/shard_map/all_to_all | solution.py:135
  161.6 0.3 convolution_bitcast_fusion.1
  161.9 0.5 copy-done.7
  162.5 1.3 fusion.refs_1_
  163.7 42.5 %all-to-all-done.2 = bf16[32,8,2,16,128]{4,3,2,1,0:T(8,128)(2,1)} async-done(((bf16[32,8,2,16,128]{4,3,2,1,0:T(8,128)(2,1)}), bf16[32,8,2,16,128]{4,3,2,1,0:T(8,128)(2,1)}, u32[]{:S(2)}, u32[]{:S(2)}) %all-to-all-start.2) | async-done | bytes 2097184 | tf_op jit(solution)/shard_map/all_to_all | solution.py:135
  206.2 1.0 copy-done.6
  207.3 2.7 %shard_map.79 = (bf16[2,8,32,256]{3,2,1,0:T(8,128)(2,1)}, f32[2,2]{1,0:T(2,128)S(1)}) custom-call(bf16[8,4,8,2,16,128]{5,4,3,2,1,0:T(8,128)(2,1)} %bitcast.1.refs_0_, f32[2,8,32,256]{3,2,1,0:T(8,128)S(1)} %copy-done.6, bf16[2,8,32,256]{3,2,1,0:T(8,128)(2,1)S(1)} %constant_dynamic-slice_fusion.refs_2_), custom_call_target="tpu_custom_call" | custom-call | tf_op jit(solution)/shard_map/pallas_call | solution.py:122
  210.0 16.7 %all_to_all.26 = f32[32,2,2]{2,1,0:T(2,128)S(1)} all-to-all(f32[32,2,2]{2,1,0:T(2,128)S(1)} %broadcast_in_dim.10), channel_id=1, replica_groups=mesh['z'=8,'x'=4,'y'=4,'core'=2] {'z','x'}, dimensions={0} | all-to-all | bytes 1024 | tf_op jit(solution)/shard_map/all_to_all | solution.py:135
  226.8 26.7 %all_to_all.27 = f32[8,2,2]{2,1,0:T(2,128)S(1)} all-to-all(f32[8,2,2]{2,1,0:T(2,128)S(1)} %broadcast_in_dim.22), channel_id=1, replica_groups=mesh['z'=8,'x'=4,'y'=4,'core'=2] {'y','core'}, dimensions={0} | all-to-all | bytes 256 | tf_op jit(solution)/shard_map/all_to_all | solution.py:135
  253.5 0.6 reduce_sum.19
  (15 shorter events, 0.1 us)
Async XLA Ops:
  0.6 161.0 %copy-start = (bf16[8,256,256]{2,1,0:T(8,128)(2,1)S(1)}, bf16[8,256,256]{2,1,0:T(8,128)(2,1)}, u32[]{:S(2)}) copy-start(bf16[8,256,256]{2,1,0:T(8,128)(2,1)} %param.10) | copy-start | bytes 3145732
  2.1 21.4 %all-to-all-start = ((s32[32,1,32]{2,1,0:T(1,128)}), s32[32,1,32]{2,1,0:T(1,128)S(1)}, u32[]{:S(2)}, u32[]{:S(2)}) async-start(s32[32,1,32]{2,1,0:T(1,128)} %broadcast_in_dim.9), calls=%async_computation | async-start | bytes 32768 | tf_op jit(solution)/shard_map/all_to_all | solution.py:135
  10.7 1.6 copy-start.1
  12.3 2.2 copy-start.4
  14.5 2.2 copy-start.5
  23.5 116.0 %all-to-all-start.1 = ((bf16[32,32,2,16,128]{4,3,2,1,0:T(8,128)(2,1)}), bf16[32,32,2,16,128]{4,3,2,1,0:T(8,128)(2,1)}, u32[]{:S(2)}, u32[]{:S(2)}) async-start(bf16[32,32,2,16,128]{4,3,2,1,0:T(8,128)(2,1)} %shard_map.77), calls=%async_computation.1 | async-start | bytes 16777216 | tf_op jit(solution)/shard_map/all_to_all | solution.py:135
  148.0 1.3 copy-start.3
  149.3 12.3 %copy-start.2 = (bf16[2,8,256,256]{3,2,1,0:T(8,128)(2,1)S(1)}, bf16[2,8,256,256]{3,2,1,0:T(8,128)(2,1)}, u32[]{:S(2)}) copy-start(bf16[2,8,256,256]{3,2,1,0:T(8,128)(2,1)} %trial_ref.1) | copy-start | bytes 6291460
  149.3 56.9 %all-to-all-start.2 = ((bf16[32,8,2,16,128]{4,3,2,1,0:T(8,128)(2,1)}), bf16[32,8,2,16,128]{4,3,2,1,0:T(8,128)(2,1)}, u32[]{:S(2)}, u32[]{:S(2)}) async-start(bf16[32,8,2,16,128]{4,3,2,1,0:T(8,128)(2,1)} %bitcast.16), calls=%async_computation.2 | async-start | bytes 4194304 | tf_op jit(solution)/shard_map/all_to_all | solution.py:135
  161.6 0.9 copy-start.7
  206.2 1.0 copy-start.6

commit v3 on v2

v3 whole, which is shorter than its diff:
```python
import functools

import jax
import jax.numpy as jnp
from jax import lax
from jax.experimental import pallas as pl
from jax.experimental.pallas import tpu as pltpu
from jax.sharding import Mesh
from jax.sharding import PartitionSpec as P

BF16 = jnp.bfloat16
F32 = jnp.float32
RING = 4
GROUPS = 8
SUB = 16
VMEM = pl.BlockSpec(memory_space=pltpu.VMEM)
SMEM = pl.BlockSpec(memory_space=pltpu.SMEM)
ANY = pl.BlockSpec(memory_space=pl.ANY)


def params(mib):
    return pltpu.CompilerParams(vmem_limit_bytes=mib * 2**20)


def contract_kernel(part, hint_ref, place_ref, slab_ref, left_ref, right_ref, trial_ref, *outs):
    step = pl.program_id(0)
    here, size = left_ref.shape[1], left_ref.shape[3]
    if part == 1:
        order = [SUB * (2 * r + 1) for r in range(GROUPS)]
    else:
        x, core = place_ref[0], place_ref[1]
        order = [
            pl.multiple_of(((x + k) % RING * 2 + c) * 2 * SUB, SUB)
            for c in (core, 1 - core)
            for k in range(RING)
        ]
    each = GROUPS // len(outs)

    @pl.when(step == 0)
    def _():
        for out in outs:
            for g in range(each):
                for v in range(2):
                    out[g, out.shape[1] - 1, v] = slab_ref[...]

    for s in range(here):
        rows = jnp.concatenate([left_ref[0, s, pl.ds(a, SUB), :] for a in order], axis=0)
        for v in range(2):
            half = jnp.dot(rows, trial_ref[v, s], preferred_element_type=F32).astype(BF16)
            piece = jnp.dot(half, right_ref[0, s], preferred_element_type=F32).astype(BF16)
            piece = piece.reshape(GROUPS, SUB, size)
            for n, out in enumerate(outs):
                out[:, step * here + s, v] = piece[n * each : (n + 1) * each]


def contract(part, hint, place, slab, trial, left_env, right_env):
    terms, here, size, _ = left_env.shape
    outs = (2, 1)[part]
    shape = (GROUPS // outs, terms * here + 1, 2, SUB, size)
    return pl.pallas_call(
        functools.partial(contract_kernel, part),
        grid=(terms,),
        in_specs=[
            ANY,
            SMEM,
            VMEM,
            pl.BlockSpec((1, here, size, size), lambda w: (w, 0, 0, 0)),
            pl.BlockSpec((1, here, size, size), lambda w: (w, 0, 0, 0)),
            pl.BlockSpec((2, here, size, size), lambda w: (0, 0, 0, 0)),
        ],
        out_specs=[pl.BlockSpec(shape, lambda w: (0, 0, 0, 0, 0))] * outs,
        out_shape=[jax.ShapeDtypeStruct(shape, BF16)] * outs,
        cost_estimate=pl.CostEstimate(
            flops=4 * terms * here * size**3,
            bytes_accessed=8 * terms * here * size * size,
            transcendentals=0,
        ),
        compiler_params=params(56),
    )(hint, place, slab, left_env, right_env, trial)


def pack_kernel(mine_ref, got_ref, *outs):
    for k in range(RING):
        outs[k][0] = mine_ref[k]
        outs[k][1] = got_ref[k]


def pack(mine, got):
    shape = jax.ShapeDtypeStruct((2, *mine.shape[1:]), BF16)
    return pl.pallas_call(
        pack_kernel,
        in_specs=[VMEM] * 2,
        out_specs=[VMEM] * RING,
        out_shape=[shape] * RING,
        cost_estimate=pl.CostEstimate(
            flops=0, bytes_accessed=14 * mine.size // 4, transcendentals=0
        ),
        compiler_params=params(60),
    )(mine, got)


def merge_kernel(z_first, hint_ref, *refs):
    ins, out = refs[:-4], refs[-4]
    rows, table, sums = refs[-3:]
    sources = [(ref, j) for ref in ins for j in range(ref.shape[0])]
    pairs = ins[0].shape[1] - 1

    def fetch(sem):
        for i, (ref, j) in enumerate(sources):
            rows[i : i + 1, :] = ref[j, pairs, 0, :, :128].astype(F32)[0:1].astype(jnp.int32)
        copy = pltpu.make_async_copy(rows, table, sem)
        copy.start()
        sums[...] = jnp.zeros_like(sums)
        copy.wait()

    pl.run_scoped(fetch, pltpu.SemaphoreType.DMA)
    for i, (ref, j) in enumerate(sources):

        def add(p, carry, i=i, ref=ref, j=j):
            t = table[i, p]
            slot = t if z_first else t // 8 % RING * 64 + t // 32 * 8 + t % 8
            sums[slot] += ref[j, p].astype(F32)
            return carry

        lax.fori_loop(0, pairs, add, 0, unroll=8)
    out[...] = sums[...].astype(BF16)


def merge(hint, blocks, sectors, z_first):
    block = blocks[0].shape[2:]
    return pl.pallas_call(
        functools.partial(merge_kernel, z_first),
        in_specs=[ANY] + [VMEM] * len(blocks),
        out_specs=VMEM,
        out_shape=jax.ShapeDtypeStruct((sectors, *block), BF16),
        scratch_shapes=[
            pltpu.VMEM((GROUPS, 128), jnp.int32),
            pltpu.SMEM((GROUPS, 128), jnp.int32),
            pltpu.VMEM((sectors, *block), F32),
        ],
        cost_estimate=pl.CostEstimate(flops=2**22, bytes_accessed=2**23, transcendentals=0),
        compiler_params=params(40),
    )(hint, *blocks)


def reduce_kernel(blocks, out):
    out[...] = sum(blocks[x].astype(F32) for x in range(RING)).astype(BF16)


def reduce(blocks):
    _, count, *rest = blocks.shape
    steps = 8
    return pl.pallas_call(
        reduce_kernel,
        grid=(steps,),
        in_specs=[pl.BlockSpec((RING, count // steps, *rest), lambda i: (0, i, 0, 0, 0))],
        out_specs=pl.BlockSpec((count // steps, *rest), lambda i: (i, 0, 0, 0)),
        out_shape=jax.ShapeDtypeStruct((count, *rest), BF16),
        cost_estimate=pl.CostEstimate(flops=2**22, bytes_accessed=2**22, transcendentals=0),
        compiler_params=params(24),
    )(blocks)


def finish_kernel(scale, first, second, local, trial_rows, out, gram):
    size = out.shape[-1]
    found = [[jnp.zeros((SUB, size), F32) for _ in range(2)] for _ in range(2)]
    for half in range(2):
        rows = slice(half * SUB, (half + 1) * SUB)
        for b in range(2):
            if half == 0:
                total = first[:, b].astype(F32)
            else:
                total = sum(second[z, :, b].astype(F32) for z in range(second.shape[0]))
            total = total + local[b, :, rows]
            out[b, :, rows] = total.astype(BF16)
            for a in range(2):
                found[a][b] += jnp.sum(trial_rows[a, :, rows].astype(F32) * total, axis=0)
    for a in range(2):
        for b in range(2):
            gram[a, b] = jnp.sum(found[a][b]) * scale


def finish(scale, *args):
    local = args[2]
    return pl.pallas_call(
        functools.partial(finish_kernel, scale),
        in_specs=[VMEM] * 4,
        out_specs=[VMEM, SMEM],
        out_shape=[
            jax.ShapeDtypeStruct(local.shape, BF16),
            jax.ShapeDtypeStruct((2, 2), F32),
        ],
        cost_estimate=pl.CostEstimate(flops=2**21, bytes_accessed=2**21, transcendentals=0),
        compiler_params=params(24),
    )(*args)


def to_all(x, axes):
    return lax.all_to_all(x, axes, 0, 0, tiled=True)


def spread(x, axes):
    return to_all(jnp.broadcast_to(x[None], (lax.axis_size(axes), *x.shape)), axes)


def shift(x, axis, k):
    n = lax.axis_size(axis)
    return lax.ppermute(x, axis, [(i, (i + k) % n) for i in range(n)])


def swap(x):
    return lax.ppermute(x, "core", [(0, 1), (1, 0)])


def turn(x):
    pairs = [(a * RING + b, b * RING + a) for a in range(RING) for b in range(RING)]
    return lax.ppermute(x, ("x", "y"), pairs)


def body(trial, left_env, right_env, left_block_ham, right_block_ham, target):
    op = ("y", "core")
    nz, nx = lax.axis_size("z"), lax.axis_size("x")
    terms, here, size, _ = left_env.shape
    sectors = nz * nx * here
    rows = size // lax.axis_size(op)
    places = [lax.axis_index(name) for name in ("x", "core", "y", "z")]
    place = jnp.stack(places)
    place = place.astype(jnp.int32)
    pairs = terms * here
    slab = jnp.pad(target.reshape(1, pairs).astype(BF16), ((0, SUB - 1), (0, size - pairs)))

    first_row = lax.axis_index(op) * rows
    trial_rows = lax.dynamic_slice_in_dim(trial, first_row, rows, 2)
    local = jnp.einsum("sij,vsjk->vsik", left_block_ham, trial, preferred_element_type=F32)
    local = local + jnp.einsum(
        "vsij,sjk->vsik", trial_rows, right_block_ham, preferred_element_type=F32
    )

    (pieces,) = contract(1, slab, place, slab, trial, left_env, right_env)
    mine, other = contract(0, pieces, place, slab, trial, left_env, right_env)
    pieces = to_all(pieces, op)
    packed = pack(mine, swap(other))
    arrived = [shift(packed[k], "x", k) for k in range(1, RING)]

    blocks = merge(slab, [pieces], sectors, False)
    dense = merge(blocks, [packed[0], *arrived], sectors, True)
    blocks = to_all(blocks.reshape(nx, nz * here, 2, SUB, size), "x")
    reduced = lax.psum_scatter(dense, "z", scatter_dimension=0, tiled=True)
    second = to_all(reduce(blocks).reshape(nz, here, 2, SUB, size), "z")

    reduced = reduced.reshape(nx, here, 2, SUB, size)
    y = places[2]
    first = lax.dynamic_index_in_dim(reduced, y, 0, keepdims=False).astype(F32)
    for k in range(1, RING):
        block = lax.dynamic_index_in_dim(reduced, (y + k) % RING, 0, keepdims=False)
        first = first + shift(block, "y", k).astype(F32)
    first = turn(first.astype(BF16))

    scale = 1.0 / (sectors * size * size)
    hpsi, gram = finish(scale, first, second, local, trial_rows)
    gram = jnp.sum(spread(gram, ("z", "x")), axis=0)
    gram = jnp.sum(spread(gram, op), axis=0)
    return hpsi, gram


def solution(mesh):
    sizes = {"z": 8, "x": 4, "y": 4, "core": 2}
    fine = Mesh(mesh.devices.reshape(tuple(sizes.values())), tuple(sizes))
    sec, op = ("z", "x"), ("y", "core")
    return jax.shard_map(
        body,
        mesh=fine,
        in_specs=(
            P(None, sec, None, None),
            P(op, sec, None, None),
            P(op, sec, None, None),
            P(sec, op, None),
            P(sec, None, None),
            P(op, sec),
        ),
        out_specs=(P(None, sec, op, None), P()),
        check_vma=False,
    )
```

time: 255 us -> 227 us (0.89)
  waiting for transfers between devices: 150 us -> 60.3 us
  blocking collectives: 43.4 us -> 77.2 us
  Pallas kernels: 18 us -> 37.5 us
  between operations: 0.76 us -> 14.1 us
  starting transfers between devices: 28.3 us -> 22.7 us
  local copies, waits for them, and re-layouts: 11 us -> 8.1 us
    all_to_all x3 -> x2, waiting for transfers between devices: 150 us -> 39.1 us  [to_all(): return lax.all_to_all(x, axes, 0, 0, tiled=True)]
    all_to_all x2 -> x3, blocking collectives: 43.4 us -> 77.2 us  [to_all(): return lax.all_to_all(x, axes, 0, 0, tiled=True)]
    ppermute x0 -> x8, waiting for transfers between devices: none -> 21.1 us  [the longest x6 16.9 us: shift(): return lax.ppermute(x, axis, [(i, (i + k) % n) for i in range(n)])]
    pallas_call x3 -> x7, Pallas kernels: 18 us -> 37.5 us  [the longest x2 17.1 us: contract(): pl.pallas_call(functools.partial(contract_kernel, part), grid=(terms,), i...]
    all_to_all x3 -> x2, starting transfers between devices: 28.3 us -> 14.1 us  [to_all(): return lax.all_to_all(x, axes, 0, 0, tiled=True)]
    ppermute x0 -> x8, starting transfers between devices: none -> 8.61 us  [the longest x6 6.87 us: shift(): return lax.ppermute(x, axis, [(i, (i + k) % n) for i in range(n)])]
    unnamed x16 -> x12, local copies, waits for them, and re-layouts: 8.86 us -> 5.36 us
  transfers between devices with their start and end apart: 3 -> 11, of which waited for: 2 -> 8; matrix products, arithmetic and copies ran while one was open for 1% -> 3% of each run, Pallas kernels for 3% -> 10%
where the time goes in v3:
time: 227 us; the launch traced here: 226 us
  blocking collectives  77.2 us (34%)
  waiting for transfers between devices  60.3 us (27%)
  Pallas kernels  37.5 us (17%)
  starting transfers between devices  22.7 us (10%)
  between operations  14.1 us (6%)
  local copies, waits for them, and re-layouts  8.1 us (4%)
  other arithmetic  3.7 us (2%)
  matrix products  2.4 us (1%)
    all_to_all x3, blocking collectives, to_all(): return lax.all_to_all(x, axes, 0, 0, tiled=True)  77.2 us
    all_to_all x2, waiting for transfers between devices, to_all(): return lax.all_to_all(x, axes, 0, 0, tiled=True)  39.1 us
    pallas_call x2, Pallas kernels, contract(): pl.pallas_call(functools.partial(contract_kernel, part), grid=(terms,), i...  17.1 us
    ppermute x6, waiting for transfers between devices, shift(): return lax.ppermute(x, axis, [(i, (i + k) % n) for i in range(n)])  16.9 us
    all_to_all x2, starting transfers between devices, to_all(): return lax.all_to_all(x, axes, 0, 0, tiled=True)  14.1 us
    pallas_call x2, Pallas kernels, merge(): pl.pallas_call(functools.partial(merge_kernel, z_first), in_specs=[ANY] +...  11.9 us
    ppermute x6, starting transfers between devices, shift(): return lax.ppermute(x, axis, [(i, (i + k) % n) for i in range(n)])  6.87 us
    unnamed x12, local copies, waits for them, and re-layouts  5.36 us
  transfers between devices with their start and end apart: 11, of which 8 were waited for; matrix products, arithmetic and copies ran while one was open for 3% of the time, Pallas kernels for 10%

profile of v3, /device:TPU:1, one launch (start us, length us, event | category | flops | bytes accessed | tf_op | source)
XLA Modules:
  0.0 226.0 jit_solution(5713749429198838148)
XLA Ops:
  9.3 8.5 %shard_map.77.hint_ref = bf16[8,33,2,16,256]{4,3,2,1,0:T(8,128)(2,1)} custom-call(bf16[16,256]{1,0:T(8,128)(2,1)} %pad.4.hint_ref.slab_ref, s32[4]{0:T(128)} %pad_add_fusion.place_ref, bf16[16,256]{1,0:T(8,128)(2,1)} %pad.4.hint_ref.slab_ref, bf16[4,8,256,256]{3,2,1,0:T(8,128)(2,1)} %left_ref.3, bf16[4,8,256,256]{3,2,1,0:T(8,128)(2,1)} %right_ref.3, ...), custom_call_target="tpu_custom_call" | custom-call | flops 2147483648 | bytes 16777216 | tf_op jit(solution)/shard_map/pallas_call | solution.py:60
  17.8 7.7 %all-to-all-start = ((bf16[8,33,2,16,256]{4,3,2,1,0:T(8,128)(2,1)}), bf16[8,33,2,16,256]{4,3,2,1,0:T(8,128)(2,1)}, u32[]{:S(2)}, u32[]{:S(2)}) async-start(bf16[8,33,2,16,256]{4,3,2,1,0:T(8,128)(2,1)} %shard_map.77.hint_ref), calls=%async_computation | async-start | bytes 8650752 | tf_op jit(solution)/shard_map/all_to_all | solution.py:199
  25.4 8.6 %shard_map.79 = (bf16[4,33,2,16,256]{4,3,2,1,0:T(8,128)(2,1)}, bf16[4,33,2,16,256]{4,3,2,1,0:T(8,128)(2,1)}) custom-call(bf16[8,33,2,16,256]{4,3,2,1,0:T(8,128)(2,1)} %shard_map.77.hint_ref, s32[4]{0:T(128)} %pad_add_fusion.place_ref, bf16[16,256]{1,0:T(8,128)(2,1)} %pad.4.hint_ref.slab_ref, bf16[4,8,256,256]{3,2,1,0:T(8,128)(2,1)} %left_ref.3, ...), custom_call_target="tpu_custom_call" | custom-call | flops 2147483648 | bytes 16777216 | tf_op jit(solution)/shard_map/pallas_call | solution.py:60
  34.2 4.3 %collective-permute-done.got_ref = bf16[4,33,2,16,256]{4,3,2,1,0:T(8,128)(2,1)S(1)} collective-permute-done((bf16[4,33,2,16,256]{4,3,2,1,0:T(8,128)(2,1)}, bf16[4,33,2,16,256]{4,3,2,1,0:T(8,128)(2,1)S(1)}, u32[]{:S(2)}, u32[]{:S(2)}) %collective-permute-start) | collective-permute-done | bytes 2162720 | tf_op jit(solution)/shard_map/ppermute | solution.py:212
  39.9 4.3 %shard_map.80 = (bf16[2,33,2,16,256]{4,3,2,1,0:T(8,128)(2,1)}, bf16[2,33,2,16,256]{4,3,2,1,0:T(8,128)(2,1)}, bf16[2,33,2,16,256]{4,3,2,1,0:T(8,128)(2,1)}, bf16[2,33,2,16,256]{4,3,2,1,0:T(8,128)(2,1)}) custom-call(bf16[4,33,2,16,256]{4,3,2,1,0:T(8,128)(2,1)} %get-tuple-element.10.mine_ref, bf16[4,33,2,16,256]{4,3,2,1,0:T(8,128)(2,1)} %copy-done.5), custom_call_target="tpu_custom_call" | custom-call | bytes 3784704 | tf_op jit(solution)/shard_map/pallas_call | solution.py:90
  44.2 2.0 collective-permute-start.2
  47.3 28.4 %all-to-all-done.refs_0_ = bf16[8,33,2,16,256]{4,3,2,1,0:T(8,128)(2,1)} async-done(((bf16[8,33,2,16,256]{4,3,2,1,0:T(8,128)(2,1)}), bf16[8,33,2,16,256]{4,3,2,1,0:T(8,128)(2,1)}, u32[]{:S(2)}, u32[]{:S(2)}) %all-to-all-start) | async-done | bytes 4325408 | tf_op jit(solution)/shard_map/all_to_all | solution.py:199
  75.8 7.4 %shard_map.78.hint_ref = bf16[256,2,16,256]{3,2,1,0:T(8,128)(2,1)S(1)} custom-call(bf16[16,256]{1,0:T(8,128)(2,1)S(1)} %copy-done.4, bf16[8,33,2,16,256]{4,3,2,1,0:T(8,128)(2,1)} %all-to-all-done.refs_0_), custom_call_target="tpu_custom_call" | custom-call | flops 4194304 | bytes 8388608 | tf_op jit(solution)/shard_map/pallas_call | solution.py:131
  83.2 10.9 %collective-permute-done.1.refs_1_ = bf16[2,33,2,16,256]{4,3,2,1,0:T(8,128)(2,1)S(1)} collective-permute-done((bf16[2,33,2,16,256]{4,3,2,1,0:T(8,128)(2,1)}, bf16[2,33,2,16,256]{4,3,2,1,0:T(8,128)(2,1)S(1)}, u32[]{:S(2)}, u32[]{:S(2)}) %collective-permute-start.1) | collective-permute-done | bytes 1081376 | tf_op jit(solution)/shard_map/ppermute | solution.py:208
  94.5 4.5 %shard_map.81 = bf16[256,2,16,256]{3,2,1,0:T(8,128)(2,1)S(1)} custom-call(bf16[256,2,16,256]{3,2,1,0:T(8,128)(2,1)S(1)} %shard_map.78.hint_ref, bf16[2,33,2,16,256]{4,3,2,1,0:T(8,128)(2,1)S(1)} %copy-done.3, bf16[2,33,2,16,256]{4,3,2,1,0:T(8,128)(2,1)S(1)} %collective-permute-done.1.refs_1_, bf16[2,33,2,16,256]{4,3,2,1,0:T(8,128)(2,1)} %collective-permute-done.2.refs_2_, ...), custom_call_target="tpu_custom_call" | custom-call | flops 4194304 | bytes 8388608 | tf_op jit(solution)/shard_map/pallas_call | solution.py:131
  99.0 2.0 copy-done.1
  101.0 2.0 copy-done.2
  103.0 52.3 %all_to_all.25.blocks = bf16[4,64,2,16,256]{4,3,2,1,0:T(8,128)(2,1)S(1)} all-to-all(bf16[4,64,2,16,256]{4,3,2,1,0:T(8,128)(2,1)} %bitcast.30), channel_id=1, replica_groups=mesh['z'=8,'x'=4,'y'=4,'core'=2] {'x'}, dimensions={0} | all-to-all | bytes 8388608 | tf_op jit(solution)/shard_map/all_to_all | solution.py:199
  155.2 3.2 %shard_map.82 = bf16[64,2,16,256]{3,2,1,0:T(8,128)(2,1)} custom-call(bf16[4,64,2,16,256]{4,3,2,1,0:T(8,128)(2,1)S(1)} %all_to_all.25.blocks), custom_call_target="tpu_custom_call" | custom-call | flops 4194304 | bytes 4194304 | tf_op jit(solution)/shard_map/pallas_call | solution.py:153
  158.4 6.4 %all-to-all-start.2 = ((bf16[8,8,2,16,256]{4,3,2,1,0:T(8,128)(2,1)}), bf16[8,8,2,16,256]{4,3,2,1,0:T(8,128)(2,1)S(1)}, u32[]{:S(2)}, u32[]{:S(2)}) async-start(bf16[8,8,2,16,256]{4,3,2,1,0:T(8,128)(2,1)} %bitcast.10), calls=%async_computation.3 | async-start | bytes 2097152 | tf_op jit(solution)/shard_map/all_to_all | solution.py:199
  166.9 2.6 %collective-permute-start.6 = (bf16[8,2,16,256]{3,2,1,0:T(8,128)(2,1)S(1)}, bf16[8,2,16,256]{3,2,1,0:T(8,128)(2,1)S(1)}, u32[]{:S(2)}, u32[]{:S(2)}) collective-permute-start(bf16[8,2,16,256]{3,2,1,0:T(8,128)(2,1)S(1)} %get-tuple-element.19), channel_id=1, source_target_pairs={{0,6},{2,0},{4,2},{6,4},{1,7},{3,1},{5,3},{7,5},{8,14},{10,8},{12,... | collective-permute-start | bytes 393224 | tf_op jit(solution)/shard_map/ppermute | solution.py:208
  172.3 2.8 %collective-permute-done.5 = bf16[8,2,16,256]{3,2,1,0:T(8,128)(2,1)S(1)} collective-permute-done((bf16[8,2,16,256]{3,2,1,0:T(8,128)(2,1)S(1)}, bf16[8,2,16,256]{3,2,1,0:T(8,128)(2,1)S(1)}, u32[]{:S(2)}, u32[]{:S(2)}) %collective-permute-start.5) | collective-permute-done | bytes 131104 | tf_op jit(solution)/shard_map/ppermute | solution.py:208
  175.1 1.4 collective-permute-done.4
  176.5 1.7 fusion.4
  178.2 1.6 collective-permute-start.7
  179.8 2.1 fusion.local
  181.9 10.7 %all-to-all-done.2.second = bf16[8,8,2,16,256]{4,3,2,1,0:T(8,128)(2,1)S(1)} async-done(((bf16[8,8,2,16,256]{4,3,2,1,0:T(8,128)(2,1)}), bf16[8,8,2,16,256]{4,3,2,1,0:T(8,128)(2,1)S(1)}, u32[]{:S(2)}, u32[]{:S(2)}) %all-to-all-start.2) | async-done | bytes 1048608 | tf_op jit(solution)/shard_map/all_to_all | solution.py:199
  193.6 12.0 %all_to_all.26 = f32[32,2,2]{2,1,0:T(2,128)S(1)} all-to-all(f32[32,2,2]{2,1,0:T(2,128)S(1)} %broadcast_in_dim.4), channel_id=1, replica_groups=mesh['z'=8,'x'=4,'y'=4,'core'=2] {'z','x'}, dimensions={0} | all-to-all | bytes 1024 | tf_op jit(solution)/shard_map/all_to_all | solution.py:199
  205.6 13.0 %all_to_all.27 = f32[8,2,2]{2,1,0:T(2,128)S(1)} all-to-all(f32[8,2,2]{2,1,0:T(2,128)S(1)} %broadcast_in_dim.5), channel_id=1, replica_groups=mesh['z'=8,'x'=4,'y'=4,'core'=2] {'y','core'}, dimensions={0} | all-to-all | bytes 256 | tf_op jit(solution)/shard_map/all_to_all | solution.py:199
  (34 shorter events, 11.8 us)
Async XLA Ops:
  7.2 163.5 %copy-start = (bf16[8,256,256]{2,1,0:T(8,128)(2,1)S(1)}, bf16[8,256,256]{2,1,0:T(8,128)(2,1)}, u32[]{:S(2)}) copy-start(bf16[8,256,256]{2,1,0:T(8,128)(2,1)} %param.10) | copy-start | bytes 3145732
  17.8 58.0 %all-to-all-start = ((bf16[8,33,2,16,256]{4,3,2,1,0:T(8,128)(2,1)}), bf16[8,33,2,16,256]{4,3,2,1,0:T(8,128)(2,1)}, u32[]{:S(2)}, u32[]{:S(2)}) async-start(bf16[8,33,2,16,256]{4,3,2,1,0:T(8,128)(2,1)} %shard_map.77.hint_ref), calls=%async_computation | async-start | bytes 8650752 | tf_op jit(solution)/shard_map/all_to_all | solution.py:199
  25.4 140.4 %reduce-scatter.2.cloned.1.call-start = ((), (), s32[]{:S(2)}) async-start(), calls=%async_computation.6 | async-start | bytes 4718592 | tf_op jit(solution)/shard_map/reduce_scatter | solution.py:248
  34.0 4.5 %collective-permute-start = (bf16[4,33,2,16,256]{4,3,2,1,0:T(8,128)(2,1)}, bf16[4,33,2,16,256]{4,3,2,1,0:T(8,128)(2,1)S(1)}, u32[]{:S(2)}, u32[]{:S(2)}) collective-permute-start(bf16[4,33,2,16,256]{4,3,2,1,0:T(8,128)(2,1)} %get-tuple-element.11), channel_id=1, source_target_pairs={{0,1},{1,0},{2,3},{3,2},{4,5},{5,4},{6,7},{7,6},{8,9},{9,8},{10,11... | collective-permute-start | bytes 6488072 | tf_op jit(solution)/shard_map/ppermute | solution.py:212
  38.5 1.4 copy-start.5
  39.9 35.9 %copy-start.4 = (bf16[16,256]{1,0:T(8,128)(2,1)S(1)}, bf16[16,256]{1,0:T(8,128)(2,1)}, u32[]{:S(2)}) copy-start(bf16[16,256]{1,0:T(8,128)(2,1)} %pad.4.hint_ref.slab_ref) | copy-start | bytes 24580
  44.2 49.9 %collective-permute-start.1 = (bf16[2,33,2,16,256]{4,3,2,1,0:T(8,128)(2,1)}, bf16[2,33,2,16,256]{4,3,2,1,0:T(8,128)(2,1)S(1)}, u32[]{:S(2)}, u32[]{:S(2)}) collective-permute-start(bf16[2,33,2,16,256]{4,3,2,1,0:T(8,128)(2,1)} %get-tuple-element.13), channel_id=1, source_target_pairs={{0,8},{8,16},{16,24},{24,0},{1,9},{9,17},{17,25},{25,1},{2,10},{10... | collective-permute-start | bytes 3244040 | tf_op jit(solution)/shard_map/ppermute | solution.py:208
  44.2 49.9 %collective-permute-start.2 = (bf16[2,33,2,16,256]{4,3,2,1,0:T(8,128)(2,1)}, bf16[2,33,2,16,256]{4,3,2,1,0:T(8,128)(2,1)}, u32[]{:S(2)}, u32[]{:S(2)}) collective-permute-start(bf16[2,33,2,16,256]{4,3,2,1,0:T(8,128)(2,1)} %get-tuple-element.14), channel_id=1, source_target_pairs={{0,16},{8,24},{16,0},{24,8},{1,17},{9,25},{17,1},{25,9},{2,18},{10... | collective-permute-start | bytes 3244040 | tf_op jit(solution)/shard_map/ppermute | solution.py:208
  46.2 48.3 %copy-start.3 = (bf16[2,33,2,16,256]{4,3,2,1,0:T(8,128)(2,1)S(1)}, bf16[2,33,2,16,256]{4,3,2,1,0:T(8,128)(2,1)}, u32[]{:S(2)}) copy-start(bf16[2,33,2,16,256]{4,3,2,1,0:T(8,128)(2,1)} %get-tuple-element.12.refs_0_) | copy-start | bytes 3244036
  46.2 48.3 %collective-permute-start.3 = (bf16[2,33,2,16,256]{4,3,2,1,0:T(8,128)(2,1)}, bf16[2,33,2,16,256]{4,3,2,1,0:T(8,128)(2,1)}, u32[]{:S(2)}, u32[]{:S(2)}) collective-permute-start(bf16[2,33,2,16,256]{4,3,2,1,0:T(8,128)(2,1)} %get-tuple-element.15), channel_id=1, source_target_pairs={{0,24},{8,0},{16,8},{24,16},{1,25},{9,1},{17,9},{25,17},{2,26},{10... | collective-permute-start | bytes 3244040 | tf_op jit(solution)/shard_map/ppermute | solution.py:208
  99.0 2.0 copy-start.1
  101.0 2.0 copy-start.2
  158.4 34.1 %all-to-all-start.2 = ((bf16[8,8,2,16,256]{4,3,2,1,0:T(8,128)(2,1)}), bf16[8,8,2,16,256]{4,3,2,1,0:T(8,128)(2,1)S(1)}, u32[]{:S(2)}, u32[]{:S(2)}) async-start(bf16[8,8,2,16,256]{4,3,2,1,0:T(8,128)(2,1)} %bitcast.10), calls=%async_computation.3 | async-start | bytes 2097152 | tf_op jit(solution)/shard_map/all_to_all | solution.py:199
  166.9 5.4 %collective-permute-start.6 = (bf16[8,2,16,256]{3,2,1,0:T(8,128)(2,1)S(1)}, bf16[8,2,16,256]{3,2,1,0:T(8,128)(2,1)S(1)}, u32[]{:S(2)}, u32[]{:S(2)}) collective-permute-start(bf16[8,2,16,256]{3,2,1,0:T(8,128)(2,1)S(1)} %get-tuple-element.19), channel_id=1, source_target_pairs={{0,6},{2,0},{4,2},{6,4},{1,7},{3,1},{5,3},{7,5},{8,14},{10,8},{12,... | collective-permute-start | bytes 393224 | tf_op jit(solution)/shard_map/ppermute | solution.py:208
  169.5 5.6 %collective-permute-start.5 = (bf16[8,2,16,256]{3,2,1,0:T(8,128)(2,1)S(1)}, bf16[8,2,16,256]{3,2,1,0:T(8,128)(2,1)S(1)}, u32[]{:S(2)}, u32[]{:S(2)}) collective-permute-start(bf16[8,2,16,256]{3,2,1,0:T(8,128)(2,1)S(1)} %get-tuple-element.20), channel_id=1, source_target_pairs={{0,4},{2,6},{4,0},{6,2},{1,5},{3,7},{5,1},{7,3},{8,12},{10,14},{12... | collective-permute-start | bytes 393224 | tf_op jit(solution)/shard_map/ppermute | solution.py:208
  170.1 6.4 %collective-permute-start.4 = (bf16[8,2,16,256]{3,2,1,0:T(8,128)(2,1)S(1)}, bf16[8,2,16,256]{3,2,1,0:T(8,128)(2,1)}, u32[]{:S(2)}, u32[]{:S(2)}) collective-permute-start(bf16[8,2,16,256]{3,2,1,0:T(8,128)(2,1)S(1)} %get-tuple-element.18), channel_id=1, source_target_pairs={{0,2},{2,4},{4,6},{6,0},{1,3},{3,5},{5,7},{7,1},{8,10},{10,12},{12... | collective-permute-start | bytes 393224 | tf_op jit(solution)/shard_map/ppermute | solution.py:208
  178.2 14.3 %collective-permute-start.7 = (bf16[8,2,16,256]{3,2,1,0:T(8,128)(2,1)}, bf16[8,2,16,256]{3,2,1,0:T(8,128)(2,1)S(1)}, u32[]{:S(2)}, u32[]{:S(2)}) collective-permute-start(bf16[8,2,16,256]{3,2,1,0:T(8,128)(2,1)} %fusion.4), channel_id=1, source_target_pairs={{0,0},{2,8},{4,16},{6,24},{8,2},{10,10},{12,18},{14,26},{16,4},{18... | collective-permute-start | bytes 393224 | tf_op jit(solution)/shard_map/ppermute | solution.py:217
Sparse Core Ops, SparseCore 0:
  103.1 57.2 reduce-scatter.1

commit v4 on v3

v4 whole, which is shorter than its diff:
```python
import functools

import jax
import jax.numpy as jnp
from jax import lax
from jax.experimental import pallas as pl
from jax.experimental.pallas import tpu as pltpu
from jax.sharding import Mesh
from jax.sharding import PartitionSpec as P

BF16 = jnp.bfloat16
F32 = jnp.float32
RING = 4
GROUPS = 8
SUB = 16
STEPS = 8
VMEM = pl.BlockSpec(memory_space=pltpu.VMEM)
SMEM = pl.BlockSpec(memory_space=pltpu.SMEM)
HBM = pl.BlockSpec(memory_space=pltpu.HBM)


def params(mib):
    return pltpu.CompilerParams(vmem_limit_bytes=mib * 2**20)


def contract_kernel(target_ref, left_ref, right_ref, trial_ref, *refs):
    outs, (stage, slab, wide, sems, slab_sems) = refs[: 1 + RING], refs[1 + RING :]
    step = pl.program_id(0)
    last = pl.num_programs(0) - 1
    here, size = left_ref.shape[1], left_ref.shape[3]
    x, core = lax.axis_index("x"), lax.axis_index("core")
    order = [SUB * (2 * r + 1) for r in range(GROUPS)]
    order += [
        pl.multiple_of(((x + k) % RING * 2 + c) * 2 * SUB, SUB)
        for k in range(RING)
        for c in (core, 1 - core)
    ]
    places = [(0, GROUPS)] + [(GROUPS + 2 * k, 2) for k in range(RING)]

    def copies(i):
        rows = pl.ds(i * here, here)
        return [
            pltpu.make_async_copy(
                stage.at[i % 2, pl.ds(a, n)], out.at[:, rows], sems.at[i % 2, j]
            )
            for j, (out, (a, n)) in enumerate(zip(outs, places, strict=True))
        ]

    def slab_copies():
        return [
            pltpu.make_async_copy(
                slab.at[pl.ds(0, n)], out.at[:, pl.ds(here * (last + 1), 1)], slab_sems.at[j]
            )
            for j, (out, (_, n)) in enumerate(zip(outs, places, strict=True))
        ]

    @pl.when(step == 0)
    def _():
        wide[...] = jnp.zeros_like(wide)
        wide[:4, :8] = target_ref[...].astype(F32)
        for g in range(GROUPS):
            for v in range(2):
                slab[g, 0, v] = wide[...].astype(BF16)
        for copy in slab_copies():
            copy.start()

    @pl.when(step >= 2)
    def _():
        for copy in copies(step - 2):
            copy.wait()

    for s in range(here):
        rows = jnp.concatenate([left_ref[0, s, pl.ds(a, SUB), :] for a in order], axis=0)
        half = [
            jnp.dot(rows, trial_ref[v, s], preferred_element_type=F32).astype(BF16)
            for v in range(2)
        ]
        half = jnp.concatenate(half, axis=0)
        piece = jnp.dot(half, right_ref[0, s], preferred_element_type=F32).astype(BF16)
        piece = piece.reshape(2, 2 * GROUPS, SUB, size)
        for v in range(2):
            stage[step % 2, :, s, v] = piece[v]
    for copy in copies(step):
        copy.start()

    @pl.when(step == last)
    def _():
        for copy in copies(step - 1) + copies(step) + slab_copies():
            copy.wait()


def contract(target, trial, left_env, right_env):
    terms, here, size, _ = left_env.shape
    shapes = [(n, terms * here + 1, 2, SUB, size) for n in (GROUPS, 2, 2, 2, 2)]
    return pl.pallas_call(
        contract_kernel,
        grid=(terms,),
        in_specs=[
            VMEM,
            pl.BlockSpec((1, here, size, size), lambda w: (w, 0, 0, 0)),
            pl.BlockSpec((1, here, size, size), lambda w: (w, 0, 0, 0)),
            pl.BlockSpec((2, here, size, size), lambda w: (0, 0, 0, 0)),
        ],
        out_specs=[HBM] * len(shapes),
        out_shape=[jax.ShapeDtypeStruct(shape, BF16) for shape in shapes],
        scratch_shapes=[
            pltpu.VMEM((2, 2 * GROUPS, here, 2, SUB, size), BF16),
            pltpu.VMEM((GROUPS, 1, 2, SUB, size), BF16),
            pltpu.VMEM((SUB, size), F32),
            pltpu.SemaphoreType.DMA((2, len(shapes))),
            pltpu.SemaphoreType.DMA((len(shapes),)),
        ],
        cost_estimate=pl.CostEstimate(
            flops=8 * terms * here * size**3,
            bytes_accessed=8 * terms * here * size * size,
            transcendentals=0,
        ),
        compiler_params=params(56),
    )(target, left_env, right_env, trial)


def pack_kernel(*refs):
    ins, out, sems = refs[:RING], refs[-2], refs[-1]
    copies = [
        pltpu.make_async_copy(ref.at[1], out.at[k], sems.at[k]) for k, ref in enumerate(ins)
    ]
    for copy in copies:
        copy.start()
    for copy in copies:
        copy.wait()


def pack(blocks):
    shape = blocks[0].shape[1:]
    return pl.pallas_call(
        pack_kernel,
        in_specs=[HBM] * RING,
        out_specs=HBM,
        out_shape=jax.ShapeDtypeStruct((RING, *shape), BF16),
        scratch_shapes=[pltpu.SemaphoreType.DMA((RING,))],
        cost_estimate=pl.CostEstimate(
            flops=0, bytes_accessed=4 * blocks[0].size, transcendentals=0
        ),
        compiler_params=params(24),
    )(*blocks)


def merge_kernel(z_first, hint_ref, *refs):
    rows, table, sums, stage, table_sem, sems = refs[-6:]
    ins, outs = (refs[: RING + 1], refs[RING + 1 : -6]) if z_first else (refs[:1], refs[1:-6])
    sources = [(ref, j) for ref in ins for j in range(ref.shape[0])]
    pairs = ins[0].shape[1] - 1
    for i, (ref, j) in enumerate(sources):
        line = ref[j, pairs, 0, :, :128].astype(F32)[:8]
        rows[8 * i : 8 * i + 8, :] = line.astype(jnp.int32)
    copy = pltpu.make_async_copy(rows, table, table_sem)
    copy.start()
    sums[...] = jnp.zeros_like(sums)
    copy.wait()
    here = lax.axis_index("z")
    for i, (ref, j) in enumerate(sources):

        def add_line(w, carry, i=i, ref=ref, j=j):
            for s in range(8):
                t = table[8 * i + w, s]
                if z_first:
                    slot = (t // 32 - here) % 8 * 32 + t % 32
                else:
                    slot = t // 8 % RING * 64 + t // 32 * 8 + t % 8
                sums[slot] += ref[j, w * 8 + s].astype(F32)
            return carry

        lax.fori_loop(0, pairs // 8, add_line, 0)
    some = sums.shape[0] // STEPS
    copies = []
    for n in range(STEPS):
        part = pl.ds(n * some, some)
        stage[part] = sums[part].astype(BF16)
        if not z_first:
            pieces = [(part, outs[0].at[part])]
        elif n == 4:
            pieces = [(pl.ds((8 + m) * some // 2, some // 2), outs[1 + m]) for m in range(2)]
        else:
            pieces = [(part, outs[0].at[n])]
        for source, out in pieces:
            copies.append(pltpu.make_async_copy(stage.at[source], out, sems.at[len(copies)]))
            copies[-1].start()
    for copy in copies:
        copy.wait()


def merge(hint, blocks, sectors, z_first):
    block = blocks[0].shape[2:]
    shapes = [(8, 32), (16,), (16,)] if z_first else [(sectors,)]
    full = pl.BlockSpec(blocks[-1].shape, lambda i: (0, 0, 0, 0, 0))
    own = pl.BlockSpec((1, *blocks[-1].shape[1:]), lambda i: (0, 0, 0, 0, 0))
    return pl.pallas_call(
        functools.partial(merge_kernel, z_first),
        grid=(1,),
        in_specs=[HBM] + [own] * (len(blocks) - 1) + [full],
        out_specs=[HBM] * len(shapes),
        out_shape=[jax.ShapeDtypeStruct((*shape, *block), BF16) for shape in shapes],
        scratch_shapes=[
            pltpu.VMEM((GROUPS * 8, 128), jnp.int32),
            pltpu.SMEM((GROUPS * 8, 128), jnp.int32),
            pltpu.VMEM((sectors, *block), F32),
            pltpu.VMEM((sectors, *block), BF16),
            pltpu.SemaphoreType.DMA,
            pltpu.SemaphoreType.DMA((STEPS + 1,)),
        ],
        cost_estimate=pl.CostEstimate(flops=2**22, bytes_accessed=2**23, transcendentals=0),
        compiler_params=params(56),
    )(hint, *blocks)


def join_kernel(first, up_base, down_base, up, down, up_out, down_out):
    half = up.shape[0]
    if first:
        up_out[:half] = (up_base[0, :half].astype(F32) + up[...].astype(F32)).astype(BF16)
        up_out[half:] = up_base[0, half:]
        down_out[:half] = down_base[0, :half]
        down_out[half:] = (down_base[0, half:].astype(F32) + down[...].astype(F32)).astype(BF16)
    else:
        up_out[...] = (up_base[0].astype(F32) + up[...].astype(F32)).astype(BF16)
        down_out[...] = (down_base[0].astype(F32) + down[...].astype(F32)).astype(BF16)


def join(dense, near, up, down):
    shape = dense.shape[1:]
    first = up.shape[0] != shape[0]

    def pick(n):
        return pl.BlockSpec((1, *shape), lambda i: (n, 0, 0, 0, 0))

    return pl.pallas_call(
        functools.partial(join_kernel, first),
        grid=(1,),
        in_specs=[pick(near), pick(8 - near), VMEM, VMEM],
        out_specs=[VMEM] * 2,
        out_shape=[jax.ShapeDtypeStruct(shape, BF16)] * 2,
        cost_estimate=pl.CostEstimate(flops=2**20, bytes_accessed=2**21, transcendentals=0),
        compiler_params=params(56),
    )(dense, dense, up, down)


def settle_kernel(own, up, down, *parts):
    here = parts[0].shape[0]
    y = lax.axis_index("y")
    for k in range(RING):
        rows = pl.ds(pl.multiple_of((y + k) % RING * here, here), here)
        total = own[0, rows].astype(F32) + up[rows].astype(F32) + down[rows].astype(F32)
        parts[k][...] = total.astype(BF16)


def settle(dense, up, down):
    count, *rest = dense.shape[1:]
    return pl.pallas_call(
        settle_kernel,
        grid=(1,),
        in_specs=[pl.BlockSpec((1, count, *rest), lambda i: (0, 0, 0, 0, 0)), VMEM, VMEM],
        out_specs=[VMEM] * RING,
        out_shape=[jax.ShapeDtypeStruct((count // RING, *rest), BF16)] * RING,
        cost_estimate=pl.CostEstimate(flops=2**20, bytes_accessed=2**21, transcendentals=0),
        compiler_params=params(56),
    )(dense, up, down)


def reduce_kernel(blocks, out):
    out[...] = sum(blocks[x].astype(F32) for x in range(RING)).astype(BF16)


def reduce(blocks):
    _, count, *rest = blocks.shape
    steps = 4
    return pl.pallas_call(
        reduce_kernel,
        grid=(steps,),
        in_specs=[pl.BlockSpec((RING, count // steps, *rest), lambda i: (0, i, 0, 0, 0))],
        out_specs=pl.BlockSpec((count // steps, *rest), lambda i: (i, 0, 0, 0)),
        out_shape=jax.ShapeDtypeStruct((count, *rest), BF16),
        cost_estimate=pl.CostEstimate(flops=2**22, bytes_accessed=2**22, transcendentals=0),
        compiler_params=params(56),
    )(blocks)


def gate(x, *waits):
    return pl.pallas_call(
        lambda *refs: None,
        in_specs=[HBM] * (1 + len(waits)),
        out_specs=HBM,
        out_shape=jax.ShapeDtypeStruct(x.shape, x.dtype),
        input_output_aliases={0: 0},
        compiler_params=params(16),
    )(x, *waits)


def finish_kernel(scale, first, second, local, trial_rows, out, gram):
    size = out.shape[-1]
    found = [[jnp.zeros((SUB, size), F32) for _ in range(2)] for _ in range(2)]
    for half in range(2):
        rows = slice(half * SUB, (half + 1) * SUB)
        for b in range(2):
            if half == 0:
                total = first[:, b].astype(F32)
            else:
                total = sum(second[z, :, b].astype(F32) for z in range(second.shape[0]))
            total = total + local[b, :, rows]
            out[b, :, rows] = total.astype(BF16)
            for a in range(2):
                found[a][b] += jnp.sum(trial_rows[a, :, rows].astype(F32) * total, axis=0)
    for a in range(2):
        for b in range(2):
            gram[a, b] = jnp.sum(found[a][b]) * scale


def finish(scale, *args):
    local = args[2]
    return pl.pallas_call(
        functools.partial(finish_kernel, scale),
        in_specs=[VMEM] * 4,
        out_specs=[VMEM, SMEM],
        out_shape=[
            jax.ShapeDtypeStruct(local.shape, BF16),
            jax.ShapeDtypeStruct((2, 2), F32),
        ],
        cost_estimate=pl.CostEstimate(flops=2**21, bytes_accessed=2**21, transcendentals=0),
        compiler_params=params(24),
    )(*args)


def to_all(x, axes):
    return lax.all_to_all(x, axes, 0, 0, tiled=True)


def spread(x, axes):
    return to_all(jnp.broadcast_to(x[None], (lax.axis_size(axes), *x.shape)), axes)


def shift(x, axis, k):
    n = lax.axis_size(axis)
    return lax.ppermute(x, axis, [(i, (i + k) % n) for i in range(n)])


def swap(x):
    return lax.ppermute(x, "core", [(0, 1), (1, 0)])


def turn(x, k):
    pairs = [
        (a * RING + b, (b + k) % RING * RING + a) for a in range(RING) for b in range(RING)
    ]
    return lax.ppermute(x, ("x", "y"), pairs)


def add(*arrays):
    return sum(x.astype(F32) for x in arrays).astype(BF16)


def body(trial, left_env, right_env, left_block_ham, right_block_ham, target):
    op = ("y", "core")
    nz, nx = lax.axis_size("z"), lax.axis_size("x")
    terms, here, size, _ = left_env.shape
    sectors = nz * nx * here
    rows = size // lax.axis_size(op)
    first_row = lax.axis_index(op) * rows
    trial_rows = lax.dynamic_slice_in_dim(trial, first_row, rows, 2)
    local = jnp.einsum("sij,vsjk->vsik", left_block_ham, trial, preferred_element_type=F32)
    local = local + jnp.einsum(
        "vsij,sjk->vsik", trial_rows, right_block_ham, preferred_element_type=F32
    )

    pieces, *strips = contract(target, trial, left_env, right_env)
    pieces = to_all(pieces, op)
    strips = [strips[0]] + [shift(strips[k], "x", k) for k in range(1, RING)]
    others = pack(strips)

    (blocks,) = merge(others, [pieces], sectors, False)
    dense, up, down = merge(blocks, [*strips, swap(others)], sectors, True)
    blocks = to_all(blocks.reshape(nx, nz * here, 2, SUB, size), "x")
    for near in (3, 2, 1):
        up, down = join(dense, near, shift(up, "z", 1), shift(down, "z", -1))
    up, down = shift(up, "z", 1), shift(down, "z", -1)
    halves = gate(reduce(blocks), up, down)
    second = to_all(halves.reshape(nz, here, 2, SUB, size), "z")
    parts = settle(dense, up, down)

    first = add(*(turn(parts[k], k) for k in range(RING)))

    scale = 1.0 / (sectors * size * size)
    hpsi, gram = finish(scale, first, second, local, trial_rows)
    gram = jnp.sum(spread(gram, ("z", "x")), axis=0)
    gram = jnp.sum(spread(gram, op), axis=0)
    return hpsi, gram


def solution(mesh):
    sizes = {"z": 8, "x": 4, "y": 4, "core": 2}
    fine = Mesh(mesh.devices.reshape(tuple(sizes.values())), tuple(sizes))
    sec, op = ("z", "x"), ("y", "core")
    return jax.shard_map(
        body,
        mesh=fine,
        in_specs=(
            P(None, sec, None, None),
            P(op, sec, None, None),
            P(op, sec, None, None),
            P(sec, op, None),
            P(sec, None, None),
            P(op, sec),
        ),
        out_specs=(P(None, sec, op, None), P()),
        check_vma=False,
    )
```

time: 227 us -> 215 us (0.947)
  blocking collectives: 77.2 us -> 25.5 us
  waiting for transfers between devices: 60.3 us -> 90.4 us
  starting transfers between devices: 22.7 us -> 42.5 us
  between operations: 14.1 us -> 0.84 us
  Pallas kernels: 37.5 us -> 44.1 us
  other arithmetic: 3.7 us -> 0.7 us
    ppermute x6 -> x11, waiting for transfers between devices: 16.9 us -> 78.3 us  [shift(): return lax.ppermute(x, axis, [(i, (i + k) % n) for i in range(n)])]
    all_to_all x3 -> x2, blocking collectives: 77.2 us -> 25.5 us  [to_all(): return lax.all_to_all(x, axes, 0, 0, tiled=True)]
    all_to_all x2 -> x3, waiting for transfers between devices: 39.1 us -> 8.19 us  [to_all(): return lax.all_to_all(x, axes, 0, 0, tiled=True)]
    ppermute x6 -> x11, starting transfers between devices: 6.87 us -> 16 us  [shift(): return lax.ppermute(x, axis, [(i, (i + k) % n) for i in range(n)])]
    ppermute x1 -> x4, starting transfers between devices: 1.55 us -> 8.67 us  [turn(): return lax.ppermute(x, ('x', 'y'), pairs)]
    pallas_call x5 -> x9, Pallas kernels: 33.3 us -> 38.8 us  [the longest x2 18 us: merge(): pl.pallas_call(functools.partial(merge_kernel, z_first), grid=(1,), in_sp...]
    ppermute x1, waiting for transfers between devices: 4.28 us -> 0.01 us  [swap(): return lax.ppermute(x, 'core', [(0, 1), (1, 0)])]
    ppermute x1 -> x4, waiting for transfers between devices: 0.01 us -> 3.99 us  [turn(): return lax.ppermute(x, ('x', 'y'), pairs)]
  transfers between devices with their start and end apart: 11 -> 19, of which waited for: 8 -> 9; matrix products, arithmetic and copies ran while one was open for 3% -> 1% of each run, Pallas kernels for 10% -> 15%
where the time goes in v4:
time: 215 us
  waiting for transfers between devices  90.4 us (42%)
  Pallas kernels  44.1 us (21%)
  starting transfers between devices  42.5 us (20%)
  blocking collectives  25.5 us (12%)
  local copies, waits for them, and re-layouts  9.73 us (5%)
    ppermute x11, waiting for transfers between devices, shift(): return lax.ppermute(x, axis, [(i, (i + k) % n) for i in range(n)])  78.3 us
    all_to_all x2, blocking collectives, to_all(): return lax.all_to_all(x, axes, 0, 0, tiled=True)  25.5 us
    pallas_call x2, Pallas kernels, merge(): pl.pallas_call(functools.partial(merge_kernel, z_first), grid=(1,), in_sp...  18 us
    all_to_all x3, starting transfers between devices, to_all(): return lax.all_to_all(x, axes, 0, 0, tiled=True)  16.7 us
    ppermute x11, starting transfers between devices, shift(): return lax.ppermute(x, axis, [(i, (i + k) % n) for i in range(n)])  16 us
    pallas_call x1, Pallas kernels, contract(): pl.pallas_call(contract_kernel, grid=(terms,), in_specs=[VMEM, pl.BlockSp...  10.5 us
    unnamed x40, local copies, waits for them, and re-layouts  8.74 us
    ppermute x4, starting transfers between devices, turn(): return lax.ppermute(x, ('x', 'y'), pairs)  8.67 us
  transfers between devices with their start and end apart: 19, of which 9 were waited for; matrix products, arithmetic and copies ran while one was open for 1% of the time, Pallas kernels for 15%

profile of v4, /device:TPU:1, one launch (start us, length us, event | category | flops | bytes accessed | tf_op | source)
XLA Modules:
  0.0 214.5 jit_solution(12675179958524383649)
XLA Ops:
  0.6 10.5 %shard_map.77 = (bf16[8,33,2,16,256]{4,3,2,1,0:T(8,128)(2,1)}, bf16[2,33,2,16,256]{4,3,2,1,0:T(8,128)(2,1)}, bf16[2,33,2,16,256]{4,3,2,1,0:T(8,128)(2,1)}, bf16[...) custom-call(s32[4,8]{1,0:T(4,128)} %target_ref.1, bf16[4,8,256,256]{3,2,1,0:T(8,128)(2,1)} %left_ref.1, ...), custom_call_target="tpu_custom_call" | custom-call | flops 4294967296 | bytes 16777216 | tf_op jit(solution)/shard_map/pallas_call | solution.py:95
  11.2 7.8 %all-to-all-start = ((bf16[8,33,2,16,256]{4,3,2,1,0:T(8,128)(2,1)}), bf16[8,33,2,16,256]{4,3,2,1,0:T(8,128)(2,1)}, u32[]{:S(2)}, u32[]{:S(2)}) async-start(bf16[8,33,2,16,256]{4,3,2,1,0:T(8,128)(2,1)} %get-tuple-element.26), calls=%async_computation | async-start | bytes 8650752 | tf_op jit(solution)/shard_map/all_to_all | solution.py:332
  22.1 46.8 %collective-permute-done.refs_1_ = bf16[2,33,2,16,256]{4,3,2,1,0:T(8,128)(2,1)S(1)} collective-permute-done((bf16[2,33,2,16,256]{4,3,2,1,0:T(8,128)(2,1)}, bf16[2,33,2,16,256]{4,3,2,1,0:T(8,128)(2,1)S(1)}, u32[]{:S(2)}, u32[]{:S(2)}) %collective-permute-start) | collective-permute-done | bytes 1081376 | tf_op jit(solution)/shard_map/ppermute | solution.py:341
  72.7 9.3 %shard_map.79.hint_ref = bf16[256,2,16,256]{3,2,1,0:T(8,128)(2,1)} custom-call(bf16[4,33,2,16,256]{4,3,2,1,0:T(8,128)(2,1)} %copy-done.3, bf16[8,33,2,16,256]{4,3,2,1,0:T(8,128)(2,1)} %all-to-all-done.refs_0_), custom_call_target="tpu_custom_call" | custom-call | flops 4194304 | bytes 8388608 | tf_op jit(solution)/shard_map/pallas_call | solution.py:197
  82.1 4.8 %all-to-all-start.1 = ((bf16[4,64,2,16,256]{4,3,2,1,0:T(8,128)(2,1)}), bf16[4,64,2,16,256]{4,3,2,1,0:T(8,128)(2,1)}, u32[]{:S(2)}, u32[]{:S(2)}) async-start(bf16[4,64,2,16,256]{4,3,2,1,0:T(8,128)(2,1)} %bitcast.17), calls=%async_computation.1 | async-start | bytes 8388608 | tf_op jit(solution)/shard_map/all_to_all | solution.py:332
  86.9 8.7 %shard_map.80 = (bf16[8,32,2,16,256]{4,3,2,1,0:T(8,128)(2,1)}, bf16[16,2,16,256]{3,2,1,0:T(8,128)(2,1)}, bf16[16,2,16,256]{3,2,1,0:T(8,128)(2,1)}) custom-call(bf16[256,2,16,256]{3,2,1,0:T(8,128)(2,1)} %shard_map.79.hint_ref, bf16[2,33,2,16,256]{4,3,2,1,0:T(8,128)(2,1)} %get-tuple-element.22.refs_0_, bf16[2,33,2,16,256]{4,3,2,1,0:T(8,128)(2,1)} %copy-done.5, ...), custom_call_target="tpu_custom_call" | custom-call | flops 4194304 | bytes 8388608 | tf_op jit(solution)/shard_map/pallas_call | solution.py:197
  96.4 4.0 %collective-permute-start.5 = (bf16[16,2,16,256]{3,2,1,0:T(8,128)(2,1)}, bf16[16,2,16,256]{3,2,1,0:T(8,128)(2,1)S(1)}, u32[]{:S(2)}, u32[]{:S(2)}) collective-permute-start(bf16[16,2,16,256]{3,2,1,0:T(8,128)(2,1)} %get-tuple-element.29), channel_id=1, source_target_pairs={{0,224},{32,0},{64,32},{96,64},{128,96},{160,128},{192,160},{224,1... | collective-permute-start | bytes 786440 | tf_op jit(solution)/shard_map/ppermute | solution.py:341
  100.4 5.9 %collective-permute-done.4.up = bf16[16,2,16,256]{3,2,1,0:T(8,128)(2,1)S(1)} collective-permute-done((bf16[16,2,16,256]{3,2,1,0:T(8,128)(2,1)}, bf16[16,2,16,256]{3,2,1,0:T(8,128)(2,1)S(1)}, u32[]{:S(2)}, u32[]{:S(2)}) %collective-permute-start.4) | collective-permute-done | bytes 262176 | tf_op jit(solution)/shard_map/ppermute | solution.py:341
  109.5 2.7 %collective-permute-start.7 = (bf16[32,2,16,256]{3,2,1,0:T(8,128)(2,1)}, bf16[32,2,16,256]{3,2,1,0:T(8,128)(2,1)S(1)}, u32[]{:S(2)}, u32[]{:S(2)}) collective-permute-start(bf16[32,2,16,256]{3,2,1,0:T(8,128)(2,1)} %get-tuple-element.31), channel_id=1, source_target_pairs={{0,224},{32,0},{64,32},{96,64},{128,96},{160,128},{192,160},{224,1... | collective-permute-start | bytes 1572872 | tf_op jit(solution)/shard_map/ppermute | solution.py:341
  112.2 10.8 %collective-permute-done.6.up = bf16[32,2,16,256]{3,2,1,0:T(8,128)(2,1)S(1)} collective-permute-done((bf16[32,2,16,256]{3,2,1,0:T(8,128)(2,1)}, bf16[32,2,16,256]{3,2,1,0:T(8,128)(2,1)S(1)}, u32[]{:S(2)}, u32[]{:S(2)}) %collective-permute-start.6) | collective-permute-done | bytes 524320 | tf_op jit(solution)/shard_map/ppermute | solution.py:341
  124.6 2.7 %shard_map.82 = (bf16[32,2,16,256]{3,2,1,0:T(8,128)(2,1)}, bf16[32,2,16,256]{3,2,1,0:T(8,128)(2,1)}) custom-call(bf16[8,32,2,16,256]{4,3,2,1,0:T(8,128)(2,1)} %get-tuple-element.27.up_base.down_base.own, bf16[8,32,2,16,256]{4,3,2,1,0:T(8,128)(2,1)} %get-tuple-element.27.up_base.down_base.own, bf16[32,2,16,256]{3,2,1,0:T(8,128)(2,1)} %copy-done.11, ...), custom_call_target="tpu_custom_call" | custom-call | flops 1048576 | bytes 2097152 | tf_op jit(solution)/shard_map/pallas_call | solution.py:235
  127.3 2.6 %collective-permute-start.9 = (bf16[32,2,16,256]{3,2,1,0:T(8,128)(2,1)}, bf16[32,2,16,256]{3,2,1,0:T(8,128)(2,1)S(1)}, u32[]{:S(2)}, u32[]{:S(2)}) collective-permute-start(bf16[32,2,16,256]{3,2,1,0:T(8,128)(2,1)} %get-tuple-element.33), channel_id=1, source_target_pairs={{0,224},{32,0},{64,32},{96,64},{128,96},{160,128},{192,160},{224,1... | collective-permute-start | bytes 1572872 | tf_op jit(solution)/shard_map/ppermute | solution.py:341
  129.9 9.9 %collective-permute-done.8.up = bf16[32,2,16,256]{3,2,1,0:T(8,128)(2,1)S(1)} collective-permute-done((bf16[32,2,16,256]{3,2,1,0:T(8,128)(2,1)}, bf16[32,2,16,256]{3,2,1,0:T(8,128)(2,1)S(1)}, u32[]{:S(2)}, u32[]{:S(2)}) %collective-permute-start.8) | collective-permute-done | bytes 524320 | tf_op jit(solution)/shard_map/ppermute | solution.py:341
  141.4 2.6 %shard_map.83 = (bf16[32,2,16,256]{3,2,1,0:T(8,128)(2,1)}, bf16[32,2,16,256]{3,2,1,0:T(8,128)(2,1)}) custom-call(bf16[8,32,2,16,256]{4,3,2,1,0:T(8,128)(2,1)} %get-tuple-element.27.up_base.down_base.own, bf16[8,32,2,16,256]{4,3,2,1,0:T(8,128)(2,1)} %get-tuple-element.27.up_base.down_base.own, bf16[32,2,16,256]{3,2,1,0:T(8,128)(2,1)} %copy-done.12, ...), custom_call_target="tpu_custom_call" | custom-call | flops 1048576 | bytes 2097152 | tf_op jit(solution)/shard_map/pallas_call | solution.py:235
  144.0 2.7 %collective-permute-start.11 = (bf16[32,2,16,256]{3,2,1,0:T(8,128)(2,1)}, bf16[32,2,16,256]{3,2,1,0:T(8,128)(2,1)S(1)}, u32[]{:S(2)}, u32[]{:S(2)}) collective-permute-start(bf16[32,2,16,256]{3,2,1,0:T(8,128)(2,1)} %get-tuple-element.35), channel_id=1, source_target_pairs={{0,224},{32,0},{64,32},{96,64},{128,96},{160,128},{192,160},{224,1... | collective-permute-start | bytes 1572872 | tf_op jit(solution)/shard_map/ppermute | solution.py:341
  146.7 4.2 %shard_map.85.refs_0_ = bf16[64,2,16,256]{3,2,1,0:T(8,128)(2,1)} custom-call(bf16[4,64,2,16,256]{4,3,2,1,0:T(8,128)(2,1)} %all-to-all-done.1.blocks), custom_call_target="tpu_custom_call" | custom-call | flops 4194304 | bytes 4194304 | tf_op jit(solution)/shard_map/pallas_call | solution.py:275
  150.9 4.7 %collective-permute-done.10.up.refs_1_ = bf16[32,2,16,256]{3,2,1,0:T(8,128)(2,1)S(1)} collective-permute-done((bf16[32,2,16,256]{3,2,1,0:T(8,128)(2,1)}, bf16[32,2,16,256]{3,2,1,0:T(8,128)(2,1)S(1)}, u32[]{:S(2)}, u32[]{:S(2)}) %collective-permute-start.10) | collective-permute-done | bytes 524320 | tf_op jit(solution)/shard_map/ppermute | solution.py:341
  158.2 4.0 %all-to-all-start.2 = ((bf16[8,8,2,16,256]{4,3,2,1,0:T(8,128)(2,1)}), bf16[8,8,2,16,256]{4,3,2,1,0:T(8,128)(2,1)S(1)}, u32[]{:S(2)}, u32[]{:S(2)}) async-start(bf16[8,8,2,16,256]{4,3,2,1,0:T(8,128)(2,1)} %bitcast.16), calls=%async_computation.2 | async-start | bytes 2097152 | tf_op jit(solution)/shard_map/all_to_all | solution.py:332
  163.6 2.4 %shard_map.84 = (bf16[8,2,16,256]{3,2,1,0:T(8,128)(2,1)}, bf16[8,2,16,256]{3,2,1,0:T(8,128)(2,1)}, bf16[8,2,16,256]{3,2,1,0:T(8,128)(2,1)}, bf16[8,2,16,256]{3,2,1,0:T(8,128)(2,1)}) custom-call(bf16[8,32,2,16,256]{4,3,2,1,0:T(8,128)(2,1)} %get-tuple-element.27.up_base.down_base.own, bf16[32,2,16,256]{3,2,1,0:T(8,128)(2,1)} %copy-done.8, ...), custom_call_target="tpu_custom_call" | custom-call | flops 1048576 | bytes 2097152 | tf_op jit(solution)/shard_map/pallas_call | solution.py:257
  169.7 3.1 %collective-permute-start.14 = (bf16[8,2,16,256]{3,2,1,0:T(8,128)(2,1)}, bf16[8,2,16,256]{3,2,1,0:T(8,128)(2,1)S(1)}, u32[]{:S(2)}, u32[]{:S(2)}) collective-permute-start(bf16[8,2,16,256]{3,2,1,0:T(8,128)(2,1)} %get-tuple-element.38), channel_id=1, source_target_pairs={{0,16},{2,24},{4,0},{6,8},{8,18},{10,26},{12,2},{14,10},{16,20},{1... | collective-permute-start | bytes 393224 | tf_op jit(solution)/shard_map/ppermute | solution.py:352
  175.1 3.9 %collective-permute-done.14 = bf16[8,2,16,256]{3,2,1,0:T(8,128)(2,1)S(1)} collective-permute-done((bf16[8,2,16,256]{3,2,1,0:T(8,128)(2,1)}, bf16[8,2,16,256]{3,2,1,0:T(8,128)(2,1)S(1)}, u32[]{:S(2)}, u32[]{:S(2)}) %collective-permute-start.14) | collective-permute-done | bytes 131104 | tf_op jit(solution)/shard_map/ppermute | solution.py:352
  179.2 8.2 %all-to-all-done.2.second = bf16[8,8,2,16,256]{4,3,2,1,0:T(8,128)(2,1)S(1)} async-done(((bf16[8,8,2,16,256]{4,3,2,1,0:T(8,128)(2,1)}), bf16[8,8,2,16,256]{4,3,2,1,0:T(8,128)(2,1)S(1)}, u32[]{:S(2)}, u32[]{:S(2)}) %all-to-all-start.2) | async-done | bytes 1048608 | tf_op jit(solution)/shard_map/all_to_all | solution.py:332
  188.4 12.1 %all_to_all.25 = f32[32,2,2]{2,1,0:T(2,128)S(1)} all-to-all(f32[32,2,2]{2,1,0:T(2,128)S(1)} %broadcast_in_dim.4), channel_id=1, replica_groups=mesh['z'=8,'x'=4,'y'=4,'core'=2] {'z','x'}, dimensions={0} | all-to-all | bytes 1024 | tf_op jit(solution)/shard_map/all_to_all | solution.py:332
  200.5 13.4 %all_to_all.26 = f32[8,2,2]{2,1,0:T(2,128)S(1)} all-to-all(f32[8,2,2]{2,1,0:T(2,128)S(1)} %broadcast_in_dim.5), channel_id=1, replica_groups=mesh['z'=8,'x'=4,'y'=4,'core'=2] {'y','core'}, dimensions={0} | all-to-all | bytes 256 | tf_op jit(solution)/shard_map/all_to_all | solution.py:332
  (75 shorter events, 25.8 us)
Async XLA Ops:
  0.6 162.6 %copy-start = (bf16[8,256,256]{2,1,0:T(8,128)(2,1)S(1)}, bf16[8,256,256]{2,1,0:T(8,128)(2,1)}, u32[]{:S(2)}) copy-start(bf16[8,256,256]{2,1,0:T(8,128)(2,1)} %param.10) | copy-start | bytes 3145732
  11.1 7.8 %copy-start.19 = (bf16[2,33,2,16,256]{4,3,2,1,0:T(8,128)(2,1)S(1)}, bf16[2,33,2,16,256]{4,3,2,1,0:T(8,128)(2,1)}, u32[]{:S(2)}) copy-start(bf16[2,33,2,16,256]{4,3,2,1,0:T(8,128)(2,1)} %get-tuple-element.24) | copy-start | bytes 3244036
  11.1 9.8 %copy-start.18 = (bf16[2,33,2,16,256]{4,3,2,1,0:T(8,128)(2,1)S(1)}, bf16[2,33,2,16,256]{4,3,2,1,0:T(8,128)(2,1)}, u32[]{:S(2)}) copy-start(bf16[2,33,2,16,256]{4,3,2,1,0:T(8,128)(2,1)} %get-tuple-element.25) | copy-start | bytes 3244036
  11.2 61.5 %all-to-all-start = ((bf16[8,33,2,16,256]{4,3,2,1,0:T(8,128)(2,1)}), bf16[8,33,2,16,256]{4,3,2,1,0:T(8,128)(2,1)}, u32[]{:S(2)}, u32[]{:S(2)}) async-start(bf16[8,33,2,16,256]{4,3,2,1,0:T(8,128)(2,1)} %get-tuple-element.26), calls=%async_computation | async-start | bytes 8650752 | tf_op jit(solution)/shard_map/all_to_all | solution.py:332
  19.0 50.0 %collective-permute-start = (bf16[2,33,2,16,256]{4,3,2,1,0:T(8,128)(2,1)}, bf16[2,33,2,16,256]{4,3,2,1,0:T(8,128)(2,1)S(1)}, u32[]{:S(2)}, u32[]{:S(2)}) collective-permute-start(bf16[2,33,2,16,256]{4,3,2,1,0:T(8,128)(2,1)} %get-tuple-element.23), channel_id=1, source_target_pairs={{0,8},{8,16},{16,24},{24,0},{1,9},{9,17},{17,25},{25,1},{2,10},{10... | collective-permute-start | bytes 3244040 | tf_op jit(solution)/shard_map/ppermute | solution.py:341
  19.0 50.0 %collective-permute-start.1 = (bf16[2,33,2,16,256]{4,3,2,1,0:T(8,128)(2,1)S(1)}, bf16[2,33,2,16,256]{4,3,2,1,0:T(8,128)(2,1)S(1)}, u32[]{:S(2)}, u32[]{:S(2)}) collective-permute-start(bf16[2,33,2,16,256]{4,3,2,1,0:T(8,128)(2,1)S(1)} %copy-done.19), channel_id=1, source_target_pairs={{0,16},{8,24},{16,0},{24,8},{1,17},{9,25},{17,1},{25,9},{2,18},{10... | collective-permute-start | bytes 3244040 | tf_op jit(solution)/shard_map/ppermute | solution.py:341
  20.9 48.1 %collective-permute-start.2 = (bf16[2,33,2,16,256]{4,3,2,1,0:T(8,128)(2,1)S(1)}, bf16[2,33,2,16,256]{4,3,2,1,0:T(8,128)(2,1)S(1)}, u32[]{:S(2)}, u32[]{:S(2)}) collective-permute-start(bf16[2,33,2,16,256]{4,3,2,1,0:T(8,128)(2,1)S(1)} %copy-done.18), channel_id=1, source_target_pairs={{0,24},{8,0},{16,8},{24,16},{1,25},{9,1},{17,9},{25,17},{2,26},{10... | collective-permute-start | bytes 3244040 | tf_op jit(solution)/shard_map/ppermute | solution.py:341
  71.4 15.5 %collective-permute-start.3 = (bf16[4,33,2,16,256]{4,3,2,1,0:T(8,128)(2,1)S(1)}, bf16[4,33,2,16,256]{4,3,2,1,0:T(8,128)(2,1)}, u32[]{:S(2)}, u32[]{:S(2)}) collective-permute-start(bf16[4,33,2,16,256]{4,3,2,1,0:T(8,128)(2,1)S(1)} %shard_map.78.hint_ref), channel_id=1, source_target_pairs={{0,1},{1,0},{2,3},{3,2},{4,5},{5,4},{6,7},{7,6},{8,9},{9,8},{10,11... | collective-permute-start | bytes 6488072 | tf_op jit(solution)/shard_map/ppermute | solution.py:345
  82.1 64.6 %all-to-all-start.1 = ((bf16[4,64,2,16,256]{4,3,2,1,0:T(8,128)(2,1)}), bf16[4,64,2,16,256]{4,3,2,1,0:T(8,128)(2,1)}, u32[]{:S(2)}, u32[]{:S(2)}) async-start(bf16[4,64,2,16,256]{4,3,2,1,0:T(8,128)(2,1)} %bitcast.17), calls=%async_computation.1 | async-start | bytes 8388608 | tf_op jit(solution)/shard_map/all_to_all | solution.py:332
  95.6 10.7 %collective-permute-start.4 = (bf16[16,2,16,256]{3,2,1,0:T(8,128)(2,1)}, bf16[16,2,16,256]{3,2,1,0:T(8,128)(2,1)S(1)}, u32[]{:S(2)}, u32[]{:S(2)}) collective-permute-start(bf16[16,2,16,256]{3,2,1,0:T(8,128)(2,1)} %get-tuple-element.28), channel_id=1, source_target_pairs={{0,32},{32,64},{64,96},{96,128},{128,160},{160,192},{192,224},{224... | collective-permute-start | bytes 786440 | tf_op jit(solution)/shard_map/ppermute | solution.py:341
  96.4 9.9 %collective-permute-start.5 = (bf16[16,2,16,256]{3,2,1,0:T(8,128)(2,1)}, bf16[16,2,16,256]{3,2,1,0:T(8,128)(2,1)S(1)}, u32[]{:S(2)}, u32[]{:S(2)}) collective-permute-start(bf16[16,2,16,256]{3,2,1,0:T(8,128)(2,1)} %get-tuple-element.29), channel_id=1, source_target_pairs={{0,224},{32,0},{64,32},{96,64},{128,96},{160,128},{192,160},{224,1... | collective-permute-start | bytes 786440 | tf_op jit(solution)/shard_map/ppermute | solution.py:341
  109.5 13.5 %collective-permute-start.6 = (bf16[32,2,16,256]{3,2,1,0:T(8,128)(2,1)}, bf16[32,2,16,256]{3,2,1,0:T(8,128)(2,1)S(1)}, u32[]{:S(2)}, u32[]{:S(2)}) collective-permute-start(bf16[32,2,16,256]{3,2,1,0:T(8,128)(2,1)} %get-tuple-element.30), channel_id=1, source_target_pairs={{0,32},{32,64},{64,96},{96,128},{128,160},{160,192},{192,224},{224... | collective-permute-start | bytes 1572872 | tf_op jit(solution)/shard_map/ppermute | solution.py:341
  109.5 13.5 %collective-permute-start.7 = (bf16[32,2,16,256]{3,2,1,0:T(8,128)(2,1)}, bf16[32,2,16,256]{3,2,1,0:T(8,128)(2,1)S(1)}, u32[]{:S(2)}, u32[]{:S(2)}) collective-permute-start(bf16[32,2,16,256]{3,2,1,0:T(8,128)(2,1)} %get-tuple-element.31), channel_id=1, source_target_pairs={{0,224},{32,0},{64,32},{96,64},{128,96},{160,128},{192,160},{224,1... | collective-permute-start | bytes 1572872 | tf_op jit(solution)/shard_map/ppermute | solution.py:341
  127.3 12.5 %collective-permute-start.8 = (bf16[32,2,16,256]{3,2,1,0:T(8,128)(2,1)}, bf16[32,2,16,256]{3,2,1,0:T(8,128)(2,1)S(1)}, u32[]{:S(2)}, u32[]{:S(2)}) collective-permute-start(bf16[32,2,16,256]{3,2,1,0:T(8,128)(2,1)} %get-tuple-element.32), channel_id=1, source_target_pairs={{0,32},{32,64},{64,96},{96,128},{128,160},{160,192},{192,224},{224... | collective-permute-start | bytes 1572872 | tf_op jit(solution)/shard_map/ppermute | solution.py:341
  127.3 12.5 %collective-permute-start.9 = (bf16[32,2,16,256]{3,2,1,0:T(8,128)(2,1)}, bf16[32,2,16,256]{3,2,1,0:T(8,128)(2,1)S(1)}, u32[]{:S(2)}, u32[]{:S(2)}) collective-permute-start(bf16[32,2,16,256]{3,2,1,0:T(8,128)(2,1)} %get-tuple-element.33), channel_id=1, source_target_pairs={{0,224},{32,0},{64,32},{96,64},{128,96},{160,128},{192,160},{224,1... | collective-permute-start | bytes 1572872 | tf_op jit(solution)/shard_map/ppermute | solution.py:341
  144.0 11.6 %collective-permute-start.10 = (bf16[32,2,16,256]{3,2,1,0:T(8,128)(2,1)}, bf16[32,2,16,256]{3,2,1,0:T(8,128)(2,1)S(1)}, u32[]{:S(2)}, u32[]{:S(2)}) collective-permute-start(bf16[32,2,16,256]{3,2,1,0:T(8,128)(2,1)} %get-tuple-element.34), channel_id=1, source_target_pairs={{0,32},{32,64},{64,96},{96,128},{128,160},{160,192},{192,224},{224... | collective-permute-start | bytes 1572872 | tf_op jit(solution)/shard_map/ppermute | solution.py:341
  144.0 11.6 %collective-permute-start.11 = (bf16[32,2,16,256]{3,2,1,0:T(8,128)(2,1)}, bf16[32,2,16,256]{3,2,1,0:T(8,128)(2,1)S(1)}, u32[]{:S(2)}, u32[]{:S(2)}) collective-permute-start(bf16[32,2,16,256]{3,2,1,0:T(8,128)(2,1)} %get-tuple-element.35), channel_id=1, source_target_pairs={{0,224},{32,0},{64,32},{96,64},{128,96},{160,128},{192,160},{224,1... | collective-permute-start | bytes 1572872 | tf_op jit(solution)/shard_map/ppermute | solution.py:341
  158.2 29.1 %all-to-all-start.2 = ((bf16[8,8,2,16,256]{4,3,2,1,0:T(8,128)(2,1)}), bf16[8,8,2,16,256]{4,3,2,1,0:T(8,128)(2,1)S(1)}, u32[]{:S(2)}, u32[]{:S(2)}) async-start(bf16[8,8,2,16,256]{4,3,2,1,0:T(8,128)(2,1)} %bitcast.16), calls=%async_computation.2 | async-start | bytes 2097152 | tf_op jit(solution)/shard_map/all_to_all | solution.py:332
  163.5 11.1 %copy-start.10 = (bf16[2,8,256,256]{3,2,1,0:T(8,128)(2,1)S(1)}, bf16[2,8,256,256]{3,2,1,0:T(8,128)(2,1)}, u32[]{:S(2)}) copy-start(bf16[2,8,256,256]{3,2,1,0:T(8,128)(2,1)} %trial_ref.1) | copy-start | bytes 6291460
  163.6 11.1 %copy-start.17 = (bf16[8,32,256]{2,1,0:T(8,128)(2,1)S(1)}, bf16[8,32,256]{2,1,0:T(8,128)(2,1)}, u32[]{:S(2)}) copy-start(bf16[8,32,256]{2,1,0:T(8,128)(2,1)} %param.9) | copy-start | bytes 393220
  166.0 9.1 %collective-permute-start.12 = (bf16[8,2,16,256]{3,2,1,0:T(8,128)(2,1)}, bf16[8,2,16,256]{3,2,1,0:T(8,128)(2,1)S(1)}, u32[]{:S(2)}, u32[]{:S(2)}) collective-permute-start(bf16[8,2,16,256]{3,2,1,0:T(8,128)(2,1)} %get-tuple-element.36), channel_id=1, source_target_pairs={{0,0},{2,8},{4,16},{6,24},{8,2},{10,10},{12,18},{14,26},{16,4},{18... | collective-permute-start | bytes 393224 | tf_op jit(solution)/shard_map/ppermute | solution.py:352
  167.5 7.6 %collective-permute-start.13 = (bf16[8,2,16,256]{3,2,1,0:T(8,128)(2,1)}, bf16[8,2,16,256]{3,2,1,0:T(8,128)(2,1)S(1)}, u32[]{:S(2)}, u32[]{:S(2)}) collective-permute-start(bf16[8,2,16,256]{3,2,1,0:T(8,128)(2,1)} %get-tuple-element.37), channel_id=1, source_target_pairs={{0,8},{2,16},{4,24},{6,0},{8,10},{10,18},{12,26},{14,2},{16,12},{1... | collective-permute-start | bytes 393224 | tf_op jit(solution)/shard_map/ppermute | solution.py:352
  169.7 9.4 %collective-permute-start.14 = (bf16[8,2,16,256]{3,2,1,0:T(8,128)(2,1)}, bf16[8,2,16,256]{3,2,1,0:T(8,128)(2,1)S(1)}, u32[]{:S(2)}, u32[]{:S(2)}) collective-permute-start(bf16[8,2,16,256]{3,2,1,0:T(8,128)(2,1)} %get-tuple-element.38), channel_id=1, source_target_pairs={{0,16},{2,24},{4,0},{6,8},{8,18},{10,26},{12,2},{14,10},{16,20},{1... | collective-permute-start | bytes 393224 | tf_op jit(solution)/shard_map/ppermute | solution.py:352
  172.8 6.3 %collective-permute-start.15 = (bf16[8,2,16,256]{3,2,1,0:T(8,128)(2,1)}, bf16[8,2,16,256]{3,2,1,0:T(8,128)(2,1)S(1)}, u32[]{:S(2)}, u32[]{:S(2)}) collective-permute-start(bf16[8,2,16,256]{3,2,1,0:T(8,128)(2,1)} %get-tuple-element.39), channel_id=1, source_target_pairs={{0,24},{2,0},{4,8},{6,16},{8,26},{10,2},{12,10},{14,18},{16,28},{1... | collective-permute-start | bytes 393224 | tf_op jit(solution)/shard_map/ppermute | solution.py:352
  (15 other events, 21.3 us)

commit v5 on v4

--- a/solution.py
+++ b/solution.py
@@ -17,6 +17,8 @@
 VMEM = pl.BlockSpec(memory_space=pltpu.VMEM)
 SMEM = pl.BlockSpec(memory_space=pltpu.SMEM)
 HBM = pl.BlockSpec(memory_space=pltpu.HBM)
+ANY = pl.BlockSpec(memory_space=pl.ANY)
+HINT = jax.ShapeDtypeStruct((8, 128), F32)
 
 
 def params(mib):
@@ -24,7 +26,7 @@
 
 
 def contract_kernel(target_ref, left_ref, right_ref, trial_ref, *refs):
-    outs, (stage, slab, wide, sems, slab_sems) = refs[: 1 + RING], refs[1 + RING :]
+    outs, (stage, slab, wide, sems, slab_sems) = refs[: 2 + RING], refs[2 + RING :]
     step = pl.program_id(0)
     last = pl.num_programs(0) - 1
     here, size = left_ref.shape[1], left_ref.shape[3]
@@ -35,7 +37,8 @@
         for k in range(RING)
         for c in (core, 1 - core)
     ]
-    places = [(0, GROUPS)] + [(GROUPS + 2 * k, 2) for k in range(RING)]
+    places = [(0, GROUPS), (GROUPS, 1), (GROUPS + 1, 1)]
+    places += [(GROUPS + 2 * k, 2) for k in range(1, RING)]
 
     def copies(i):
         rows = pl.ds(i * here, here)
@@ -91,7 +94,7 @@
 
 def contract(target, trial, left_env, right_env):
     terms, here, size, _ = left_env.shape
-    shapes = [(n, terms * here + 1, 2, SUB, size) for n in (GROUPS, 2, 2, 2, 2)]
+    shapes = [(n, terms * here + 1, 2, SUB, size) for n in (GROUPS, 1, 1, 2, 2, 2)]
     return pl.pallas_call(
         contract_kernel,
         grid=(terms,),
@@ -120,7 +123,8 @@
 
 
 def pack_kernel(*refs):
-    ins, out, sems = refs[:RING], refs[-2], refs[-1]
+    ins, (out, hint, sems) = refs[: RING - 1], refs[RING - 1 :]
+    hint[...] = jnp.zeros_like(hint)
     copies = [
         pltpu.make_async_copy(ref.at[1], out.at[k], sems.at[k]) for k, ref in enumerate(ins)
     ]
@@ -134,10 +138,10 @@
     shape = blocks[0].shape[1:]
     return pl.pallas_call(
         pack_kernel,
-        in_specs=[HBM] * RING,
-        out_specs=HBM,
-        out_shape=jax.ShapeDtypeStruct((RING, *shape), BF16),
-        scratch_shapes=[pltpu.SemaphoreType.DMA((RING,))],
+        in_specs=[HBM] * (RING - 1),
+        out_specs=[HBM, VMEM],
+        out_shape=[jax.ShapeDtypeStruct((RING - 1, *shape), BF16), HINT],
+        scratch_shapes=[pltpu.SemaphoreType.DMA((RING - 1,))],
         cost_estimate=pl.CostEstimate(
             flops=0, bytes_accessed=4 * blocks[0].size, transcendentals=0
         ),
@@ -145,29 +149,29 @@
     )(*blocks)
 
 
-def merge_kernel(z_first, hint_ref, *refs):
+def merge_kernel(z_first, hints, *refs):
+    refs = refs[hints:]
     rows, table, sums, stage, table_sem, sems = refs[-6:]
-    ins, outs = (refs[: RING + 1], refs[RING + 1 : -6]) if z_first else (refs[:1], refs[1:-6])
+    ins, outs = (refs[: RING + 2], refs[RING + 2 : -6]) if z_first else (refs[:1], refs[1:-6])
     sources = [(ref, j) for ref in ins for j in range(ref.shape[0])]
     pairs = ins[0].shape[1] - 1
+    here = lax.axis_index("z")
     for i, (ref, j) in enumerate(sources):
-        line = ref[j, pairs, 0, :, :128].astype(F32)[:8]
-        rows[8 * i : 8 * i + 8, :] = line.astype(jnp.int32)
+        t = ref[j, pairs, 0, :, :128].astype(F32)[:8].astype(jnp.int32)
+        if z_first:
+            t = (((t >> 5) - here) & 7) * 32 + (t & 31)
+        else:
+            t = ((t >> 3) & 3) * 64 + (t >> 5) * 8 + (t & 7)
+        rows[8 * i : 8 * i + 8, :] = t
     copy = pltpu.make_async_copy(rows, table, table_sem)
     copy.start()
     sums[...] = jnp.zeros_like(sums)
     copy.wait()
-    here = lax.axis_index("z")
     for i, (ref, j) in enumerate(sources):
 
         def add_line(w, carry, i=i, ref=ref, j=j):
             for s in range(8):
-                t = table[8 * i + w, s]
-                if z_first:
-                    slot = (t // 32 - here) % 8 * 32 + t % 32
-                else:
-                    slot = t // 8 % RING * 64 + t // 32 * 8 + t % 8
-                sums[slot] += ref[j, w * 8 + s].astype(F32)
+                sums[table[8 * i + w, s]] += ref[j, w * 8 + s].astype(F32)
             return carry
 
         lax.fori_loop(0, pairs // 8, add_line, 0)
@@ -189,15 +193,15 @@
         copy.wait()
 
 
-def merge(hint, blocks, sectors, z_first):
+def merge(hints, blocks, sectors, z_first):
     block = blocks[0].shape[2:]
     shapes = [(8, 32), (16,), (16,)] if z_first else [(sectors,)]
     full = pl.BlockSpec(blocks[-1].shape, lambda i: (0, 0, 0, 0, 0))
     own = pl.BlockSpec((1, *blocks[-1].shape[1:]), lambda i: (0, 0, 0, 0, 0))
     return pl.pallas_call(
-        functools.partial(merge_kernel, z_first),
+        functools.partial(merge_kernel, z_first, len(hints)),
         grid=(1,),
-        in_specs=[HBM] + [own] * (len(blocks) - 1) + [full],
+        in_specs=[ANY] * len(hints) + [own] * (len(blocks) - 1) + [full],
         out_specs=[HBM] * len(shapes),
         out_shape=[jax.ShapeDtypeStruct((*shape, *block), BF16) for shape in shapes],
         scratch_shapes=[
@@ -210,7 +214,7 @@
         ],
         cost_estimate=pl.CostEstimate(flops=2**22, bytes_accessed=2**23, transcendentals=0),
         compiler_params=params(56),
-    )(hint, *blocks)
+    )(*hints, *blocks)
 
 
 def join_kernel(first, up_base, down_base, up, down, up_out, down_out):
@@ -239,7 +243,7 @@
         out_specs=[VMEM] * 2,
         out_shape=[jax.ShapeDtypeStruct(shape, BF16)] * 2,
         cost_estimate=pl.CostEstimate(flops=2**20, bytes_accessed=2**21, transcendentals=0),
-        compiler_params=params(56),
+        compiler_params=params(16),
     )(dense, dense, up, down)
 
 
@@ -261,12 +265,26 @@
         out_specs=[VMEM] * RING,
         out_shape=[jax.ShapeDtypeStruct((count // RING, *rest), BF16)] * RING,
         cost_estimate=pl.CostEstimate(flops=2**20, bytes_accessed=2**21, transcendentals=0),
-        compiler_params=params(56),
+        compiler_params=params(16),
     )(dense, up, down)
 
 
-def reduce_kernel(blocks, out):
-    out[...] = sum(blocks[x].astype(F32) for x in range(RING)).astype(BF16)
+def reduce_kernel(blocks, out, stage, sems):
+    step = pl.program_id(0)
+    some = blocks.shape[1]
+
+    def copy(i):
+        part = pl.ds(i * some, some)
+        return pltpu.make_async_copy(stage.at[part], out.at[part], sems.at[i])
+
+    total = sum(blocks[x].astype(F32) for x in range(RING))
+    stage[pl.ds(step * some, some)] = total.astype(BF16)
+    copy(step).start()
+
+    @pl.when(step == pl.num_programs(0) - 1)
+    def _():
+        for i in range(4):
+            copy(i).wait()
 
 
 def reduce(blocks):
@@ -276,21 +294,25 @@
         reduce_kernel,
         grid=(steps,),
         in_specs=[pl.BlockSpec((RING, count // steps, *rest), lambda i: (0, i, 0, 0, 0))],
-        out_specs=pl.BlockSpec((count // steps, *rest), lambda i: (i, 0, 0, 0)),
+        out_specs=HBM,
         out_shape=jax.ShapeDtypeStruct((count, *rest), BF16),
+        scratch_shapes=[
+            pltpu.VMEM((count, *rest), BF16),
+            pltpu.SemaphoreType.DMA((steps,)),
+        ],
         cost_estimate=pl.CostEstimate(flops=2**22, bytes_accessed=2**22, transcendentals=0),
-        compiler_params=params(56),
+        compiler_params=params(16),
     )(blocks)
 
 
 def gate(x, *waits):
     return pl.pallas_call(
         lambda *refs: None,
-        in_specs=[HBM] * (1 + len(waits)),
+        in_specs=[HBM] + [ANY] * len(waits),
         out_specs=HBM,
         out_shape=jax.ShapeDtypeStruct(x.shape, x.dtype),
         input_output_aliases={0: 0},
-        compiler_params=params(16),
+        compiler_params=params(62),
     )(x, *waits)
 
 
@@ -369,13 +391,14 @@
         "vsij,sjk->vsik", trial_rows, right_block_ham, preferred_element_type=F32
     )
 
-    pieces, *strips = contract(target, trial, left_env, right_env)
+    pieces, mine, other, *strips = contract(target, trial, left_env, right_env)
     pieces = to_all(pieces, op)
-    strips = [strips[0]] + [shift(strips[k], "x", k) for k in range(1, RING)]
-    others = pack(strips)
-
-    (blocks,) = merge(others, [pieces], sectors, False)
-    dense, up, down = merge(blocks, [*strips, swap(others)], sectors, True)
+    strips = [shift(strip, "x", k) for k, strip in enumerate(strips, 1)]
+    others, hint = pack(strips)
+    got = swap(other)
+
+    (blocks,) = merge([hint, got], [pieces], sectors, False)
+    dense, up, down = merge([blocks], [mine, got, *strips, swap(others)], sectors, True)
     blocks = to_all(blocks.reshape(nx, nz * here, 2, SUB, size), "x")
     for near in (3, 2, 1):
         up, down = join(dense, near, shift(up, "z", 1), shift(down, "z", -1))

time: 215 us -> 208 us (0.967)
  Pallas kernels: 44.1 us -> 32.4 us
  waiting for transfers between devices: 90.4 us -> 93.5 us
    pallas_call x3, Pallas kernels: 7.67 us -> 0.61 us  [join(): pl.pallas_call(functools.partial(join_kernel, first), grid=(1,), in_specs...]
    ppermute x11, waiting for transfers between devices: 78.3 us -> 82.5 us  [shift(): return lax.ppermute(x, axis, [(i, (i + k) % n) for i in range(n)])]
    pallas_call x4, Pallas kernels: 18.3 us -> 15.7 us  [the longest x2 14.5 us: merge(): pl.pallas_call(functools.partial(merge_kernel, z_first, len(hints)), grid...]
    unnamed x40 -> x24, local copies, waits for them, and re-layouts: 8.74 us -> 7.77 us
  transfers between devices with their start and end apart: 19 -> 20, of which waited for: 9 -> 11; matrix products, arithmetic and copies ran while one was open for 1% -> 1% of each run, Pallas kernels for 15% -> 10%
where the time goes in v5:
time: 208 us; the launch traced here: 207 us
  waiting for transfers between devices  93.5 us (45%)
  starting transfers between devices  44.4 us (21%)
  Pallas kernels  32.4 us (16%)
  blocking collectives  25.7 us (12%)
  local copies, waits for them, and re-layouts  8.75 us (4%)
    ppermute x11, waiting for transfers between devices, shift(): return lax.ppermute(x, axis, [(i, (i + k) % n) for i in range(n)])  82.5 us
    all_to_all x2, blocking collectives, to_all(): return lax.all_to_all(x, axes, 0, 0, tiled=True)  25.7 us
    all_to_all x3, starting transfers between devices, to_all(): return lax.all_to_all(x, axes, 0, 0, tiled=True)  17.3 us
    ppermute x11, starting transfers between devices, shift(): return lax.ppermute(x, axis, [(i, (i + k) % n) for i in range(n)])  15.6 us
    pallas_call x2, Pallas kernels, merge(): pl.pallas_call(functools.partial(merge_kernel, z_first, len(hints)), grid...  14.5 us
    pallas_call x1, Pallas kernels, contract(): pl.pallas_call(contract_kernel, grid=(terms,), in_specs=[VMEM, pl.BlockSp...  10.5 us
    ppermute x4, starting transfers between devices, turn(): return lax.ppermute(x, ('x', 'y'), pairs)  9.27 us
    unnamed x24, local copies, waits for them, and re-layouts  7.77 us
  transfers between devices with their start and end apart: 20, of which 11 were waited for; matrix products, arithmetic and copies ran while one was open for 1% of the time, Pallas kernels for 10%

profile of v5, /device:TPU:1, one launch (start us, length us, event | category | flops | bytes accessed | tf_op | source)
XLA Modules:
  0.0 207.0 jit_solution(14525064764548008381)
XLA Ops:
  0.6 10.5 %shard_map.77 = (bf16[8,33,2,16,256]{4,3,2,1,0:T(8,128)(2,1)}, bf16[1,33,2,16,256]{4,3,2,1,0:T(8,128)(2,1)}, bf16[1,33,2,16,256]{4,3,2,1,0:T(8,128)(2,1)}, bf16[...) custom-call(s32[4,8]{1,0:T(4,128)} %target_ref.1, ...), custom_call_target="tpu_custom_call" | custom-call | flops 4294967296 | bytes 16777216 | tf_op jit(solution)/shard_map/pallas_call | solution.py:98
  11.2 7.7 %all-to-all-start = ((bf16[8,33,2,16,256]{4,3,2,1,0:T(8,128)(2,1)}), bf16[8,33,2,16,256]{4,3,2,1,0:T(8,128)(2,1)}, u32[]{:S(2)}, u32[]{:S(2)}) async-start(bf16[8,33,2,16,256]{4,3,2,1,0:T(8,128)(2,1)} %get-tuple-element.30), calls=%async_computation | async-start | bytes 8650752 | tf_op jit(solution)/shard_map/all_to_all | solution.py:354
  23.0 23.3 %collective-permute-done.refs_0_.refs_3_ = bf16[2,33,2,16,256]{4,3,2,1,0:T(8,128)(2,1)S(1)} collective-permute-done((bf16[2,33,2,16,256]{4,3,2,1,0:T(8,128)(2,1)}, bf16[2,33,2,16,256]{4,3,2,1,0:T(8,128)(2,1)S(1)}, u32[]{:S(2)}, u32[]{:S(2)}) %collective-permute-start) | collective-permute-done | bytes 1081376 | tf_op jit(solution)/shard_map/ppermute | solution.py:363
  46.2 21.9 %collective-permute-done.1.refs_1_.refs_4_ = bf16[2,33,2,16,256]{4,3,2,1,0:T(8,128)(2,1)S(1)} collective-permute-done((bf16[2,33,2,16,256]{4,3,2,1,0:T(8,128)(2,1)}, bf16[2,33,2,16,256]{4,3,2,1,0:T(8,128)(2,1)S(1)}, u32[]{:S(2)}, u32[]{:S(2)}) %collective-permute-start.1) | collective-permute-done | bytes 1081376 | tf_op jit(solution)/shard_map/ppermute | solution.py:363
  73.2 7.2 %shard_map.79.refs_0_ = bf16[256,2,16,256]{3,2,1,0:T(8,128)(2,1)} custom-call(f32[8,128]{1,0:T(8,128)} %copy-done.9, bf16[1,33,2,16,256]{4,3,2,1,0:T(8,128)(2,1)} %collective-permute-done.3.refs_1_.refs_2_, bf16[8,33,2,16,256]{4,3,2,1,0:T(8,128)(2,1)} %all-to-all-done.refs_2_), custom_call_target="tpu_custom_call" | custom-call | flops 4194304 | bytes 8388608 | tf_op jit(solution)/shard_map/pallas_call | solution.py:201
  80.5 4.9 %all-to-all-start.1 = ((bf16[4,64,2,16,256]{4,3,2,1,0:T(8,128)(2,1)}), bf16[4,64,2,16,256]{4,3,2,1,0:T(8,128)(2,1)}, u32[]{:S(2)}, u32[]{:S(2)}) async-start(bf16[4,64,2,16,256]{4,3,2,1,0:T(8,128)(2,1)} %bitcast.17), calls=%async_computation.1 | async-start | bytes 8388608 | tf_op jit(solution)/shard_map/all_to_all | solution.py:354
  85.3 7.2 %shard_map.80 = (bf16[8,32,2,16,256]{4,3,2,1,0:T(8,128)(2,1)}, bf16[16,2,16,256]{3,2,1,0:T(8,128)(2,1)}, bf16[16,2,16,256]{3,2,1,0:T(8,128)(2,1)}) custom-call(bf16[256,2,16,256]{3,2,1,0:T(8,128)(2,1)} %shard_map.79.refs_0_, bf16[1,33,2,16,256]{4,3,2,1,0:T(8,128)(2,1)} %get-tuple-element.31.refs_1_, ...), custom_call_target="tpu_custom_call" | custom-call | flops 4194304 | bytes 8388608 | tf_op jit(solution)/shard_map/pallas_call | solution.py:201
  92.9 4.0 %collective-permute-start.6 = (bf16[16,2,16,256]{3,2,1,0:T(8,128)(2,1)}, bf16[16,2,16,256]{3,2,1,0:T(8,128)(2,1)S(1)}, u32[]{:S(2)}, u32[]{:S(2)}) collective-permute-start(bf16[16,2,16,256]{3,2,1,0:T(8,128)(2,1)} %get-tuple-element.35), channel_id=1, source_target_pairs={{0,224},{32,0},{64,32},{96,64},{128,96},{160,128},{192,160},{224,1... | collective-permute-start | bytes 786440 | tf_op jit(solution)/shard_map/ppermute | solution.py:363
  96.9 6.9 %collective-permute-done.5.up = bf16[16,2,16,256]{3,2,1,0:T(8,128)(2,1)S(1)} collective-permute-done((bf16[16,2,16,256]{3,2,1,0:T(8,128)(2,1)}, bf16[16,2,16,256]{3,2,1,0:T(8,128)(2,1)S(1)}, u32[]{:S(2)}, u32[]{:S(2)}) %collective-permute-start.5) | collective-permute-done | bytes 262176 | tf_op jit(solution)/shard_map/ppermute | solution.py:363
  106.3 2.7 %collective-permute-start.8 = (bf16[32,2,16,256]{3,2,1,0:T(8,128)(2,1)S(1)}, bf16[32,2,16,256]{3,2,1,0:T(8,128)(2,1)S(1)}, u32[]{:S(2)}, u32[]{:S(2)}) collective-permute-start(bf16[32,2,16,256]{3,2,1,0:T(8,128)(2,1)S(1)} %get-tuple-element.37), channel_id=1, source_target_pairs={{0,224},{32,0},{64,32},{96,64},{128,96},{160,128},{192,160},{224,1... | collective-permute-start | bytes 1572872 | tf_op jit(solution)/shard_map/ppermute | solution.py:363
  108.9 11.7 %collective-permute-done.7.up = bf16[32,2,16,256]{3,2,1,0:T(8,128)(2,1)S(1)} collective-permute-done((bf16[32,2,16,256]{3,2,1,0:T(8,128)(2,1)S(1)}, bf16[32,2,16,256]{3,2,1,0:T(8,128)(2,1)S(1)}, u32[]{:S(2)}, u32[]{:S(2)}) %collective-permute-start.7) | collective-permute-done | bytes 524320 | tf_op jit(solution)/shard_map/ppermute | solution.py:363
  120.8 2.6 %collective-permute-start.10 = (bf16[32,2,16,256]{3,2,1,0:T(8,128)(2,1)S(1)}, bf16[32,2,16,256]{3,2,1,0:T(8,128)(2,1)S(1)}, u32[]{:S(2)}, u32[]{:S(2)}) collective-permute-start(bf16[32,2,16,256]{3,2,1,0:T(8,128)(2,1)S(1)} %get-tuple-element.39), channel_id=1, source_target_pairs={{0,224},{32,0},{64,32},{96,64},{128,96},{160,128},{192,160},{224,1... | collective-permute-start | bytes 1572872 | tf_op jit(solution)/shard_map/ppermute | solution.py:363
  123.5 9.9 %collective-permute-done.10.down = bf16[32,2,16,256]{3,2,1,0:T(8,128)(2,1)S(1)} collective-permute-done((bf16[32,2,16,256]{3,2,1,0:T(8,128)(2,1)S(1)}, bf16[32,2,16,256]{3,2,1,0:T(8,128)(2,1)S(1)}, u32[]{:S(2)}, u32[]{:S(2)}) %collective-permute-start.10) | collective-permute-done | bytes 524320 | tf_op jit(solution)/shard_map/ppermute | solution.py:363
  133.4 2.9 %collective-permute-done.9.up = bf16[32,2,16,256]{3,2,1,0:T(8,128)(2,1)S(1)} collective-permute-done((bf16[32,2,16,256]{3,2,1,0:T(8,128)(2,1)S(1)}, bf16[32,2,16,256]{3,2,1,0:T(8,128)(2,1)S(1)}, u32[]{:S(2)}, u32[]{:S(2)}) %collective-permute-start.9) | collective-permute-done | bytes 524320 | tf_op jit(solution)/shard_map/ppermute | solution.py:363
  136.6 2.7 %collective-permute-start.12 = (bf16[32,2,16,256]{3,2,1,0:T(8,128)(2,1)S(1)}, bf16[32,2,16,256]{3,2,1,0:T(8,128)(2,1)}, u32[]{:S(2)}, u32[]{:S(2)}) collective-permute-start(bf16[32,2,16,256]{3,2,1,0:T(8,128)(2,1)S(1)} %get-tuple-element.41), channel_id=1, source_target_pairs={{0,224},{32,0},{64,32},{96,64},{128,96},{160,128},{192,160},{224,1... | collective-permute-start | bytes 1572872 | tf_op jit(solution)/shard_map/ppermute | solution.py:363
  139.3 3.2 %shard_map.85.refs_0_ = bf16[64,2,16,256]{3,2,1,0:T(8,128)(2,1)S(1)} custom-call(bf16[4,64,2,16,256]{4,3,2,1,0:T(8,128)(2,1)} %all-to-all-done.1.blocks), custom_call_target="tpu_custom_call" | custom-call | flops 4194304 | bytes 4194304 | tf_op jit(solution)/shard_map/pallas_call | solution.py:293
  143.5 5.0 %collective-permute-done.11.up.refs_1_ = bf16[32,2,16,256]{3,2,1,0:T(8,128)(2,1)S(1)} collective-permute-done((bf16[32,2,16,256]{3,2,1,0:T(8,128)(2,1)S(1)}, bf16[32,2,16,256]{3,2,1,0:T(8,128)(2,1)S(1)}, u32[]{:S(2)}, u32[]{:S(2)}) %collective-permute-start.11) | collective-permute-done | bytes 524320 | tf_op jit(solution)/shard_map/ppermute | solution.py:363
  149.3 4.7 %all-to-all-start.2 = ((bf16[8,8,2,16,256]{4,3,2,1,0:T(8,128)(2,1)}), bf16[8,8,2,16,256]{4,3,2,1,0:T(8,128)(2,1)S(1)}, u32[]{:S(2)}, u32[]{:S(2)}) async-start(bf16[8,8,2,16,256]{4,3,2,1,0:T(8,128)(2,1)} %bitcast.16), calls=%async_computation.2 | async-start | bytes 2097152 | tf_op jit(solution)/shard_map/all_to_all | solution.py:354
  159.5 3.9 %collective-permute-start.14 = (bf16[8,2,16,256]{3,2,1,0:T(8,128)(2,1)S(1)}, bf16[8,2,16,256]{3,2,1,0:T(8,128)(2,1)S(1)}, u32[]{:S(2)}, u32[]{:S(2)}) collective-permute-start(bf16[8,2,16,256]{3,2,1,0:T(8,128)(2,1)S(1)} %get-tuple-element.43), channel_id=1, source_target_pairs={{0,8},{2,16},{4,24},{6,0},{8,10},{10,18},{12,26},{14,2},{16,12},{1... | collective-permute-start | bytes 393224 | tf_op jit(solution)/shard_map/ppermute | solution.py:374
  163.4 3.1 %collective-permute-start.15 = (bf16[8,2,16,256]{3,2,1,0:T(8,128)(2,1)S(1)}, bf16[8,2,16,256]{3,2,1,0:T(8,128)(2,1)S(1)}, u32[]{:S(2)}, u32[]{:S(2)}) collective-permute-start(bf16[8,2,16,256]{3,2,1,0:T(8,128)(2,1)S(1)} %get-tuple-element.44), channel_id=1, source_target_pairs={{0,16},{2,24},{4,0},{6,8},{8,18},{10,26},{12,2},{14,10},{16,20},{1... | collective-permute-start | bytes 393224 | tf_op jit(solution)/shard_map/ppermute | solution.py:374
  168.6 3.2 %collective-permute-done.15 = bf16[8,2,16,256]{3,2,1,0:T(8,128)(2,1)S(1)} collective-permute-done((bf16[8,2,16,256]{3,2,1,0:T(8,128)(2,1)S(1)}, bf16[8,2,16,256]{3,2,1,0:T(8,128)(2,1)S(1)}, u32[]{:S(2)}, u32[]{:S(2)}) %collective-permute-start.15) | collective-permute-done | bytes 131104 | tf_op jit(solution)/shard_map/ppermute | solution.py:374
  172.7 6.9 %all-to-all-done.2.second = bf16[8,8,2,16,256]{4,3,2,1,0:T(8,128)(2,1)S(1)} async-done(((bf16[8,8,2,16,256]{4,3,2,1,0:T(8,128)(2,1)}), bf16[8,8,2,16,256]{4,3,2,1,0:T(8,128)(2,1)S(1)}, u32[]{:S(2)}, u32[]{:S(2)}) %all-to-all-start.2) | async-done | bytes 1048608 | tf_op jit(solution)/shard_map/all_to_all | solution.py:354
  180.7 11.6 %all_to_all.25 = f32[32,2,2]{2,1,0:T(2,128)S(1)} all-to-all(f32[32,2,2]{2,1,0:T(2,128)S(1)} %broadcast_in_dim.4), channel_id=1, replica_groups=mesh['z'=8,'x'=4,'y'=4,'core'=2] {'z','x'}, dimensions={0} | all-to-all | bytes 1024 | tf_op jit(solution)/shard_map/all_to_all | solution.py:354
  192.3 14.1 %all_to_all.26 = f32[8,2,2]{2,1,0:T(2,128)S(1)} all-to-all(f32[8,2,2]{2,1,0:T(2,128)S(1)} %broadcast_in_dim.5), channel_id=1, replica_groups=mesh['z'=8,'x'=4,'y'=4,'core'=2] {'y','core'}, dimensions={0} | all-to-all | bytes 256 | tf_op jit(solution)/shard_map/all_to_all | solution.py:354
  (61 shorter events, 24.4 us)
Async XLA Ops:
  0.6 154.3 %copy-start = (bf16[8,256,256]{2,1,0:T(8,128)(2,1)S(1)}, bf16[8,256,256]{2,1,0:T(8,128)(2,1)}, u32[]{:S(2)}) copy-start(bf16[8,256,256]{2,1,0:T(8,128)(2,1)} %param.10) | copy-start | bytes 3145732
  11.2 62.0 %all-to-all-start = ((bf16[8,33,2,16,256]{4,3,2,1,0:T(8,128)(2,1)}), bf16[8,33,2,16,256]{4,3,2,1,0:T(8,128)(2,1)}, u32[]{:S(2)}, u32[]{:S(2)}) async-start(bf16[8,33,2,16,256]{4,3,2,1,0:T(8,128)(2,1)} %get-tuple-element.30), calls=%async_computation | async-start | bytes 8650752 | tf_op jit(solution)/shard_map/all_to_all | solution.py:354
  18.9 27.4 %collective-permute-start = (bf16[2,33,2,16,256]{4,3,2,1,0:T(8,128)(2,1)}, bf16[2,33,2,16,256]{4,3,2,1,0:T(8,128)(2,1)S(1)}, u32[]{:S(2)}, u32[]{:S(2)}) collective-permute-start(bf16[2,33,2,16,256]{4,3,2,1,0:T(8,128)(2,1)} %get-tuple-element.25), channel_id=1, source_target_pairs={{0,8},{8,16},{16,24},{24,0},{1,9},{9,17},{17,25},{25,1},{2,10},{10... | collective-permute-start | bytes 3244040 | tf_op jit(solution)/shard_map/ppermute | solution.py:363
  18.9 49.3 %collective-permute-start.1 = (bf16[2,33,2,16,256]{4,3,2,1,0:T(8,128)(2,1)}, bf16[2,33,2,16,256]{4,3,2,1,0:T(8,128)(2,1)S(1)}, u32[]{:S(2)}, u32[]{:S(2)}) collective-permute-start(bf16[2,33,2,16,256]{4,3,2,1,0:T(8,128)(2,1)} %get-tuple-element.26), channel_id=1, source_target_pairs={{0,16},{8,24},{16,0},{24,8},{1,17},{9,25},{17,1},{25,9},{2,18},{10... | collective-permute-start | bytes 3244040 | tf_op jit(solution)/shard_map/ppermute | solution.py:363
  20.8 48.3 %collective-permute-start.2 = (bf16[2,33,2,16,256]{4,3,2,1,0:T(8,128)(2,1)}, bf16[2,33,2,16,256]{4,3,2,1,0:T(8,128)(2,1)S(1)}, u32[]{:S(2)}, u32[]{:S(2)}) collective-permute-start(bf16[2,33,2,16,256]{4,3,2,1,0:T(8,128)(2,1)} %get-tuple-element.27), channel_id=1, source_target_pairs={{0,24},{8,0},{16,8},{24,16},{1,25},{9,1},{17,9},{25,17},{2,26},{10... | collective-permute-start | bytes 3244040 | tf_op jit(solution)/shard_map/ppermute | solution.py:363
  22.0 51.2 %collective-permute-start.3 = (bf16[1,33,2,16,256]{4,3,2,1,0:T(8,128)(2,1)}, bf16[1,33,2,16,256]{4,3,2,1,0:T(8,128)(2,1)}, u32[]{:S(2)}, u32[]{:S(2)}) collective-permute-start(bf16[1,33,2,16,256]{4,3,2,1,0:T(8,128)(2,1)} %get-tuple-element.29), channel_id=1, source_target_pairs={{0,1},{1,0},{2,3},{3,2},{4,5},{5,4},{6,7},{7,6},{8,9},{9,8},{10,11... | collective-permute-start | bytes 1622024 | tf_op jit(solution)/shard_map/ppermute | solution.py:367
  46.2 34.2 %copy-start.4 = (bf16[2,33,2,16,256]{4,3,2,1,0:T(8,128)(2,1)}, bf16[2,33,2,16,256]{4,3,2,1,0:T(8,128)(2,1)S(1)}, u32[]{:S(2)}) copy-start(bf16[2,33,2,16,256]{4,3,2,1,0:T(8,128)(2,1)S(1)} %collective-permute-done.refs_0_.refs_3_) | copy-start | bytes 3244036
  68.2 12.3 %copy-start.5 = (bf16[2,33,2,16,256]{4,3,2,1,0:T(8,128)(2,1)}, bf16[2,33,2,16,256]{4,3,2,1,0:T(8,128)(2,1)S(1)}, u32[]{:S(2)}) copy-start(bf16[2,33,2,16,256]{4,3,2,1,0:T(8,128)(2,1)S(1)} %collective-permute-done.1.refs_1_.refs_4_) | copy-start | bytes 3244036
  71.9 13.4 %collective-permute-start.4 = (bf16[3,33,2,16,256]{4,3,2,1,0:T(8,128)(2,1)}, bf16[3,33,2,16,256]{4,3,2,1,0:T(8,128)(2,1)}, u32[]{:S(2)}, u32[]{:S(2)}) collective-permute-start(bf16[3,33,2,16,256]{4,3,2,1,0:T(8,128)(2,1)} %get-tuple-element.32), channel_id=1, source_target_pairs={{0,1},{1,0},{2,3},{3,2},{4,5},{5,4},{6,7},{7,6},{8,9},{9,8},{10,11... | collective-permute-start | bytes 4866056 | tf_op jit(solution)/shard_map/ppermute | solution.py:367
  80.5 58.8 %all-to-all-start.1 = ((bf16[4,64,2,16,256]{4,3,2,1,0:T(8,128)(2,1)}), bf16[4,64,2,16,256]{4,3,2,1,0:T(8,128)(2,1)}, u32[]{:S(2)}, u32[]{:S(2)}) async-start(bf16[4,64,2,16,256]{4,3,2,1,0:T(8,128)(2,1)} %bitcast.17), calls=%async_computation.1 | async-start | bytes 8388608 | tf_op jit(solution)/shard_map/all_to_all | solution.py:354
  92.6 11.3 %collective-permute-start.5 = (bf16[16,2,16,256]{3,2,1,0:T(8,128)(2,1)}, bf16[16,2,16,256]{3,2,1,0:T(8,128)(2,1)S(1)}, u32[]{:S(2)}, u32[]{:S(2)}) collective-permute-start(bf16[16,2,16,256]{3,2,1,0:T(8,128)(2,1)} %get-tuple-element.34), channel_id=1, source_target_pairs={{0,32},{32,64},{64,96},{96,128},{128,160},{160,192},{192,224},{224... | collective-permute-start | bytes 786440 | tf_op jit(solution)/shard_map/ppermute | solution.py:363
  92.9 10.9 %collective-permute-start.6 = (bf16[16,2,16,256]{3,2,1,0:T(8,128)(2,1)}, bf16[16,2,16,256]{3,2,1,0:T(8,128)(2,1)S(1)}, u32[]{:S(2)}, u32[]{:S(2)}) collective-permute-start(bf16[16,2,16,256]{3,2,1,0:T(8,128)(2,1)} %get-tuple-element.35), channel_id=1, source_target_pairs={{0,224},{32,0},{64,32},{96,64},{128,96},{160,128},{192,160},{224,1... | collective-permute-start | bytes 786440 | tf_op jit(solution)/shard_map/ppermute | solution.py:363
  106.2 14.4 %collective-permute-start.7 = (bf16[32,2,16,256]{3,2,1,0:T(8,128)(2,1)S(1)}, bf16[32,2,16,256]{3,2,1,0:T(8,128)(2,1)S(1)}, u32[]{:S(2)}, u32[]{:S(2)}) collective-permute-start(bf16[32,2,16,256]{3,2,1,0:T(8,128)(2,1)S(1)} %get-tuple-element.36), channel_id=1, source_target_pairs={{0,32},{32,64},{64,96},{96,128},{128,160},{160,192},{192,224},{224... | collective-permute-start | bytes 1572872 | tf_op jit(solution)/shard_map/ppermute | solution.py:363
  106.3 14.3 %collective-permute-start.8 = (bf16[32,2,16,256]{3,2,1,0:T(8,128)(2,1)S(1)}, bf16[32,2,16,256]{3,2,1,0:T(8,128)(2,1)S(1)}, u32[]{:S(2)}, u32[]{:S(2)}) collective-permute-start(bf16[32,2,16,256]{3,2,1,0:T(8,128)(2,1)S(1)} %get-tuple-element.37), channel_id=1, source_target_pairs={{0,224},{32,0},{64,32},{96,64},{128,96},{160,128},{192,160},{224,1... | collective-permute-start | bytes 1572872 | tf_op jit(solution)/shard_map/ppermute | solution.py:363
  120.8 12.6 %collective-permute-start.10 = (bf16[32,2,16,256]{3,2,1,0:T(8,128)(2,1)S(1)}, bf16[32,2,16,256]{3,2,1,0:T(8,128)(2,1)S(1)}, u32[]{:S(2)}, u32[]{:S(2)}) collective-permute-start(bf16[32,2,16,256]{3,2,1,0:T(8,128)(2,1)S(1)} %get-tuple-element.39), channel_id=1, source_target_pairs={{0,224},{32,0},{64,32},{96,64},{128,96},{160,128},{192,160},{224,1... | collective-permute-start | bytes 1572872 | tf_op jit(solution)/shard_map/ppermute | solution.py:363
  123.5 12.8 %collective-permute-start.9 = (bf16[32,2,16,256]{3,2,1,0:T(8,128)(2,1)S(1)}, bf16[32,2,16,256]{3,2,1,0:T(8,128)(2,1)S(1)}, u32[]{:S(2)}, u32[]{:S(2)}) collective-permute-start(bf16[32,2,16,256]{3,2,1,0:T(8,128)(2,1)S(1)} %get-tuple-element.38), channel_id=1, source_target_pairs={{0,32},{32,64},{64,96},{96,128},{128,160},{160,192},{192,224},{224... | collective-permute-start | bytes 1572872 | tf_op jit(solution)/shard_map/ppermute | solution.py:363
  136.5 12.0 %collective-permute-start.11 = (bf16[32,2,16,256]{3,2,1,0:T(8,128)(2,1)S(1)}, bf16[32,2,16,256]{3,2,1,0:T(8,128)(2,1)S(1)}, u32[]{:S(2)}, u32[]{:S(2)}) collective-permute-start(bf16[32,2,16,256]{3,2,1,0:T(8,128)(2,1)S(1)} %get-tuple-element.40), channel_id=1, source_target_pairs={{0,32},{32,64},{64,96},{96,128},{128,160},{160,192},{192,224},{224... | collective-permute-start | bytes 1572872 | tf_op jit(solution)/shard_map/ppermute | solution.py:363
  136.6 11.9 %collective-permute-start.12 = (bf16[32,2,16,256]{3,2,1,0:T(8,128)(2,1)S(1)}, bf16[32,2,16,256]{3,2,1,0:T(8,128)(2,1)}, u32[]{:S(2)}, u32[]{:S(2)}) collective-permute-start(bf16[32,2,16,256]{3,2,1,0:T(8,128)(2,1)S(1)} %get-tuple-element.41), channel_id=1, source_target_pairs={{0,224},{32,0},{64,32},{96,64},{128,96},{160,128},{192,160},{224,1... | collective-permute-start | bytes 1572872 | tf_op jit(solution)/shard_map/ppermute | solution.py:363
  149.3 30.4 %all-to-all-start.2 = ((bf16[8,8,2,16,256]{4,3,2,1,0:T(8,128)(2,1)}), bf16[8,8,2,16,256]{4,3,2,1,0:T(8,128)(2,1)S(1)}, u32[]{:S(2)}, u32[]{:S(2)}) async-start(bf16[8,8,2,16,256]{4,3,2,1,0:T(8,128)(2,1)} %bitcast.16), calls=%async_computation.2 | async-start | bytes 2097152 | tf_op jit(solution)/shard_map/all_to_all | solution.py:354
  157.5 10.7 %copy-start.11 = (bf16[8,32,256]{2,1,0:T(8,128)(2,1)S(1)}, bf16[8,32,256]{2,1,0:T(8,128)(2,1)}, u32[]{:S(2)}) copy-start(bf16[8,32,256]{2,1,0:T(8,128)(2,1)} %param.9) | copy-start | bytes 393220
  158.9 9.7 %collective-permute-start.13 = (bf16[8,2,16,256]{3,2,1,0:T(8,128)(2,1)S(1)}, bf16[8,2,16,256]{3,2,1,0:T(8,128)(2,1)S(1)}, u32[]{:S(2)}, u32[]{:S(2)}) collective-permute-start(bf16[8,2,16,256]{3,2,1,0:T(8,128)(2,1)S(1)} %get-tuple-element.42), channel_id=1, source_target_pairs={{0,0},{2,8},{4,16},{6,24},{8,2},{10,10},{12,18},{14,26},{16,4},{18... | collective-permute-start | bytes 393224 | tf_op jit(solution)/shard_map/ppermute | solution.py:374
  159.5 9.1 %collective-permute-start.14 = (bf16[8,2,16,256]{3,2,1,0:T(8,128)(2,1)S(1)}, bf16[8,2,16,256]{3,2,1,0:T(8,128)(2,1)S(1)}, u32[]{:S(2)}, u32[]{:S(2)}) collective-permute-start(bf16[8,2,16,256]{3,2,1,0:T(8,128)(2,1)S(1)} %get-tuple-element.43), channel_id=1, source_target_pairs={{0,8},{2,16},{4,24},{6,0},{8,10},{10,18},{12,26},{14,2},{16,12},{1... | collective-permute-start | bytes 393224 | tf_op jit(solution)/shard_map/ppermute | solution.py:374
  163.4 8.4 %collective-permute-start.15 = (bf16[8,2,16,256]{3,2,1,0:T(8,128)(2,1)S(1)}, bf16[8,2,16,256]{3,2,1,0:T(8,128)(2,1)S(1)}, u32[]{:S(2)}, u32[]{:S(2)}) collective-permute-start(bf16[8,2,16,256]{3,2,1,0:T(8,128)(2,1)S(1)} %get-tuple-element.44), channel_id=1, source_target_pairs={{0,16},{2,24},{4,0},{6,8},{8,18},{10,26},{12,2},{14,10},{16,20},{1... | collective-permute-start | bytes 393224 | tf_op jit(solution)/shard_map/ppermute | solution.py:374
  166.5 6.1 %collective-permute-start.16 = (bf16[8,2,16,256]{3,2,1,0:T(8,128)(2,1)S(1)}, bf16[8,2,16,256]{3,2,1,0:T(8,128)(2,1)S(1)}, u32[]{:S(2)}, u32[]{:S(2)}) collective-permute-start(bf16[8,2,16,256]{3,2,1,0:T(8,128)(2,1)S(1)} %get-tuple-element.45), channel_id=1, source_target_pairs={{0,24},{2,0},{4,8},{6,16},{8,26},{10,2},{12,10},{14,18},{16,28},{1... | collective-permute-start | bytes 393224 | tf_op jit(solution)/shard_map/ppermute | solution.py:374
  (8 other events, 24.5 us)

commit v6 on v5

--- a/solution.py
+++ b/solution.py
@@ -74,11 +74,9 @@
 
     for s in range(here):
         rows = jnp.concatenate([left_ref[0, s, pl.ds(a, SUB), :] for a in order], axis=0)
-        half = [
-            jnp.dot(rows, trial_ref[v, s], preferred_element_type=F32).astype(BF16)
-            for v in range(2)
-        ]
-        half = jnp.concatenate(half, axis=0)
+        both = jnp.concatenate([trial_ref[0, s], trial_ref[1, s]], axis=1)
+        half = jnp.dot(rows, both, preferred_element_type=F32).astype(BF16)
+        half = jnp.concatenate([half[:, :size], half[:, size:]], axis=0)
         piece = jnp.dot(half, right_ref[0, s], preferred_element_type=F32).astype(BF16)
         piece = piece.reshape(2, 2 * GROUPS, SUB, size)
         for v in range(2):
@@ -217,34 +215,29 @@
     )(*hints, *blocks)
 
 
-def join_kernel(first, up_base, down_base, up, down, up_out, down_out):
-    half = up.shape[0]
-    if first:
-        up_out[:half] = (up_base[0, :half].astype(F32) + up[...].astype(F32)).astype(BF16)
-        up_out[half:] = up_base[0, half:]
-        down_out[:half] = down_base[0, :half]
-        down_out[half:] = (down_base[0, half:].astype(F32) + down[...].astype(F32)).astype(BF16)
-    else:
-        up_out[...] = (up_base[0].astype(F32) + up[...].astype(F32)).astype(BF16)
-        down_out[...] = (down_base[0].astype(F32) + down[...].astype(F32)).astype(BF16)
-
-
-def join(dense, near, up, down):
+def join_kernel(side, base, extra, out):
+    half = extra.shape[0]
+    if side == 0:
+        out[...] = (base[0].astype(F32) + extra[...].astype(F32)).astype(BF16)
+        return
+    mixed = slice(0, half) if side == 1 else slice(half, None)
+    kept = slice(half, None) if side == 1 else slice(0, half)
+    out[mixed] = (base[0, mixed].astype(F32) + extra[...].astype(F32)).astype(BF16)
+    out[kept] = base[0, kept]
+
+
+def join(dense, n, extra):
     shape = dense.shape[1:]
-    first = up.shape[0] != shape[0]
-
-    def pick(n):
-        return pl.BlockSpec((1, *shape), lambda i: (n, 0, 0, 0, 0))
-
-    return pl.pallas_call(
-        functools.partial(join_kernel, first),
+    side = 0 if extra.shape[0] == shape[0] else 1 if n < 4 else 2
+    return pl.pallas_call(
+        functools.partial(join_kernel, side),
         grid=(1,),
-        in_specs=[pick(near), pick(8 - near), VMEM, VMEM],
-        out_specs=[VMEM] * 2,
-        out_shape=[jax.ShapeDtypeStruct(shape, BF16)] * 2,
+        in_specs=[pl.BlockSpec((1, *shape), lambda i: (n, 0, 0, 0, 0)), VMEM],
+        out_specs=VMEM,
+        out_shape=jax.ShapeDtypeStruct(shape, BF16),
         cost_estimate=pl.CostEstimate(flops=2**20, bytes_accessed=2**21, transcendentals=0),
         compiler_params=params(16),
-    )(dense, dense, up, down)
+    )(dense, extra)
 
 
 def settle_kernel(own, up, down, *parts):
@@ -401,7 +394,8 @@
     dense, up, down = merge([blocks], [mine, got, *strips, swap(others)], sectors, True)
     blocks = to_all(blocks.reshape(nx, nz * here, 2, SUB, size), "x")
     for near in (3, 2, 1):
-        up, down = join(dense, near, shift(up, "z", 1), shift(down, "z", -1))
+        up, down = shift(up, "z", 1), shift(down, "z", -1)
+        up, down = join(dense, near, up), join(dense, 8 - near, down)
     up, down = shift(up, "z", 1), shift(down, "z", -1)
     halves = gate(reduce(blocks), up, down)
     second = to_all(halves.reshape(nz, here, 2, SUB, size), "z")
@@ -411,8 +405,8 @@
 
     scale = 1.0 / (sectors * size * size)
     hpsi, gram = finish(scale, first, second, local, trial_rows)
+    gram = jnp.sum(spread(gram, ("y", "core")), axis=0)
     gram = jnp.sum(spread(gram, ("z", "x")), axis=0)
-    gram = jnp.sum(spread(gram, op), axis=0)
     return hpsi, gram
 
 

time: 208 us -> 205 us (0.986)
  blocking collectives: 25.7 us -> 23.6 us
    ppermute x11, starting transfers between devices: 15.6 us -> 18.5 us  [shift(): return lax.ppermute(x, axis, [(i, (i + k) % n) for i in range(n)])]
    ppermute x11, waiting for transfers between devices: 82.5 us -> 80.1 us  [shift(): return lax.ppermute(x, axis, [(i, (i + k) % n) for i in range(n)])]
where the time goes in v6:
time: 205 us
  waiting for transfers between devices  91.7 us (45%)
  starting transfers between devices  46.4 us (23%)
  Pallas kernels  32.4 us (16%)
  blocking collectives  23.6 us (12%)
  local copies, waits for them, and re-layouts  8 us (4%)
    ppermute x11, waiting for transfers between devices, shift(): return lax.ppermute(x, axis, [(i, (i + k) % n) for i in range(n)])  80.1 us
    all_to_all x2, blocking collectives, to_all(): return lax.all_to_all(x, axes, 0, 0, tiled=True)  23.6 us
    ppermute x11, starting transfers between devices, shift(): return lax.ppermute(x, axis, [(i, (i + k) % n) for i in range(n)])  18.5 us
    all_to_all x3, starting transfers between devices, to_all(): return lax.all_to_all(x, axes, 0, 0, tiled=True)  16.2 us
    pallas_call x2, Pallas kernels, merge(): pl.pallas_call(functools.partial(merge_kernel, z_first, len(hints)), grid...  14.5 us
    pallas_call x1, Pallas kernels, contract(): pl.pallas_call(contract_kernel, grid=(terms,), in_specs=[VMEM, pl.BlockSp...  10.5 us
    ppermute x4, starting transfers between devices, turn(): return lax.ppermute(x, ('x', 'y'), pairs)  9.38 us
    all_to_all x3, waiting for transfers between devices, to_all(): return lax.all_to_all(x, axes, 0, 0, tiled=True)  7.73 us
  transfers between devices with their start and end apart: 20, of which 11 were waited for; matrix products, arithmetic and copies ran while one was open for 1% of the time, Pallas kernels for 10%

profile of v6, /device:TPU:1, one launch (start us, length us, event | category | flops | bytes accessed | tf_op | source)
XLA Modules:
  0.0 204.5 jit_solution(7052344180505195959)
XLA Ops:
  0.6 10.5 %shard_map.77 = (bf16[8,33,2,16,256]{4,3,2,1,0:T(8,128)(2,1)}, bf16[1,33,2,16,256]{4,3,2,1,0:T(8,128)(2,1)}, bf16[1,33,2,16,256]{4,3,2,1,0:T(8,128)(2,1)}, bf16[...) custom-call(s32[4,8]{1,0:T(4,128)} %target_ref.1, ...), custom_call_target="tpu_custom_call" | custom-call | flops 4294967296 | bytes 16777216 | tf_op jit(solution)/shard_map/pallas_call | solution.py:96
  11.2 7.7 %all-to-all-start = ((bf16[8,33,2,16,256]{4,3,2,1,0:T(8,128)(2,1)}), bf16[8,33,2,16,256]{4,3,2,1,0:T(8,128)(2,1)}, u32[]{:S(2)}, u32[]{:S(2)}) async-start(bf16[8,33,2,16,256]{4,3,2,1,0:T(8,128)(2,1)} %get-tuple-element.24), calls=%async_computation | async-start | bytes 8650752 | tf_op jit(solution)/shard_map/all_to_all | solution.py:347
  23.0 23.2 %collective-permute-done.refs_0_.refs_3_ = bf16[2,33,2,16,256]{4,3,2,1,0:T(8,128)(2,1)S(1)} collective-permute-done((bf16[2,33,2,16,256]{4,3,2,1,0:T(8,128)(2,1)}, bf16[2,33,2,16,256]{4,3,2,1,0:T(8,128)(2,1)S(1)}, u32[]{:S(2)}, u32[]{:S(2)}) %collective-permute-start) | collective-permute-done | bytes 1081376 | tf_op jit(solution)/shard_map/ppermute | solution.py:356
  46.3 22.0 %collective-permute-done.1.refs_1_.refs_4_ = bf16[2,33,2,16,256]{4,3,2,1,0:T(8,128)(2,1)S(1)} collective-permute-done((bf16[2,33,2,16,256]{4,3,2,1,0:T(8,128)(2,1)}, bf16[2,33,2,16,256]{4,3,2,1,0:T(8,128)(2,1)S(1)}, u32[]{:S(2)}, u32[]{:S(2)}) %collective-permute-start.1) | collective-permute-done | bytes 1081376 | tf_op jit(solution)/shard_map/ppermute | solution.py:356
  73.2 7.2 %shard_map.79.refs_0_ = bf16[256,2,16,256]{3,2,1,0:T(8,128)(2,1)} custom-call(f32[8,128]{1,0:T(8,128)} %copy-done.9, bf16[1,33,2,16,256]{4,3,2,1,0:T(8,128)(2,1)} %collective-permute-done.3.refs_1_.refs_2_, bf16[8,33,2,16,256]{4,3,2,1,0:T(8,128)(2,1)} %all-to-all-done.refs_2_), custom_call_target="tpu_custom_call" | custom-call | flops 4194304 | bytes 8388608 | tf_op jit(solution)/shard_map/pallas_call | solution.py:199
  80.5 4.9 %all-to-all-start.1 = ((bf16[4,64,2,16,256]{4,3,2,1,0:T(8,128)(2,1)}), bf16[4,64,2,16,256]{4,3,2,1,0:T(8,128)(2,1)}, u32[]{:S(2)}, u32[]{:S(2)}) async-start(bf16[4,64,2,16,256]{4,3,2,1,0:T(8,128)(2,1)} %bitcast.17), calls=%async_computation.1 | async-start | bytes 8388608 | tf_op jit(solution)/shard_map/all_to_all | solution.py:347
  85.3 7.2 %shard_map.80 = (bf16[8,32,2,16,256]{4,3,2,1,0:T(8,128)(2,1)}, bf16[16,2,16,256]{3,2,1,0:T(8,128)(2,1)}, bf16[16,2,16,256]{3,2,1,0:T(8,128)(2,1)}) custom-call(bf16[256,2,16,256]{3,2,1,0:T(8,128)(2,1)} %shard_map.79.refs_0_, bf16[1,33,2,16,256]{4,3,2,1,0:T(8,128)(2,1)} %get-tuple-element.25.refs_1_, ...), custom_call_target="tpu_custom_call" | custom-call | flops 4194304 | bytes 8388608 | tf_op jit(solution)/shard_map/pallas_call | solution.py:199
  92.6 4.3 %collective-permute-start.9 = (bf16[16,2,16,256]{3,2,1,0:T(8,128)(2,1)}, bf16[16,2,16,256]{3,2,1,0:T(8,128)(2,1)S(1)}, u32[]{:S(2)}, u32[]{:S(2)}) collective-permute-start(bf16[16,2,16,256]{3,2,1,0:T(8,128)(2,1)} %get-tuple-element.29), channel_id=1, source_target_pairs={{0,224},{32,0},{64,32},{96,64},{128,96},{160,128},{192,160},{224,1... | collective-permute-start | bytes 786440 | tf_op jit(solution)/shard_map/ppermute | solution.py:356
  96.9 6.0 %collective-permute-done.9.extra = bf16[16,2,16,256]{3,2,1,0:T(8,128)(2,1)S(1)} collective-permute-done((bf16[16,2,16,256]{3,2,1,0:T(8,128)(2,1)}, bf16[16,2,16,256]{3,2,1,0:T(8,128)(2,1)S(1)}, u32[]{:S(2)}, u32[]{:S(2)}) %collective-permute-start.9) | collective-permute-done | bytes 262176 | tf_op jit(solution)/shard_map/ppermute | solution.py:356
  105.2 3.5 %collective-permute-start.10 = (bf16[32,2,16,256]{3,2,1,0:T(8,128)(2,1)S(1)}, bf16[32,2,16,256]{3,2,1,0:T(8,128)(2,1)S(1)}, u32[]{:S(2)}, u32[]{:S(2)}) collective-permute-start(bf16[32,2,16,256]{3,2,1,0:T(8,128)(2,1)S(1)} %shard_map.84), channel_id=1, source_target_pairs={{0,224},{32,0},{64,32},{96,64},{128,96},{160,128},{192,160},{224,1... | collective-permute-start | bytes 1572872 | tf_op jit(solution)/shard_map/ppermute | solution.py:356
  108.8 10.4 %collective-permute-done.10.extra = bf16[32,2,16,256]{3,2,1,0:T(8,128)(2,1)S(1)} collective-permute-done((bf16[32,2,16,256]{3,2,1,0:T(8,128)(2,1)S(1)}, bf16[32,2,16,256]{3,2,1,0:T(8,128)(2,1)S(1)}, u32[]{:S(2)}, u32[]{:S(2)}) %collective-permute-start.10) | collective-permute-done | bytes 524320 | tf_op jit(solution)/shard_map/ppermute | solution.py:356
  119.4 3.8 %collective-permute-start.11 = (bf16[32,2,16,256]{3,2,1,0:T(8,128)(2,1)S(1)}, bf16[32,2,16,256]{3,2,1,0:T(8,128)(2,1)S(1)}, u32[]{:S(2)}, u32[]{:S(2)}) collective-permute-start(bf16[32,2,16,256]{3,2,1,0:T(8,128)(2,1)S(1)} %shard_map.85), channel_id=1, source_target_pairs={{0,224},{32,0},{64,32},{96,64},{128,96},{160,128},{192,160},{224,1... | collective-permute-start | bytes 1572872 | tf_op jit(solution)/shard_map/ppermute | solution.py:356
  123.4 9.5 %collective-permute-done.11.extra = bf16[32,2,16,256]{3,2,1,0:T(8,128)(2,1)S(1)} collective-permute-done((bf16[32,2,16,256]{3,2,1,0:T(8,128)(2,1)S(1)}, bf16[32,2,16,256]{3,2,1,0:T(8,128)(2,1)S(1)}, u32[]{:S(2)}, u32[]{:S(2)}) %collective-permute-start.11) | collective-permute-done | bytes 524320 | tf_op jit(solution)/shard_map/ppermute | solution.py:356
  133.0 3.6 %collective-permute-start.12 = (bf16[32,2,16,256]{3,2,1,0:T(8,128)(2,1)S(1)}, bf16[32,2,16,256]{3,2,1,0:T(8,128)(2,1)S(1)}, u32[]{:S(2)}, u32[]{:S(2)}) collective-permute-start(bf16[32,2,16,256]{3,2,1,0:T(8,128)(2,1)S(1)} %shard_map.86), channel_id=1, source_target_pairs={{0,224},{32,0},{64,32},{96,64},{128,96},{160,128},{192,160},{224,1... | collective-permute-start | bytes 1572872 | tf_op jit(solution)/shard_map/ppermute | solution.py:356
  136.9 3.2 %shard_map.88.refs_0_ = bf16[64,2,16,256]{3,2,1,0:T(8,128)(2,1)S(1)} custom-call(bf16[4,64,2,16,256]{4,3,2,1,0:T(8,128)(2,1)} %all-to-all-done.1.blocks), custom_call_target="tpu_custom_call" | custom-call | flops 4194304 | bytes 4194304 | tf_op jit(solution)/shard_map/pallas_call | solution.py:286
  141.1 4.5 %collective-permute-done.12.down.refs_2_ = bf16[32,2,16,256]{3,2,1,0:T(8,128)(2,1)S(1)} collective-permute-done((bf16[32,2,16,256]{3,2,1,0:T(8,128)(2,1)S(1)}, bf16[32,2,16,256]{3,2,1,0:T(8,128)(2,1)S(1)}, u32[]{:S(2)}, u32[]{:S(2)}) %collective-permute-start.12) | collective-permute-done | bytes 524320 | tf_op jit(solution)/shard_map/ppermute | solution.py:356
  145.6 3.4 %collective-permute-done.8.up.refs_1_ = bf16[32,2,16,256]{3,2,1,0:T(8,128)(2,1)} collective-permute-done((bf16[32,2,16,256]{3,2,1,0:T(8,128)(2,1)S(1)}, bf16[32,2,16,256]{3,2,1,0:T(8,128)(2,1)}, u32[]{:S(2)}, u32[]{:S(2)}) %collective-permute-start.8) | collective-permute-done | bytes 524320 | tf_op jit(solution)/shard_map/ppermute | solution.py:356
  149.0 3.7 %all-to-all-start.2 = ((bf16[8,8,2,16,256]{4,3,2,1,0:T(8,128)(2,1)}), bf16[8,8,2,16,256]{4,3,2,1,0:T(8,128)(2,1)S(1)}, u32[]{:S(2)}, u32[]{:S(2)}) async-start(bf16[8,8,2,16,256]{4,3,2,1,0:T(8,128)(2,1)} %bitcast.16), calls=%async_computation.2 | async-start | bytes 2097152 | tf_op jit(solution)/shard_map/all_to_all | solution.py:347
  158.3 3.9 %collective-permute-start.14 = (bf16[8,2,16,256]{3,2,1,0:T(8,128)(2,1)S(1)}, bf16[8,2,16,256]{3,2,1,0:T(8,128)(2,1)S(1)}, u32[]{:S(2)}, u32[]{:S(2)}) collective-permute-start(bf16[8,2,16,256]{3,2,1,0:T(8,128)(2,1)S(1)} %get-tuple-element.31), channel_id=1, source_target_pairs={{0,8},{2,16},{4,24},{6,0},{8,10},{10,18},{12,26},{14,2},{16,12},{1... | collective-permute-start | bytes 393224 | tf_op jit(solution)/shard_map/ppermute | solution.py:367
  162.2 3.1 %collective-permute-start.15 = (bf16[8,2,16,256]{3,2,1,0:T(8,128)(2,1)S(1)}, bf16[8,2,16,256]{3,2,1,0:T(8,128)(2,1)S(1)}, u32[]{:S(2)}, u32[]{:S(2)}) collective-permute-start(bf16[8,2,16,256]{3,2,1,0:T(8,128)(2,1)S(1)} %get-tuple-element.32), channel_id=1, source_target_pairs={{0,16},{2,24},{4,0},{6,8},{8,18},{10,26},{12,2},{14,10},{16,20},{1... | collective-permute-start | bytes 393224 | tf_op jit(solution)/shard_map/ppermute | solution.py:367
  167.5 3.2 %collective-permute-done.15 = bf16[8,2,16,256]{3,2,1,0:T(8,128)(2,1)S(1)} collective-permute-done((bf16[8,2,16,256]{3,2,1,0:T(8,128)(2,1)S(1)}, bf16[8,2,16,256]{3,2,1,0:T(8,128)(2,1)S(1)}, u32[]{:S(2)}, u32[]{:S(2)}) %collective-permute-start.15) | collective-permute-done | bytes 131104 | tf_op jit(solution)/shard_map/ppermute | solution.py:367
  171.5 7.7 %all-to-all-done.2.second = bf16[8,8,2,16,256]{4,3,2,1,0:T(8,128)(2,1)S(1)} async-done(((bf16[8,8,2,16,256]{4,3,2,1,0:T(8,128)(2,1)}), bf16[8,8,2,16,256]{4,3,2,1,0:T(8,128)(2,1)S(1)}, u32[]{:S(2)}, u32[]{:S(2)}) %all-to-all-start.2) | async-done | bytes 1048608 | tf_op jit(solution)/shard_map/all_to_all | solution.py:347
  180.2 12.0 %all_to_all.25 = f32[8,2,2]{2,1,0:T(2,128)S(1)} all-to-all(f32[8,2,2]{2,1,0:T(2,128)S(1)} %broadcast_in_dim.4), channel_id=1, replica_groups=mesh['z'=8,'x'=4,'y'=4,'core'=2] {'y','core'}, dimensions={0} | all-to-all | bytes 256 | tf_op jit(solution)/shard_map/all_to_all | solution.py:347
  192.3 11.6 %all_to_all.26 = f32[32,2,2]{2,1,0:T(2,128)S(1)} all-to-all(f32[32,2,2]{2,1,0:T(2,128)S(1)} %broadcast_in_dim.5), channel_id=1, replica_groups=mesh['z'=8,'x'=4,'y'=4,'core'=2] {'z','x'}, dimensions={0} | all-to-all | bytes 1024 | tf_op jit(solution)/shard_map/all_to_all | solution.py:347
  (64 shorter events, 23.4 us)
Async XLA Ops:
  0.6 153.1 %copy-start = (bf16[8,256,256]{2,1,0:T(8,128)(2,1)S(1)}, bf16[8,256,256]{2,1,0:T(8,128)(2,1)}, u32[]{:S(2)}) copy-start(bf16[8,256,256]{2,1,0:T(8,128)(2,1)} %param.10) | copy-start | bytes 3145732
  11.2 62.0 %all-to-all-start = ((bf16[8,33,2,16,256]{4,3,2,1,0:T(8,128)(2,1)}), bf16[8,33,2,16,256]{4,3,2,1,0:T(8,128)(2,1)}, u32[]{:S(2)}, u32[]{:S(2)}) async-start(bf16[8,33,2,16,256]{4,3,2,1,0:T(8,128)(2,1)} %get-tuple-element.24), calls=%async_computation | async-start | bytes 8650752 | tf_op jit(solution)/shard_map/all_to_all | solution.py:347
  18.9 27.4 %collective-permute-start = (bf16[2,33,2,16,256]{4,3,2,1,0:T(8,128)(2,1)}, bf16[2,33,2,16,256]{4,3,2,1,0:T(8,128)(2,1)S(1)}, u32[]{:S(2)}, u32[]{:S(2)}) collective-permute-start(bf16[2,33,2,16,256]{4,3,2,1,0:T(8,128)(2,1)} %get-tuple-element.19), channel_id=1, source_target_pairs={{0,8},{8,16},{16,24},{24,0},{1,9},{9,17},{17,25},{25,1},{2,10},{10... | collective-permute-start | bytes 3244040 | tf_op jit(solution)/shard_map/ppermute | solution.py:356
  18.9 49.3 %collective-permute-start.1 = (bf16[2,33,2,16,256]{4,3,2,1,0:T(8,128)(2,1)}, bf16[2,33,2,16,256]{4,3,2,1,0:T(8,128)(2,1)S(1)}, u32[]{:S(2)}, u32[]{:S(2)}) collective-permute-start(bf16[2,33,2,16,256]{4,3,2,1,0:T(8,128)(2,1)} %get-tuple-element.20), channel_id=1, source_target_pairs={{0,16},{8,24},{16,0},{24,8},{1,17},{9,25},{17,1},{25,9},{2,18},{10... | collective-permute-start | bytes 3244040 | tf_op jit(solution)/shard_map/ppermute | solution.py:356
  20.8 48.3 %collective-permute-start.2 = (bf16[2,33,2,16,256]{4,3,2,1,0:T(8,128)(2,1)}, bf16[2,33,2,16,256]{4,3,2,1,0:T(8,128)(2,1)S(1)}, u32[]{:S(2)}, u32[]{:S(2)}) collective-permute-start(bf16[2,33,2,16,256]{4,3,2,1,0:T(8,128)(2,1)} %get-tuple-element.21), channel_id=1, source_target_pairs={{0,24},{8,0},{16,8},{24,16},{1,25},{9,1},{17,9},{25,17},{2,26},{10... | collective-permute-start | bytes 3244040 | tf_op jit(solution)/shard_map/ppermute | solution.py:356
  22.0 51.2 %collective-permute-start.3 = (bf16[1,33,2,16,256]{4,3,2,1,0:T(8,128)(2,1)}, bf16[1,33,2,16,256]{4,3,2,1,0:T(8,128)(2,1)}, u32[]{:S(2)}, u32[]{:S(2)}) collective-permute-start(bf16[1,33,2,16,256]{4,3,2,1,0:T(8,128)(2,1)} %get-tuple-element.23), channel_id=1, source_target_pairs={{0,1},{1,0},{2,3},{3,2},{4,5},{5,4},{6,7},{7,6},{8,9},{9,8},{10,11... | collective-permute-start | bytes 1622024 | tf_op jit(solution)/shard_map/ppermute | solution.py:360
  46.3 34.2 %copy-start.4 = (bf16[2,33,2,16,256]{4,3,2,1,0:T(8,128)(2,1)}, bf16[2,33,2,16,256]{4,3,2,1,0:T(8,128)(2,1)S(1)}, u32[]{:S(2)}) copy-start(bf16[2,33,2,16,256]{4,3,2,1,0:T(8,128)(2,1)S(1)} %collective-permute-done.refs_0_.refs_3_) | copy-start | bytes 3244036
  68.2 12.3 %copy-start.5 = (bf16[2,33,2,16,256]{4,3,2,1,0:T(8,128)(2,1)}, bf16[2,33,2,16,256]{4,3,2,1,0:T(8,128)(2,1)S(1)}, u32[]{:S(2)}) copy-start(bf16[2,33,2,16,256]{4,3,2,1,0:T(8,128)(2,1)S(1)} %collective-permute-done.1.refs_1_.refs_4_) | copy-start | bytes 3244036
  71.9 13.4 %collective-permute-start.4 = (bf16[3,33,2,16,256]{4,3,2,1,0:T(8,128)(2,1)}, bf16[3,33,2,16,256]{4,3,2,1,0:T(8,128)(2,1)}, u32[]{:S(2)}, u32[]{:S(2)}) collective-permute-start(bf16[3,33,2,16,256]{4,3,2,1,0:T(8,128)(2,1)} %get-tuple-element.26), channel_id=1, source_target_pairs={{0,1},{1,0},{2,3},{3,2},{4,5},{5,4},{6,7},{7,6},{8,9},{9,8},{10,11... | collective-permute-start | bytes 4866056 | tf_op jit(solution)/shard_map/ppermute | solution.py:360
  80.5 56.4 %all-to-all-start.1 = ((bf16[4,64,2,16,256]{4,3,2,1,0:T(8,128)(2,1)}), bf16[4,64,2,16,256]{4,3,2,1,0:T(8,128)(2,1)}, u32[]{:S(2)}, u32[]{:S(2)}) async-start(bf16[4,64,2,16,256]{4,3,2,1,0:T(8,128)(2,1)} %bitcast.17), calls=%async_computation.1 | async-start | bytes 8388608 | tf_op jit(solution)/shard_map/all_to_all | solution.py:347
  92.6 10.4 %collective-permute-start.9 = (bf16[16,2,16,256]{3,2,1,0:T(8,128)(2,1)}, bf16[16,2,16,256]{3,2,1,0:T(8,128)(2,1)S(1)}, u32[]{:S(2)}, u32[]{:S(2)}) collective-permute-start(bf16[16,2,16,256]{3,2,1,0:T(8,128)(2,1)} %get-tuple-element.29), channel_id=1, source_target_pairs={{0,224},{32,0},{64,32},{96,64},{128,96},{160,128},{192,160},{224,1... | collective-permute-start | bytes 786440 | tf_op jit(solution)/shard_map/ppermute | solution.py:356
  96.9 11.8 %collective-permute-start.5 = (bf16[16,2,16,256]{3,2,1,0:T(8,128)(2,1)}, bf16[16,2,16,256]{3,2,1,0:T(8,128)(2,1)S(1)}, u32[]{:S(2)}, u32[]{:S(2)}) collective-permute-start(bf16[16,2,16,256]{3,2,1,0:T(8,128)(2,1)} %get-tuple-element.28), channel_id=1, source_target_pairs={{0,32},{32,64},{64,96},{96,128},{128,160},{160,192},{192,224},{224... | collective-permute-start | bytes 786440 | tf_op jit(solution)/shard_map/ppermute | solution.py:356
  105.2 14.1 %collective-permute-start.10 = (bf16[32,2,16,256]{3,2,1,0:T(8,128)(2,1)S(1)}, bf16[32,2,16,256]{3,2,1,0:T(8,128)(2,1)S(1)}, u32[]{:S(2)}, u32[]{:S(2)}) collective-permute-start(bf16[32,2,16,256]{3,2,1,0:T(8,128)(2,1)S(1)} %shard_map.84), channel_id=1, source_target_pairs={{0,224},{32,0},{64,32},{96,64},{128,96},{160,128},{192,160},{224,1... | collective-permute-start | bytes 1572872 | tf_op jit(solution)/shard_map/ppermute | solution.py:356
  108.7 14.4 %collective-permute-start.6 = (bf16[32,2,16,256]{3,2,1,0:T(8,128)(2,1)S(1)}, bf16[32,2,16,256]{3,2,1,0:T(8,128)(2,1)S(1)}, u32[]{:S(2)}, u32[]{:S(2)}) collective-permute-start(bf16[32,2,16,256]{3,2,1,0:T(8,128)(2,1)S(1)} %shard_map.81), channel_id=1, source_target_pairs={{0,32},{32,64},{64,96},{96,128},{128,160},{160,192},{192,224},{224... | collective-permute-start | bytes 1572872 | tf_op jit(solution)/shard_map/ppermute | solution.py:356
  119.4 13.5 %collective-permute-start.11 = (bf16[32,2,16,256]{3,2,1,0:T(8,128)(2,1)S(1)}, bf16[32,2,16,256]{3,2,1,0:T(8,128)(2,1)S(1)}, u32[]{:S(2)}, u32[]{:S(2)}) collective-permute-start(bf16[32,2,16,256]{3,2,1,0:T(8,128)(2,1)S(1)} %shard_map.85), channel_id=1, source_target_pairs={{0,224},{32,0},{64,32},{96,64},{128,96},{160,128},{192,160},{224,1... | collective-permute-start | bytes 1572872 | tf_op jit(solution)/shard_map/ppermute | solution.py:356
  123.3 13.4 %collective-permute-start.7 = (bf16[32,2,16,256]{3,2,1,0:T(8,128)(2,1)S(1)}, bf16[32,2,16,256]{3,2,1,0:T(8,128)(2,1)S(1)}, u32[]{:S(2)}, u32[]{:S(2)}) collective-permute-start(bf16[32,2,16,256]{3,2,1,0:T(8,128)(2,1)S(1)} %shard_map.82), channel_id=1, source_target_pairs={{0,32},{32,64},{64,96},{96,128},{128,160},{160,192},{192,224},{224... | collective-permute-start | bytes 1572872 | tf_op jit(solution)/shard_map/ppermute | solution.py:356
  133.0 12.5 %collective-permute-start.12 = (bf16[32,2,16,256]{3,2,1,0:T(8,128)(2,1)S(1)}, bf16[32,2,16,256]{3,2,1,0:T(8,128)(2,1)S(1)}, u32[]{:S(2)}, u32[]{:S(2)}) collective-permute-start(bf16[32,2,16,256]{3,2,1,0:T(8,128)(2,1)S(1)} %shard_map.86), channel_id=1, source_target_pairs={{0,224},{32,0},{64,32},{96,64},{128,96},{160,128},{192,160},{224,1... | collective-permute-start | bytes 1572872 | tf_op jit(solution)/shard_map/ppermute | solution.py:356
  136.8 12.3 %collective-permute-start.8 = (bf16[32,2,16,256]{3,2,1,0:T(8,128)(2,1)S(1)}, bf16[32,2,16,256]{3,2,1,0:T(8,128)(2,1)}, u32[]{:S(2)}, u32[]{:S(2)}) collective-permute-start(bf16[32,2,16,256]{3,2,1,0:T(8,128)(2,1)S(1)} %shard_map.83), channel_id=1, source_target_pairs={{0,32},{32,64},{64,96},{96,128},{128,160},{160,192},{192,224},{224... | collective-permute-start | bytes 1572872 | tf_op jit(solution)/shard_map/ppermute | solution.py:356
  149.0 30.2 %all-to-all-start.2 = ((bf16[8,8,2,16,256]{4,3,2,1,0:T(8,128)(2,1)}), bf16[8,8,2,16,256]{4,3,2,1,0:T(8,128)(2,1)S(1)}, u32[]{:S(2)}, u32[]{:S(2)}) async-start(bf16[8,8,2,16,256]{4,3,2,1,0:T(8,128)(2,1)} %bitcast.16), calls=%async_computation.2 | async-start | bytes 2097152 | tf_op jit(solution)/shard_map/all_to_all | solution.py:347
  156.2 10.8 %copy-start.11 = (bf16[8,32,256]{2,1,0:T(8,128)(2,1)S(1)}, bf16[8,32,256]{2,1,0:T(8,128)(2,1)}, u32[]{:S(2)}) copy-start(bf16[8,32,256]{2,1,0:T(8,128)(2,1)} %param.9) | copy-start | bytes 393220
  157.6 9.9 %collective-permute-start.13 = (bf16[8,2,16,256]{3,2,1,0:T(8,128)(2,1)S(1)}, bf16[8,2,16,256]{3,2,1,0:T(8,128)(2,1)S(1)}, u32[]{:S(2)}, u32[]{:S(2)}) collective-permute-start(bf16[8,2,16,256]{3,2,1,0:T(8,128)(2,1)S(1)} %get-tuple-element.30), channel_id=1, source_target_pairs={{0,0},{2,8},{4,16},{6,24},{8,2},{10,10},{12,18},{14,26},{16,4},{18... | collective-permute-start | bytes 393224 | tf_op jit(solution)/shard_map/ppermute | solution.py:367
  158.3 9.2 %collective-permute-start.14 = (bf16[8,2,16,256]{3,2,1,0:T(8,128)(2,1)S(1)}, bf16[8,2,16,256]{3,2,1,0:T(8,128)(2,1)S(1)}, u32[]{:S(2)}, u32[]{:S(2)}) collective-permute-start(bf16[8,2,16,256]{3,2,1,0:T(8,128)(2,1)S(1)} %get-tuple-element.31), channel_id=1, source_target_pairs={{0,8},{2,16},{4,24},{6,0},{8,10},{10,18},{12,26},{14,2},{16,12},{1... | collective-permute-start | bytes 393224 | tf_op jit(solution)/shard_map/ppermute | solution.py:367
  162.2 8.5 %collective-permute-start.15 = (bf16[8,2,16,256]{3,2,1,0:T(8,128)(2,1)S(1)}, bf16[8,2,16,256]{3,2,1,0:T(8,128)(2,1)S(1)}, u32[]{:S(2)}, u32[]{:S(2)}) collective-permute-start(bf16[8,2,16,256]{3,2,1,0:T(8,128)(2,1)S(1)} %get-tuple-element.32), channel_id=1, source_target_pairs={{0,16},{2,24},{4,0},{6,8},{8,18},{10,26},{12,2},{14,10},{16,20},{1... | collective-permute-start | bytes 393224 | tf_op jit(solution)/shard_map/ppermute | solution.py:367
  165.3 6.1 %collective-permute-start.16 = (bf16[8,2,16,256]{3,2,1,0:T(8,128)(2,1)S(1)}, bf16[8,2,16,256]{3,2,1,0:T(8,128)(2,1)S(1)}, u32[]{:S(2)}, u32[]{:S(2)}) collective-permute-start(bf16[8,2,16,256]{3,2,1,0:T(8,128)(2,1)S(1)} %get-tuple-element.33), channel_id=1, source_target_pairs={{0,24},{2,0},{4,8},{6,16},{8,26},{10,2},{12,10},{14,18},{16,28},{1... | collective-permute-start | bytes 393224 | tf_op jit(solution)/shard_map/ppermute | solution.py:367
  (8 other events, 26.2 us)

commit v7 on v6

--- a/solution.py
+++ b/solution.py
@@ -149,10 +149,21 @@
 
 def merge_kernel(z_first, hints, *refs):
     refs = refs[hints:]
-    rows, table, sums, stage, table_sem, sems = refs[-6:]
-    ins, outs = (refs[: RING + 2], refs[RING + 2 : -6]) if z_first else (refs[:1], refs[1:-6])
-    sources = [(ref, j) for ref in ins for j in range(ref.shape[0])]
-    pairs = ins[0].shape[1] - 1
+    buf, in_sems, rows, table, sums, stage, table_sem, sems = refs[-8:]
+    ins, outs = (refs[: RING + 2], refs[RING + 2 : -8]) if z_first else (refs[:1], refs[1:-8])
+    counts = [1] * (RING + 1) + [RING - 1] if z_first else [GROUPS]
+    given = [(ref, j) for ref, n in zip(ins, counts, strict=True) for j in range(n)]
+    loads = [
+        pltpu.make_async_copy(ref.at[j], buf.at[i], in_sems.at[i])
+        for i, (ref, j) in enumerate(given)
+    ]
+    for load in loads:
+        load.start()
+    sums[...] = jnp.zeros_like(sums)
+    for load in loads:
+        load.wait()
+    sources = [(buf, i) for i in range(GROUPS)]
+    pairs = buf.shape[1] - 1
     here = lax.axis_index("z")
     for i, (ref, j) in enumerate(sources):
         t = ref[j, pairs, 0, :, :128].astype(F32)[:8].astype(jnp.int32)
@@ -163,7 +174,6 @@
         rows[8 * i : 8 * i + 8, :] = t
     copy = pltpu.make_async_copy(rows, table, table_sem)
     copy.start()
-    sums[...] = jnp.zeros_like(sums)
     copy.wait()
     for i, (ref, j) in enumerate(sources):
 
@@ -199,10 +209,12 @@
     return pl.pallas_call(
         functools.partial(merge_kernel, z_first, len(hints)),
         grid=(1,),
-        in_specs=[ANY] * len(hints) + [own] * (len(blocks) - 1) + [full],
+        in_specs=[ANY] * len(hints) + [HBM] * len(blocks),
         out_specs=[HBM] * len(shapes),
         out_shape=[jax.ShapeDtypeStruct((*shape, *block), BF16) for shape in shapes],
         scratch_shapes=[
+            pltpu.VMEM((GROUPS, *blocks[-1].shape[1:]), BF16),
+            pltpu.SemaphoreType.DMA((GROUPS,)),
             pltpu.VMEM((GROUPS * 8, 128), jnp.int32),
             pltpu.SMEM((GROUPS * 8, 128), jnp.int32),
             pltpu.VMEM((sectors, *block), F32),

time: 205 us -> 204 us (level)
  no operation moved by 1% of the time
where the time goes in v7:
time: 204 us; the launch traced here: 203 us
  waiting for transfers between devices  91.7 us (45%)
  starting transfers between devices  46.4 us (23%)
  Pallas kernels  31.4 us (15%)
  blocking collectives  23.6 us (12%)
  local copies, waits for them, and re-layouts  8 us (4%)
    ppermute x11, waiting for transfers between devices, shift(): return lax.ppermute(x, axis, [(i, (i + k) % n) for i in range(n)])  80 us
    all_to_all x2, blocking collectives, to_all(): return lax.all_to_all(x, axes, 0, 0, tiled=True)  23.6 us
    ppermute x11, starting transfers between devices, shift(): return lax.ppermute(x, axis, [(i, (i + k) % n) for i in range(n)])  18.5 us
    all_to_all x3, starting transfers between devices, to_all(): return lax.all_to_all(x, axes, 0, 0, tiled=True)  16.2 us
    pallas_call x2, Pallas kernels, merge(): pl.pallas_call(functools.partial(merge_kernel, z_first, len(hints)), grid...  13.4 us
    pallas_call x1, Pallas kernels, contract(): pl.pallas_call(contract_kernel, grid=(terms,), in_specs=[VMEM, pl.BlockSp...  10.5 us
    ppermute x4, starting transfers between devices, turn(): return lax.ppermute(x, ('x', 'y'), pairs)  9.39 us
    all_to_all x3, waiting for transfers between devices, to_all(): return lax.all_to_all(x, axes, 0, 0, tiled=True)  7.72 us
  transfers between devices with their start and end apart: 20, of which 11 were waited for; matrix products, arithmetic and copies ran while one was open for 1% of the time, Pallas kernels for 10%

profile of v7, /device:TPU:1, one launch (start us, length us, event | category | flops | bytes accessed | tf_op | source)
XLA Modules:
  0.0 203.5 jit_solution(13032282090118630065)
XLA Ops:
  0.6 10.5 %shard_map.77 = (bf16[8,33,2,16,256]{4,3,2,1,0:T(8,128)(2,1)}, bf16[1,33,2,16,256]{4,3,2,1,0:T(8,128)(2,1)}, bf16[1,33,2,16,256]{4,3,2,1,0:T(8,128)(2,1)}, bf16[...) custom-call(s32[4,8]{1,0:T(4,128)} %target_ref.1, ...), custom_call_target="tpu_custom_call" | custom-call | flops 4294967296 | bytes 16777216 | tf_op jit(solution)/shard_map/pallas_call | solution.py:96
  11.2 7.7 %all-to-all-start = ((bf16[8,33,2,16,256]{4,3,2,1,0:T(8,128)(2,1)}), bf16[8,33,2,16,256]{4,3,2,1,0:T(8,128)(2,1)}, u32[]{:S(2)}, u32[]{:S(2)}) async-start(bf16[8,33,2,16,256]{4,3,2,1,0:T(8,128)(2,1)} %get-tuple-element.24), calls=%async_computation | async-start | bytes 8650752 | tf_op jit(solution)/shard_map/all_to_all | solution.py:359
  23.0 23.2 %collective-permute-done.refs_0_.refs_3_ = bf16[2,33,2,16,256]{4,3,2,1,0:T(8,128)(2,1)S(1)} collective-permute-done((bf16[2,33,2,16,256]{4,3,2,1,0:T(8,128)(2,1)}, bf16[2,33,2,16,256]{4,3,2,1,0:T(8,128)(2,1)S(1)}, u32[]{:S(2)}, u32[]{:S(2)}) %collective-permute-start) | collective-permute-done | bytes 1081376 | tf_op jit(solution)/shard_map/ppermute | solution.py:368
  46.3 22.0 %collective-permute-done.1.refs_1_.refs_4_ = bf16[2,33,2,16,256]{4,3,2,1,0:T(8,128)(2,1)S(1)} collective-permute-done((bf16[2,33,2,16,256]{4,3,2,1,0:T(8,128)(2,1)}, bf16[2,33,2,16,256]{4,3,2,1,0:T(8,128)(2,1)S(1)}, u32[]{:S(2)}, u32[]{:S(2)}) %collective-permute-start.1) | collective-permute-done | bytes 1081376 | tf_op jit(solution)/shard_map/ppermute | solution.py:368
  73.2 6.7 %shard_map.79.refs_0_ = bf16[256,2,16,256]{3,2,1,0:T(8,128)(2,1)} custom-call(f32[8,128]{1,0:T(8,128)} %copy-done.9, bf16[1,33,2,16,256]{4,3,2,1,0:T(8,128)(2,1)} %collective-permute-done.3.refs_1_.refs_2_, bf16[8,33,2,16,256]{4,3,2,1,0:T(8,128)(2,1)} %all-to-all-done.refs_2_), custom_call_target="tpu_custom_call" | custom-call | flops 4194304 | bytes 8388608 | tf_op jit(solution)/shard_map/pallas_call | solution.py:209
  80.0 4.9 %all-to-all-start.1 = ((bf16[4,64,2,16,256]{4,3,2,1,0:T(8,128)(2,1)}), bf16[4,64,2,16,256]{4,3,2,1,0:T(8,128)(2,1)}, u32[]{:S(2)}, u32[]{:S(2)}) async-start(bf16[4,64,2,16,256]{4,3,2,1,0:T(8,128)(2,1)} %bitcast.17), calls=%async_computation.1 | async-start | bytes 8388608 | tf_op jit(solution)/shard_map/all_to_all | solution.py:359
  84.8 6.7 %shard_map.80 = (bf16[8,32,2,16,256]{4,3,2,1,0:T(8,128)(2,1)}, bf16[16,2,16,256]{3,2,1,0:T(8,128)(2,1)}, bf16[16,2,16,256]{3,2,1,0:T(8,128)(2,1)}) custom-call(bf16[256,2,16,256]{3,2,1,0:T(8,128)(2,1)} %shard_map.79.refs_0_, bf16[1,33,2,16,256]{4,3,2,1,0:T(8,128)(2,1)} %get-tuple-element.25.refs_1_, ...), custom_call_target="tpu_custom_call" | custom-call | flops 4194304 | bytes 8388608 | tf_op jit(solution)/shard_map/pallas_call | solution.py:209
  91.5 4.3 %collective-permute-start.9 = (bf16[16,2,16,256]{3,2,1,0:T(8,128)(2,1)}, bf16[16,2,16,256]{3,2,1,0:T(8,128)(2,1)S(1)}, u32[]{:S(2)}, u32[]{:S(2)}) collective-permute-start(bf16[16,2,16,256]{3,2,1,0:T(8,128)(2,1)} %get-tuple-element.29), channel_id=1, source_target_pairs={{0,224},{32,0},{64,32},{96,64},{128,96},{160,128},{192,160},{224,1... | collective-permute-start | bytes 786440 | tf_op jit(solution)/shard_map/ppermute | solution.py:368
  95.9 6.0 %collective-permute-done.9.extra = bf16[16,2,16,256]{3,2,1,0:T(8,128)(2,1)S(1)} collective-permute-done((bf16[16,2,16,256]{3,2,1,0:T(8,128)(2,1)}, bf16[16,2,16,256]{3,2,1,0:T(8,128)(2,1)S(1)}, u32[]{:S(2)}, u32[]{:S(2)}) %collective-permute-start.9) | collective-permute-done | bytes 262176 | tf_op jit(solution)/shard_map/ppermute | solution.py:368
  104.2 3.5 %collective-permute-start.10 = (bf16[32,2,16,256]{3,2,1,0:T(8,128)(2,1)S(1)}, bf16[32,2,16,256]{3,2,1,0:T(8,128)(2,1)S(1)}, u32[]{:S(2)}, u32[]{:S(2)}) collective-permute-start(bf16[32,2,16,256]{3,2,1,0:T(8,128)(2,1)S(1)} %shard_map.84), channel_id=1, source_target_pairs={{0,224},{32,0},{64,32},{96,64},{128,96},{160,128},{192,160},{224,1... | collective-permute-start | bytes 1572872 | tf_op jit(solution)/shard_map/ppermute | solution.py:368
  107.8 10.4 %collective-permute-done.10.extra = bf16[32,2,16,256]{3,2,1,0:T(8,128)(2,1)S(1)} collective-permute-done((bf16[32,2,16,256]{3,2,1,0:T(8,128)(2,1)S(1)}, bf16[32,2,16,256]{3,2,1,0:T(8,128)(2,1)S(1)}, u32[]{:S(2)}, u32[]{:S(2)}) %collective-permute-start.10) | collective-permute-done | bytes 524320 | tf_op jit(solution)/shard_map/ppermute | solution.py:368
  118.3 3.8 %collective-permute-start.11 = (bf16[32,2,16,256]{3,2,1,0:T(8,128)(2,1)S(1)}, bf16[32,2,16,256]{3,2,1,0:T(8,128)(2,1)S(1)}, u32[]{:S(2)}, u32[]{:S(2)}) collective-permute-start(bf16[32,2,16,256]{3,2,1,0:T(8,128)(2,1)S(1)} %shard_map.85), channel_id=1, source_target_pairs={{0,224},{32,0},{64,32},{96,64},{128,96},{160,128},{192,160},{224,1... | collective-permute-start | bytes 1572872 | tf_op jit(solution)/shard_map/ppermute | solution.py:368
  122.3 9.5 %collective-permute-done.11.extra = bf16[32,2,16,256]{3,2,1,0:T(8,128)(2,1)S(1)} collective-permute-done((bf16[32,2,16,256]{3,2,1,0:T(8,128)(2,1)S(1)}, bf16[32,2,16,256]{3,2,1,0:T(8,128)(2,1)S(1)}, u32[]{:S(2)}, u32[]{:S(2)}) %collective-permute-start.11) | collective-permute-done | bytes 524320 | tf_op jit(solution)/shard_map/ppermute | solution.py:368
  132.0 3.6 %collective-permute-start.12 = (bf16[32,2,16,256]{3,2,1,0:T(8,128)(2,1)S(1)}, bf16[32,2,16,256]{3,2,1,0:T(8,128)(2,1)S(1)}, u32[]{:S(2)}, u32[]{:S(2)}) collective-permute-start(bf16[32,2,16,256]{3,2,1,0:T(8,128)(2,1)S(1)} %shard_map.86), channel_id=1, source_target_pairs={{0,224},{32,0},{64,32},{96,64},{128,96},{160,128},{192,160},{224,1... | collective-permute-start | bytes 1572872 | tf_op jit(solution)/shard_map/ppermute | solution.py:368
  135.8 3.2 %shard_map.88.refs_0_ = bf16[64,2,16,256]{3,2,1,0:T(8,128)(2,1)S(1)} custom-call(bf16[4,64,2,16,256]{4,3,2,1,0:T(8,128)(2,1)} %all-to-all-done.1.blocks), custom_call_target="tpu_custom_call" | custom-call | flops 4194304 | bytes 4194304 | tf_op jit(solution)/shard_map/pallas_call | solution.py:298
  140.1 4.5 %collective-permute-done.12.down.refs_2_ = bf16[32,2,16,256]{3,2,1,0:T(8,128)(2,1)S(1)} collective-permute-done((bf16[32,2,16,256]{3,2,1,0:T(8,128)(2,1)S(1)}, bf16[32,2,16,256]{3,2,1,0:T(8,128)(2,1)S(1)}, u32[]{:S(2)}, u32[]{:S(2)}) %collective-permute-start.12) | collective-permute-done | bytes 524320 | tf_op jit(solution)/shard_map/ppermute | solution.py:368
  144.6 3.4 %collective-permute-done.8.up.refs_1_ = bf16[32,2,16,256]{3,2,1,0:T(8,128)(2,1)} collective-permute-done((bf16[32,2,16,256]{3,2,1,0:T(8,128)(2,1)S(1)}, bf16[32,2,16,256]{3,2,1,0:T(8,128)(2,1)}, u32[]{:S(2)}, u32[]{:S(2)}) %collective-permute-start.8) | collective-permute-done | bytes 524320 | tf_op jit(solution)/shard_map/ppermute | solution.py:368
  148.0 3.7 %all-to-all-start.2 = ((bf16[8,8,2,16,256]{4,3,2,1,0:T(8,128)(2,1)}), bf16[8,8,2,16,256]{4,3,2,1,0:T(8,128)(2,1)S(1)}, u32[]{:S(2)}, u32[]{:S(2)}) async-start(bf16[8,8,2,16,256]{4,3,2,1,0:T(8,128)(2,1)} %bitcast.16), calls=%async_computation.2 | async-start | bytes 2097152 | tf_op jit(solution)/shard_map/all_to_all | solution.py:359
  157.3 3.9 %collective-permute-start.14 = (bf16[8,2,16,256]{3,2,1,0:T(8,128)(2,1)S(1)}, bf16[8,2,16,256]{3,2,1,0:T(8,128)(2,1)S(1)}, u32[]{:S(2)}, u32[]{:S(2)}) collective-permute-start(bf16[8,2,16,256]{3,2,1,0:T(8,128)(2,1)S(1)} %get-tuple-element.31), channel_id=1, source_target_pairs={{0,8},{2,16},{4,24},{6,0},{8,10},{10,18},{12,26},{14,2},{16,12},{1... | collective-permute-start | bytes 393224 | tf_op jit(solution)/shard_map/ppermute | solution.py:379
  161.1 3.1 %collective-permute-start.15 = (bf16[8,2,16,256]{3,2,1,0:T(8,128)(2,1)S(1)}, bf16[8,2,16,256]{3,2,1,0:T(8,128)(2,1)S(1)}, u32[]{:S(2)}, u32[]{:S(2)}) collective-permute-start(bf16[8,2,16,256]{3,2,1,0:T(8,128)(2,1)S(1)} %get-tuple-element.32), channel_id=1, source_target_pairs={{0,16},{2,24},{4,0},{6,8},{8,18},{10,26},{12,2},{14,10},{16,20},{1... | collective-permute-start | bytes 393224 | tf_op jit(solution)/shard_map/ppermute | solution.py:379
  166.4 3.2 %collective-permute-done.15 = bf16[8,2,16,256]{3,2,1,0:T(8,128)(2,1)S(1)} collective-permute-done((bf16[8,2,16,256]{3,2,1,0:T(8,128)(2,1)S(1)}, bf16[8,2,16,256]{3,2,1,0:T(8,128)(2,1)S(1)}, u32[]{:S(2)}, u32[]{:S(2)}) %collective-permute-start.15) | collective-permute-done | bytes 131104 | tf_op jit(solution)/shard_map/ppermute | solution.py:379
  170.4 7.7 %all-to-all-done.2.second = bf16[8,8,2,16,256]{4,3,2,1,0:T(8,128)(2,1)S(1)} async-done(((bf16[8,8,2,16,256]{4,3,2,1,0:T(8,128)(2,1)}), bf16[8,8,2,16,256]{4,3,2,1,0:T(8,128)(2,1)S(1)}, u32[]{:S(2)}, u32[]{:S(2)}) %all-to-all-start.2) | async-done | bytes 1048608 | tf_op jit(solution)/shard_map/all_to_all | solution.py:359
  179.2 12.0 %all_to_all.25 = f32[8,2,2]{2,1,0:T(2,128)S(1)} all-to-all(f32[8,2,2]{2,1,0:T(2,128)S(1)} %broadcast_in_dim.4), channel_id=1, replica_groups=mesh['z'=8,'x'=4,'y'=4,'core'=2] {'y','core'}, dimensions={0} | all-to-all | bytes 256 | tf_op jit(solution)/shard_map/all_to_all | solution.py:359
  191.3 11.6 %all_to_all.26 = f32[32,2,2]{2,1,0:T(2,128)S(1)} all-to-all(f32[32,2,2]{2,1,0:T(2,128)S(1)} %broadcast_in_dim.5), channel_id=1, replica_groups=mesh['z'=8,'x'=4,'y'=4,'core'=2] {'z','x'}, dimensions={0} | all-to-all | bytes 1024 | tf_op jit(solution)/shard_map/all_to_all | solution.py:359
  (64 shorter events, 23.4 us)
Async XLA Ops:
  0.6 152.1 %copy-start = (bf16[8,256,256]{2,1,0:T(8,128)(2,1)S(1)}, bf16[8,256,256]{2,1,0:T(8,128)(2,1)}, u32[]{:S(2)}) copy-start(bf16[8,256,256]{2,1,0:T(8,128)(2,1)} %param.10) | copy-start | bytes 3145732
  11.2 62.0 %all-to-all-start = ((bf16[8,33,2,16,256]{4,3,2,1,0:T(8,128)(2,1)}), bf16[8,33,2,16,256]{4,3,2,1,0:T(8,128)(2,1)}, u32[]{:S(2)}, u32[]{:S(2)}) async-start(bf16[8,33,2,16,256]{4,3,2,1,0:T(8,128)(2,1)} %get-tuple-element.24), calls=%async_computation | async-start | bytes 8650752 | tf_op jit(solution)/shard_map/all_to_all | solution.py:359
  18.9 27.4 %collective-permute-start = (bf16[2,33,2,16,256]{4,3,2,1,0:T(8,128)(2,1)}, bf16[2,33,2,16,256]{4,3,2,1,0:T(8,128)(2,1)S(1)}, u32[]{:S(2)}, u32[]{:S(2)}) collective-permute-start(bf16[2,33,2,16,256]{4,3,2,1,0:T(8,128)(2,1)} %get-tuple-element.19), channel_id=1, source_target_pairs={{0,8},{8,16},{16,24},{24,0},{1,9},{9,17},{17,25},{25,1},{2,10},{10... | collective-permute-start | bytes 3244040 | tf_op jit(solution)/shard_map/ppermute | solution.py:368
  18.9 49.3 %collective-permute-start.1 = (bf16[2,33,2,16,256]{4,3,2,1,0:T(8,128)(2,1)}, bf16[2,33,2,16,256]{4,3,2,1,0:T(8,128)(2,1)S(1)}, u32[]{:S(2)}, u32[]{:S(2)}) collective-permute-start(bf16[2,33,2,16,256]{4,3,2,1,0:T(8,128)(2,1)} %get-tuple-element.20), channel_id=1, source_target_pairs={{0,16},{8,24},{16,0},{24,8},{1,17},{9,25},{17,1},{25,9},{2,18},{10... | collective-permute-start | bytes 3244040 | tf_op jit(solution)/shard_map/ppermute | solution.py:368
  20.8 48.3 %collective-permute-start.2 = (bf16[2,33,2,16,256]{4,3,2,1,0:T(8,128)(2,1)}, bf16[2,33,2,16,256]{4,3,2,1,0:T(8,128)(2,1)S(1)}, u32[]{:S(2)}, u32[]{:S(2)}) collective-permute-start(bf16[2,33,2,16,256]{4,3,2,1,0:T(8,128)(2,1)} %get-tuple-element.21), channel_id=1, source_target_pairs={{0,24},{8,0},{16,8},{24,16},{1,25},{9,1},{17,9},{25,17},{2,26},{10... | collective-permute-start | bytes 3244040 | tf_op jit(solution)/shard_map/ppermute | solution.py:368
  22.0 51.2 %collective-permute-start.3 = (bf16[1,33,2,16,256]{4,3,2,1,0:T(8,128)(2,1)}, bf16[1,33,2,16,256]{4,3,2,1,0:T(8,128)(2,1)}, u32[]{:S(2)}, u32[]{:S(2)}) collective-permute-start(bf16[1,33,2,16,256]{4,3,2,1,0:T(8,128)(2,1)} %get-tuple-element.23), channel_id=1, source_target_pairs={{0,1},{1,0},{2,3},{3,2},{4,5},{5,4},{6,7},{7,6},{8,9},{9,8},{10,11... | collective-permute-start | bytes 1622024 | tf_op jit(solution)/shard_map/ppermute | solution.py:372
  46.3 33.7 %copy-start.4 = (bf16[2,33,2,16,256]{4,3,2,1,0:T(8,128)(2,1)}, bf16[2,33,2,16,256]{4,3,2,1,0:T(8,128)(2,1)S(1)}, u32[]{:S(2)}) copy-start(bf16[2,33,2,16,256]{4,3,2,1,0:T(8,128)(2,1)S(1)} %collective-permute-done.refs_0_.refs_3_) | copy-start | bytes 3244036
  68.2 11.8 %copy-start.5 = (bf16[2,33,2,16,256]{4,3,2,1,0:T(8,128)(2,1)}, bf16[2,33,2,16,256]{4,3,2,1,0:T(8,128)(2,1)S(1)}, u32[]{:S(2)}) copy-start(bf16[2,33,2,16,256]{4,3,2,1,0:T(8,128)(2,1)S(1)} %collective-permute-done.1.refs_1_.refs_4_) | copy-start | bytes 3244036
  71.9 12.9 %collective-permute-start.4 = (bf16[3,33,2,16,256]{4,3,2,1,0:T(8,128)(2,1)}, bf16[3,33,2,16,256]{4,3,2,1,0:T(8,128)(2,1)}, u32[]{:S(2)}, u32[]{:S(2)}) collective-permute-start(bf16[3,33,2,16,256]{4,3,2,1,0:T(8,128)(2,1)} %get-tuple-element.26), channel_id=1, source_target_pairs={{0,1},{1,0},{2,3},{3,2},{4,5},{5,4},{6,7},{7,6},{8,9},{9,8},{10,11... | collective-permute-start | bytes 4866056 | tf_op jit(solution)/shard_map/ppermute | solution.py:372
  80.0 55.9 %all-to-all-start.1 = ((bf16[4,64,2,16,256]{4,3,2,1,0:T(8,128)(2,1)}), bf16[4,64,2,16,256]{4,3,2,1,0:T(8,128)(2,1)}, u32[]{:S(2)}, u32[]{:S(2)}) async-start(bf16[4,64,2,16,256]{4,3,2,1,0:T(8,128)(2,1)} %bitcast.17), calls=%async_computation.1 | async-start | bytes 8388608 | tf_op jit(solution)/shard_map/all_to_all | solution.py:359
  91.5 10.3 %collective-permute-start.9 = (bf16[16,2,16,256]{3,2,1,0:T(8,128)(2,1)}, bf16[16,2,16,256]{3,2,1,0:T(8,128)(2,1)S(1)}, u32[]{:S(2)}, u32[]{:S(2)}) collective-permute-start(bf16[16,2,16,256]{3,2,1,0:T(8,128)(2,1)} %get-tuple-element.29), channel_id=1, source_target_pairs={{0,224},{32,0},{64,32},{96,64},{128,96},{160,128},{192,160},{224,1... | collective-permute-start | bytes 786440 | tf_op jit(solution)/shard_map/ppermute | solution.py:368
  95.9 11.8 %collective-permute-start.5 = (bf16[16,2,16,256]{3,2,1,0:T(8,128)(2,1)}, bf16[16,2,16,256]{3,2,1,0:T(8,128)(2,1)S(1)}, u32[]{:S(2)}, u32[]{:S(2)}) collective-permute-start(bf16[16,2,16,256]{3,2,1,0:T(8,128)(2,1)} %get-tuple-element.28), channel_id=1, source_target_pairs={{0,32},{32,64},{64,96},{96,128},{128,160},{160,192},{192,224},{224... | collective-permute-start | bytes 786440 | tf_op jit(solution)/shard_map/ppermute | solution.py:368
  104.2 14.1 %collective-permute-start.10 = (bf16[32,2,16,256]{3,2,1,0:T(8,128)(2,1)S(1)}, bf16[32,2,16,256]{3,2,1,0:T(8,128)(2,1)S(1)}, u32[]{:S(2)}, u32[]{:S(2)}) collective-permute-start(bf16[32,2,16,256]{3,2,1,0:T(8,128)(2,1)S(1)} %shard_map.84), channel_id=1, source_target_pairs={{0,224},{32,0},{64,32},{96,64},{128,96},{160,128},{192,160},{224,1... | collective-permute-start | bytes 1572872 | tf_op jit(solution)/shard_map/ppermute | solution.py:368
  107.7 14.4 %collective-permute-start.6 = (bf16[32,2,16,256]{3,2,1,0:T(8,128)(2,1)S(1)}, bf16[32,2,16,256]{3,2,1,0:T(8,128)(2,1)S(1)}, u32[]{:S(2)}, u32[]{:S(2)}) collective-permute-start(bf16[32,2,16,256]{3,2,1,0:T(8,128)(2,1)S(1)} %shard_map.81), channel_id=1, source_target_pairs={{0,32},{32,64},{64,96},{96,128},{128,160},{160,192},{192,224},{224... | collective-permute-start | bytes 1572872 | tf_op jit(solution)/shard_map/ppermute | solution.py:368
  118.3 13.5 %collective-permute-start.11 = (bf16[32,2,16,256]{3,2,1,0:T(8,128)(2,1)S(1)}, bf16[32,2,16,256]{3,2,1,0:T(8,128)(2,1)S(1)}, u32[]{:S(2)}, u32[]{:S(2)}) collective-permute-start(bf16[32,2,16,256]{3,2,1,0:T(8,128)(2,1)S(1)} %shard_map.85), channel_id=1, source_target_pairs={{0,224},{32,0},{64,32},{96,64},{128,96},{160,128},{192,160},{224,1... | collective-permute-start | bytes 1572872 | tf_op jit(solution)/shard_map/ppermute | solution.py:368
  122.2 13.4 %collective-permute-start.7 = (bf16[32,2,16,256]{3,2,1,0:T(8,128)(2,1)S(1)}, bf16[32,2,16,256]{3,2,1,0:T(8,128)(2,1)S(1)}, u32[]{:S(2)}, u32[]{:S(2)}) collective-permute-start(bf16[32,2,16,256]{3,2,1,0:T(8,128)(2,1)S(1)} %shard_map.82), channel_id=1, source_target_pairs={{0,32},{32,64},{64,96},{96,128},{128,160},{160,192},{192,224},{224... | collective-permute-start | bytes 1572872 | tf_op jit(solution)/shard_map/ppermute | solution.py:368
  132.0 12.5 %collective-permute-start.12 = (bf16[32,2,16,256]{3,2,1,0:T(8,128)(2,1)S(1)}, bf16[32,2,16,256]{3,2,1,0:T(8,128)(2,1)S(1)}, u32[]{:S(2)}, u32[]{:S(2)}) collective-permute-start(bf16[32,2,16,256]{3,2,1,0:T(8,128)(2,1)S(1)} %shard_map.86), channel_id=1, source_target_pairs={{0,224},{32,0},{64,32},{96,64},{128,96},{160,128},{192,160},{224,1... | collective-permute-start | bytes 1572872 | tf_op jit(solution)/shard_map/ppermute | solution.py:368
  135.7 12.3 %collective-permute-start.8 = (bf16[32,2,16,256]{3,2,1,0:T(8,128)(2,1)S(1)}, bf16[32,2,16,256]{3,2,1,0:T(8,128)(2,1)}, u32[]{:S(2)}, u32[]{:S(2)}) collective-permute-start(bf16[32,2,16,256]{3,2,1,0:T(8,128)(2,1)S(1)} %shard_map.83), channel_id=1, source_target_pairs={{0,32},{32,64},{64,96},{96,128},{128,160},{160,192},{192,224},{224... | collective-permute-start | bytes 1572872 | tf_op jit(solution)/shard_map/ppermute | solution.py:368
  148.0 30.2 %all-to-all-start.2 = ((bf16[8,8,2,16,256]{4,3,2,1,0:T(8,128)(2,1)}), bf16[8,8,2,16,256]{4,3,2,1,0:T(8,128)(2,1)S(1)}, u32[]{:S(2)}, u32[]{:S(2)}) async-start(bf16[8,8,2,16,256]{4,3,2,1,0:T(8,128)(2,1)} %bitcast.16), calls=%async_computation.2 | async-start | bytes 2097152 | tf_op jit(solution)/shard_map/all_to_all | solution.py:359
  155.2 10.8 %copy-start.11 = (bf16[8,32,256]{2,1,0:T(8,128)(2,1)S(1)}, bf16[8,32,256]{2,1,0:T(8,128)(2,1)}, u32[]{:S(2)}) copy-start(bf16[8,32,256]{2,1,0:T(8,128)(2,1)} %param.9) | copy-start | bytes 393220
  156.6 9.9 %collective-permute-start.13 = (bf16[8,2,16,256]{3,2,1,0:T(8,128)(2,1)S(1)}, bf16[8,2,16,256]{3,2,1,0:T(8,128)(2,1)S(1)}, u32[]{:S(2)}, u32[]{:S(2)}) collective-permute-start(bf16[8,2,16,256]{3,2,1,0:T(8,128)(2,1)S(1)} %get-tuple-element.30), channel_id=1, source_target_pairs={{0,0},{2,8},{4,16},{6,24},{8,2},{10,10},{12,18},{14,26},{16,4},{18... | collective-permute-start | bytes 393224 | tf_op jit(solution)/shard_map/ppermute | solution.py:379
  157.3 9.2 %collective-permute-start.14 = (bf16[8,2,16,256]{3,2,1,0:T(8,128)(2,1)S(1)}, bf16[8,2,16,256]{3,2,1,0:T(8,128)(2,1)S(1)}, u32[]{:S(2)}, u32[]{:S(2)}) collective-permute-start(bf16[8,2,16,256]{3,2,1,0:T(8,128)(2,1)S(1)} %get-tuple-element.31), channel_id=1, source_target_pairs={{0,8},{2,16},{4,24},{6,0},{8,10},{10,18},{12,26},{14,2},{16,12},{1... | collective-permute-start | bytes 393224 | tf_op jit(solution)/shard_map/ppermute | solution.py:379
  161.1 8.5 %collective-permute-start.15 = (bf16[8,2,16,256]{3,2,1,0:T(8,128)(2,1)S(1)}, bf16[8,2,16,256]{3,2,1,0:T(8,128)(2,1)S(1)}, u32[]{:S(2)}, u32[]{:S(2)}) collective-permute-start(bf16[8,2,16,256]{3,2,1,0:T(8,128)(2,1)S(1)} %get-tuple-element.32), channel_id=1, source_target_pairs={{0,16},{2,24},{4,0},{6,8},{8,18},{10,26},{12,2},{14,10},{16,20},{1... | collective-permute-start | bytes 393224 | tf_op jit(solution)/shard_map/ppermute | solution.py:379
  164.2 6.1 %collective-permute-start.16 = (bf16[8,2,16,256]{3,2,1,0:T(8,128)(2,1)S(1)}, bf16[8,2,16,256]{3,2,1,0:T(8,128)(2,1)S(1)}, u32[]{:S(2)}, u32[]{:S(2)}) collective-permute-start(bf16[8,2,16,256]{3,2,1,0:T(8,128)(2,1)S(1)} %get-tuple-element.33), channel_id=1, source_target_pairs={{0,24},{2,0},{4,8},{6,16},{8,26},{10,2},{12,10},{14,18},{16,28},{1... | collective-permute-start | bytes 393224 | tf_op jit(solution)/shard_map/ppermute | solution.py:379
  (8 other events, 26.2 us)
